TPU v7x, 128 devices: a whole 4x4x4 slice. The times are simulated.
128 devices in a mesh: member: 4 (over y), space: 32 (over x, z, core).
Axes of the slice: x: 4, y: 4, z: 4, core: 2. Of those that a mesh axis runs over, the one named last changes fastest.
Arguments:
- prior_ensemble: bfloat16 [96, 12, 65536], P('member', None, 'space'), may hold values from -48 to 48, as said below
- measured_readings: float32 [384, 4, 128], P('space', 'member'), may hold values from -8 to 8
- measurement_error_spread: float32 [384, 4, 128], P('space', 'member'), may hold values from 307 to 30720, as said below
- mapping_submatrices: bfloat16 [384, 4, 2, 128, 128], P('space', 'member'), may hold values from -0.375 to 0.375
- submatrix_target_slots: int32 [384, 4, 2], P('space', 'member'), may hold values from 0 to 15
Outputs:
- analysis: bfloat16 [96, 12, 65536], P('member', None, 'space')
- weights: float32 [96, 96], replicated
Inputs may be any that keep to these rules, and one draw needn't show every extreme that they name: `prior_ensemble`: observed model fields with neighbouring members correlated. `measurement_error_spread`: Positive. `submatrix_target_slots`: column blocks lie in the first 4 variables.
All inputs are finite; a program needn't handle non-finite values.
Results may differ from a plain program's by a relative error of at most 0.006.
Values may be sent and summed in bfloat16 or wider, within the bound.
No kernel may reach another device: no remote copies, remote signals or barrier semaphores. Data moves between devices by JAX's collectives and lax.ppermute only.
A program may use at most 64 MiB of HBM per device.

v0:
```python
import jax
import jax.numpy as jnp
from jax import lax
from jax.sharding import PartitionSpec as P

V = 12
VOBS = 4
NS_ITERS = 4


HIGHEST_MODE = lax.Precision.HIGHEST


def observe(observed_part, op_piece, col_piece):
    realisation_sequence = observed_part.shape[0]
    blocks_here = op_piece.shape[0]
    nonzeros = op_piece.shape[1]
    observed = observed_part.reshape(realisation_sequence, -1, 128)
    picked_rows = jnp.take(observed, col_piece.reshape(-1), axis=1)
    picked_rows = picked_rows.reshape(realisation_sequence, blocks_here, nonzeros, 128)
    return jnp.einsum("kbjc,bjoc->kbo", picked_rows, op_piece, preferred_element_type=jnp.float32)


def ensemble_weights(gram, projected, realisation_sequence):
    eye_matrix = jnp.eye(realisation_sequence, dtype=jnp.float32)
    system = gram + (realisation_sequence - 1.0) * eye_matrix
    frob = jnp.sqrt(jnp.sum(system * system))

    def newton_step(step_index, carry):
        root_part, inverse_part = carry
        factor = 1.5 * eye_matrix - 0.5 * jnp.dot(inverse_part, root_part, precision=HIGHEST_MODE)
        return (
            jnp.dot(root_part, factor, precision=HIGHEST_MODE),
            jnp.dot(factor, inverse_part, precision=HIGHEST_MODE),
        )

    root_part, inverse_part = lax.fori_loop(0, NS_ITERS, newton_step, (system / frob, eye_matrix))
    inverse_root = inverse_part / jnp.sqrt(frob)
    covariance = jnp.dot(inverse_root, inverse_root, precision=HIGHEST_MODE)
    mean_shift = jnp.dot(covariance, projected, precision=HIGHEST_MODE)
    return mean_shift[:, None] + jnp.sqrt(realisation_sequence - 1.0) * inverse_root


def body(
    prior_ensemble,
    measured_readings,
    measurement_error_spread,
    mapping_submatrices,
    submatrix_target_slots,
):
    patch_prognostic_vector = lax.all_to_all(
        prior_ensemble, "member", split_axis=2, concat_axis=0, tiled=True
    )
    observed_part = patch_prognostic_vector[:, :VOBS]
    realisation_sequence = observed_part.shape[0]
    predicted = observe(observed_part, mapping_submatrices[:, 0], submatrix_target_slots[:, 0])
    values = measured_readings[:, 0]
    variances = measurement_error_spread[:, 0]
    pred_mean = jnp.mean(predicted, axis=0)
    spread = predicted - pred_mean[None]
    scaled = spread / variances[None]
    gram_part = jnp.einsum("kbo,lbo->kl", scaled, spread, precision=HIGHEST_MODE)
    projected_part = jnp.einsum("kbo,bo->k", scaled, values - pred_mean, precision=HIGHEST_MODE)
    gram, projected = lax.psum((gram_part, projected_part), ("member", "space"))
    weights = ensemble_weights(gram, projected, realisation_sequence)
    coeffs = weights.astype(jnp.bfloat16)
    keep = 1.0 - jnp.sum(coeffs.astype(jnp.float32), axis=0)
    cells_here = patch_prognostic_vector.shape[2]
    flat = patch_prognostic_vector.reshape(realisation_sequence, V * cells_here)
    ones_row = jnp.ones((1, realisation_sequence), jnp.bfloat16)
    center = jnp.dot(ones_row, flat, preferred_element_type=jnp.float32)[0] / realisation_sequence
    mixed = (
        jnp.dot(coeffs.T, flat, preferred_element_type=jnp.float32)
        + keep[:, None] * center[None, :]
    )
    analysed = mixed.astype(jnp.bfloat16).reshape(realisation_sequence, V, cells_here)
    analysis = lax.all_to_all(analysed, "member", split_axis=0, concat_axis=2, tiled=True)
    return (analysis, weights)


def solution(mesh):
    in_specs = (
        P("member", None, "space"),
        P("space", "member", None),
        P("space", "member", None),
        P("space", "member", None, None, None),
        P("space", "member", None),
    )
    out_specs = (P("member", None, "space"), P())
    return jax.shard_map(body, mesh=mesh, in_specs=in_specs, out_specs=out_specs, check_vma=False)
```

profile of v0, /device:TPU:0, one launch (start us, length us, event | category | flops | bytes accessed | tf_op | source)
XLA Modules:
  0.0 175.5 jit_solution(17839588777371846193)
XLA Ops:
  0.6 9.8 %copy.25 = bf16[24,12,2048]{0,1,2:T(8,128)(2,1)} copy(bf16[24,12,2048]{2,0,1:T(8,128)(2,1)} %param.7) | data formatting | bytes 2359296 | tf_op args[0]
  10.4 10.8 %reshape.85 = bf16[4,2,73728]{2,1,0:T(2,128)(2,1)} reshape(bf16[2048,12,24]{2,1,0:T(8,128)(2,1)} %bitcast.77) | data formatting | bytes 2359296
  21.3 4.7 %all-to-all-start = ((bf16[4,2,73728]{2,1,0:T(2,128)(2,1)}), bf16[4,2,73728]{2,1,0:T(2,128)(2,1)S(1)}, u32[]{:S(2)}, u32[]{:S(2)}) async-start(bf16[4,2,73728]{2,1,0:T(2,128)(2,1)} %reshape.85), calls=%async_computation | async-start | bytes 2359296 | tf_op jit(solution)/shard_map/all_to_all | solution.py:51
  26.9 15.5 %all-to-all-done = bf16[4,2,73728]{2,1,0:T(2,128)(2,1)S(1)} async-done(((bf16[4,2,73728]{2,1,0:T(2,128)(2,1)}), bf16[4,2,73728]{2,1,0:T(2,128)(2,1)S(1)}, u32[]{:S(2)}, u32[]{:S(2)}) %all-to-all-start) | async-done | bytes 1179680 | tf_op jit(solution)/shard_map/all_to_all | solution.py:51
  42.5 10.8 %reshape.86 = bf16[2048,12,24]{2,1,0:T(8,128)(2,1)} reshape(bf16[4,2,73728]{2,1,0:T(2,128)(2,1)S(1)} %all-to-all-done) | data formatting | bytes 2359296
  53.3 9.5 %copy.36 = bf16[24,12,4,512]{3,2,0,1:T(4,128)(2,1)S(1)} copy(bf16[24,12,4,512]{0,1,3,2:T(8,128)(2,1)} %bitcast.76) | data formatting | bytes 2359296 | tf_op jit(solution)/shard_map/all_to_all | solution.py:51
  66.3 66.7 %all-reduce = (f32[96,96]{1,0:T(8,128)S(1)}, f32[96]{0:T(128)S(1)}) all-reduce(f32[96,96]{1,0:T(8,128)S(1)} %convolution_bitcast_fusion.2, f32[96]{0:T(128)S(1)} %convolution_bitcast_fusion.3), channel_id=1, replica_groups=mesh['member'=4,'space'=32] {'member','space'}, use_global_device_ids=true, to_apply=%region_1.2 | all-reduce | flops 9312 | bytes 74496 | tf_op jit(solution)/shard_map/psum | solution.py:64
  135.7 0.9 copy.31
  136.6 8.5 %while.13 = (s32[]{:T(128)}, f32[96,96]{0,1:T(8,128)S(1)}, f32[96,96]{1,0:T(8,128)}, s32[]{:T(128)}) while((s32[]{:T(128)}, f32[96,96]{0,1:T(8,128)S(1)}, f32[96,96]{1,0:T(8,128)}, s32[]{:T(128)}) %tuple.32), condition=%wide.region_4.5_spmd.clone, body=%wide.region_3.4_spmd.clone.sunk | while | flops 31887360 | bytes 479285 | solution.py:37
  136.6 0.8 copy.59
  137.6 0.8 fusion.51
  138.7 0.8 copy.59
  139.8 0.8 fusion.51
  140.9 0.8 copy.59
  141.9 0.8 fusion.51
  143.0 0.8 copy.59
  144.0 0.8 fusion.51
  145.1 1.1 fusion.15
  146.3 0.9 convert_reduce_fusion
  147.3 0.7 copy.39
  148.8 0.8 reshape.68
  149.7 23.2 %all_to_all.36 = bf16[96,12,512]{2,1,0:T(8,128)(2,1)S(1)} all-to-all(bf16[96,12,512]{2,1,0:T(8,128)(2,1)S(1)} %reshape.68), channel_id=1, replica_groups=mesh['member'=4,'space'=32] {'member'}, dimensions={0} | all-to-all | bytes 2359296 | tf_op jit(solution)/shard_map/all_to_all | solution.py:77
  172.9 0.9 copy.33
  173.8 1.7 all_to_all.33
  (48 shorter events, 9.2 us)
Async XLA Ops:
  0.6 63.8 %copy-start = (bf16[12,1,2,128,128]{4,3,2,1,0:T(8,128)(2,1)S(1)}, bf16[12,1,2,128,128]{4,3,2,1,0:T(8,128)(2,1)}, u32[]{:S(2)}) copy-start(bf16[12,1,2,128,128]{4,3,2,1,0:T(8,128)(2,1)} %param.10) | copy-start | bytes 2359300
  21.3 4.7 %copy-start.4 = (s32[12,1,2]{0,2,1:T(2,128)S(1)}, s32[12,1,2]{0,2,1:T(2,128)}, u32[]{:S(2)}) copy-start(s32[12,1,2]{0,2,1:T(2,128)} %param.11) | copy-start | bytes 292
  21.3 5.0 %copy-start.2 = (f32[12,1,128]{2,1,0:T(1,128)S(1)}, f32[12,1,128]{2,1,0:T(1,128)}, u32[]{:S(2)}) copy-start(f32[12,1,128]{2,1,0:T(1,128)} %param.9) | copy-start | bytes 18436
  21.3 21.2 %all-to-all-start = ((bf16[4,2,73728]{2,1,0:T(2,128)(2,1)}), bf16[4,2,73728]{2,1,0:T(2,128)(2,1)S(1)}, u32[]{:S(2)}, u32[]{:S(2)}) async-start(bf16[4,2,73728]{2,1,0:T(2,128)(2,1)} %reshape.85), calls=%async_computation | async-start | bytes 2359296 | tf_op jit(solution)/shard_map/all_to_all | solution.py:51
  64.4 0.7 copy-start.3
  147.3 1.0 copy-start.1
where the time goes:
time: 177 us; the launch traced here: 175 us
  blocking collectives  89.9 us (51%)
  local copies, waits for them, and re-layouts  52 us (29%)
  waiting for transfers between devices  15.5 us (9%)
  matrix products  8.82 us (5%)
  starting transfers between devices  4.68 us (3%)
  other arithmetic  2.84 us (2%)
    psum x1, blocking collectives, body(): gram, projected = lax.psum((gram_part, projected_part), ('member', 'space'))  66.7 us
    unnamed x17, local copies, waits for them, and re-layouts  33.5 us
    all_to_all x1, blocking collectives, body(): lax.all_to_all(analysed, 'member', split_axis=0, concat_axis=2, tiled=True)  23.2 us
    all_to_all x1, waiting for transfers between devices, body(): lax.all_to_all(prior_ensemble, 'member', split_axis=2, concat_axis=0, til...  15.5 us
    all_to_all x3, local copies, waits for them, and re-layouts, body(): lax.all_to_all(prior_ensemble, 'member', split_axis=2, concat_axis=0, til...  10.4 us
    all_to_all x1, starting transfers between devices, body(): lax.all_to_all(prior_ensemble, 'member', split_axis=2, concat_axis=0, til...  4.68 us
  transfers between devices with their start and end apart: 1, of which 1 were waited for; matrix products, arithmetic and copies ran while one was open for 1% of the time, Pallas kernels for 0%

commit v1 on v0

v1 whole, which is shorter than its diff:
```python
import jax
import jax.numpy as jnp
from jax import lax
from jax.experimental import pallas as pl
from jax.experimental.pallas import tpu as pltpu
from jax.sharding import PartitionSpec as P

K = 96
V = 12
VOBS = 4
MEMBERS = 24
GROUPS = 4
TILE = 512
BLOCKS = 12
NNZ = 2
NS_ITERS = 4

EXACT = lax.Precision.HIGHEST
VMEM = pl.BlockSpec(memory_space=pltpu.VMEM)
SMEM = pl.BlockSpec(memory_space=pltpu.SMEM)
ANY = pl.BlockSpec(memory_space=pl.ANY)
ROOM = pltpu.CompilerParams(vmem_limit_bytes=48 * 1024 * 1024)


def group_from(me, shift):
    return lax.rem(me + GROUPS - shift, GROUPS)


def group_to(me, shift):
    return lax.rem(me + shift, GROUPS)


def pack_kernel(me_ref, prior_ref, *refs):
    outs, sems = refs[:-1], refs[-1]
    me = me_ref[0]
    copies = []
    for s in range(GROUPS):
        cells = pl.ds(pl.multiple_of(group_to(me, s) * TILE, TILE), TILE)
        for part, rows in enumerate((pl.ds(0, VOBS), pl.ds(VOBS, V - VOBS))):
            n = part * GROUPS + s
            copies.append(
                pltpu.make_async_copy(prior_ref.at[rows, :, cells], outs[n], sems.at[n])
            )
    for copy in copies:
        copy.start()
    for copy in copies:
        copy.wait()


def pack(me, prior):
    shapes = [jax.ShapeDtypeStruct((VOBS, MEMBERS, TILE), prior.dtype)] * GROUPS
    shapes += [jax.ShapeDtypeStruct((V - VOBS, MEMBERS, TILE), prior.dtype)] * GROUPS
    outs = pl.pallas_call(
        pack_kernel,
        out_shape=shapes,
        in_specs=[SMEM, ANY],
        out_specs=[ANY] * len(shapes),
        scratch_shapes=[pltpu.SemaphoreType.DMA((2 * GROUPS,))],
        name="pack",
    )(me, prior)
    return outs[:GROUPS], outs[GROUPS:]


def observe_kernel(me_ref, slots_ref, c0, c1, c2, c3, op_ref, y_ref, var_ref, out_ref, state, spread, scaled):
    me = me_ref[0]
    for s, chunk in enumerate((c0, c1, c2, c3)):
        rows = pl.ds(pl.multiple_of(group_from(me, s) * MEMBERS, 8), MEMBERS)
        for v in range(VOBS):
            for c in range(TILE // 128):
                state[v * (TILE // 128) + c, rows, :] = chunk[v, :, c * 128 : (c + 1) * 128].astype(jnp.float32)
    spread[K:, :] = jnp.zeros((128 - K, BLOCKS * 128), jnp.float32)
    for b in range(BLOCKS):
        pred = jnp.zeros((K, 128), jnp.float32)
        for j in range(NNZ):
            part = state[slots_ref[b * NNZ + j]].astype(jnp.bfloat16)
            pred += lax.dot_general(
                part, op_ref[b, j], (((1,), (1,)), ((), ())), preferred_element_type=jnp.float32
            )
        mean = jnp.sum(pred, axis=0, keepdims=True) * (1.0 / K)
        dev = pred - mean
        lanes = pl.ds(b * 128, 128)
        spread[:K, lanes] = dev
        spread[K : K + 1, lanes] = y_ref[b : b + 1, :] - mean
        scaled[:, lanes] = dev / var_ref[b : b + 1, :]
    out_ref[...] = lax.dot_general(
        scaled[...], spread[...], (((1,), (1,)), ((), ())), precision=EXACT, preferred_element_type=jnp.float32
    )


def observe(me, slots, chunks, op, values, variances):
    return pl.pallas_call(
        observe_kernel,
        out_shape=jax.ShapeDtypeStruct((K, 128), jnp.float32),
        in_specs=[SMEM, SMEM] + [VMEM] * 7,
        out_specs=VMEM,
        scratch_shapes=[
            pltpu.VMEM((VOBS * TILE // 128, K, 128), jnp.float32),
            pltpu.VMEM((128, BLOCKS * 128), jnp.float32),
            pltpu.VMEM((K, BLOCKS * 128), jnp.float32),
        ],
        compiler_params=ROOM,
        name="observe",
    )(me, slots, *chunks, op, values, variances)


def exact_dot(a, b):
    return jnp.dot(a, b, precision=EXACT, preferred_element_type=jnp.float32)


def weights_kernel(sums_ref, weights_ref):
    sums = sums_ref[...]
    row = lax.broadcasted_iota(jnp.int32, (K, K), 0)
    col = lax.broadcasted_iota(jnp.int32, (K, K), 1)
    eye = jnp.where(row == col, 1.0, 0.0).astype(jnp.float32)
    system = sums[:, :K] + (K - 1.0) * eye
    projected = sums[:, K : K + 1]
    frob = jnp.sqrt(jnp.sum(system * system, keepdims=True))
    root = system / frob
    inverse = None
    for step in range(NS_ITERS):
        product = root if inverse is None else exact_dot(inverse, root)
        factor = 1.5 * eye - 0.5 * product
        if step < NS_ITERS - 1:
            root = exact_dot(root, factor)
        inverse = factor if inverse is None else exact_dot(factor, inverse)
    inverse_root = inverse / jnp.sqrt(frob)
    covariance = exact_dot(inverse_root, inverse_root)
    mean_shift = exact_dot(covariance, projected)
    weights_ref[...] = mean_shift + (K - 1.0) ** 0.5 * inverse_root


def make_weights(sums):
    return pl.pallas_call(
        weights_kernel,
        out_shape=jax.ShapeDtypeStruct((K, K), jnp.float32),
        in_specs=[VMEM],
        out_specs=VMEM,
        name="transform",
    )(sums)


def analyse_kernel(me_ref, w_ref, o0, o1, o2, o3, r0, r1, r2, r3, a0, a1, a2, a3, turned):
    me = me_ref[0]

    def regroup(x, which):
        return jnp.concatenate(
            [x[pl.ds(pl.multiple_of(which(me, s) * MEMBERS, 8), MEMBERS), :] for s in range(GROUPS)], axis=0
        )

    by_source = regroup(w_ref, group_from)
    turned[...] = by_source.T
    coeffs = regroup(turned, group_to).astype(jnp.bfloat16)
    keep = 1.0 - jnp.sum(coeffs.astype(jnp.float32), axis=1, keepdims=True)
    outs = (a0, a1, a2, a3)
    for v in range(V):
        src = (o0, o1, o2, o3) if v < VOBS else (r0, r1, r2, r3)
        u = v if v < VOBS else v - VOBS
        parts = [ref[u].astype(jnp.float32) for ref in src]
        stacked = jnp.concatenate(parts, axis=0)
        center = jnp.sum(stacked, axis=0, keepdims=True) * (1.0 / K)
        mixed = jnp.dot(coeffs, stacked.astype(jnp.bfloat16), preferred_element_type=jnp.float32)
        mixed = mixed + keep * center
        for g in range(GROUPS):
            outs[g][v] = mixed[g * MEMBERS : (g + 1) * MEMBERS].astype(jnp.bfloat16)


def analyse(me, weights, observed, rest):
    return pl.pallas_call(
        analyse_kernel,
        out_shape=[jax.ShapeDtypeStruct((V, MEMBERS, TILE), jnp.bfloat16)] * GROUPS,
        in_specs=[SMEM] + [VMEM] * 9,
        out_specs=[VMEM] * GROUPS,
        scratch_shapes=[pltpu.VMEM((K, K), jnp.float32)],
        compiler_params=ROOM,
        name="analyse",
    )(me, weights, *observed, *rest)


def place_kernel(me_ref, c0, c1, c2, c3, out_ref, sems):
    me = me_ref[0]
    copies = []
    for s, chunk in enumerate((c0, c1, c2, c3)):
        cells = pl.ds(pl.multiple_of(group_from(me, s) * TILE, TILE), TILE)
        copies.append(pltpu.make_async_copy(chunk, out_ref.at[:, :, cells], sems.at[s]))
    for copy in copies:
        copy.start()
    for copy in copies:
        copy.wait()


def place(me, chunks):
    return pl.pallas_call(
        place_kernel,
        out_shape=jax.ShapeDtypeStruct((V, MEMBERS, GROUPS * TILE), jnp.bfloat16),
        in_specs=[SMEM] + [ANY] * GROUPS,
        out_specs=ANY,
        scratch_shapes=[pltpu.SemaphoreType.DMA((GROUPS,))],
        name="place",
    )(me, *chunks)


def ring(shift):
    return [(i, (i + shift) % GROUPS) for i in range(GROUPS)]


def space_shift(dx, dz, dc):
    pairs = []
    for x in range(4):
        for z in range(4):
            for c in range(2):
                to = ((x + dx) % 4) * 8 + ((z + dz) % 4) * 2 + (c + dc) % 2
                pairs.append((x * 8 + z * 2 + c, to))
    return pairs


def scatter(chunks):
    return [chunks[0]] + [lax.ppermute(chunks[s], "member", ring(s)) for s in range(1, GROUPS)]


def total(x):
    x = x + lax.ppermute(x, "space", space_shift(0, 0, 1))
    parts = [lax.ppermute(x, "member", ring(s)) for s in (2, 1, 3)]
    x = (x + parts[0]) + (parts[1] + parts[2])
    parts = [lax.ppermute(x, "space", space_shift(0, s, 0)) for s in (2, 1, 3)]
    x = (x + parts[0]) + (parts[1] + parts[2])
    parts = [lax.ppermute(x, "space", space_shift(s, 0, 0)) for s in (2, 1, 3)]
    return (x + parts[0]) + (parts[1] + parts[2])


def body(prior, readings, error_spread, mapping, slots):
    me = lax.axis_index("member").astype(jnp.int32).reshape(1)
    observed_out, rest_out = pack(me, jnp.transpose(prior, (1, 0, 2)))
    observed = scatter(observed_out)
    rest = scatter(rest_out)
    sums = total(
        observe(me, slots.reshape(-1), observed, mapping[:, 0], readings[:, 0], error_spread[:, 0])
    )
    weights = make_weights(sums)
    chunks = analyse(me, weights, observed, rest)
    out = place(me, scatter(chunks))
    return (jnp.transpose(out, (1, 0, 2)), weights)


def solution(mesh):
    in_specs = (
        P("member", None, "space"),
        P("space", "member", None),
        P("space", "member", None),
        P("space", "member", None, None, None),
        P("space", "member", None),
    )
    out_specs = (P("member", None, "space"), P())
    return jax.shard_map(body, mesh=mesh, in_specs=in_specs, out_specs=out_specs, check_vma=False)
```

time: 177 us -> 138 us (0.78)
  blocking collectives: 89.9 us -> 0 us
  Pallas kernels: 0 us -> 80 us
  local copies, waits for them, and re-layouts: 52 us -> 3.35 us
  starting transfers between devices: 4.68 us -> 30.3 us
  matrix products: 8.82 us -> 0 us
  waiting for transfers between devices: 15.5 us -> 22 us
  other arithmetic: 2.84 us -> 0.66 us
    pallas_call x0 -> x5, Pallas kernels: none -> 80 us  [the longest x1 36.9 us: pack(): pl.pallas_call(pack_kernel, out_shape=shapes, in_specs=[SMEM, ANY], out_s...]
    psum x1 -> x0, blocking collectives: 66.7 us -> none  [body(): gram, projected = lax.psum((gram_part, projected_part), ('member', 'space'))]
    ppermute x0 -> x19, starting transfers between devices: none -> 30.3 us  [the longest x9 14.5 us: scatter(): lax.ppermute(chunks[s], 'member', ring(s))]
    unnamed x17 -> x32, local copies, waits for them, and re-layouts: 33.5 us -> 3.27 us
    all_to_all x1 -> x0, blocking collectives: 23.2 us -> none  [body(): lax.all_to_all(analysed, 'member', split_axis=0, concat_axis=2, tiled=True)]
    ppermute x0 -> x19, waiting for transfers between devices: none -> 22 us  [the longest x9 13 us: scatter(): lax.ppermute(chunks[s], 'member', ring(s))]
    all_to_all x1 -> x0, waiting for transfers between devices: 15.5 us -> none  [body(): lax.all_to_all(prior_ensemble, 'member', split_axis=2, concat_axis=0, til...]
    all_to_all x5 -> x0, local copies, waits for them, and re-layouts: 13 us -> none  [the longest x3 10.4 us: body(): lax.all_to_all(prior_ensemble, 'member', split_axis=2, concat_axis=0, til...]
  transfers between devices with their start and end apart: 1 -> 19, of which waited for: 1 -> 8; matrix products, arithmetic and copies ran while one was open for 1% -> 1% of each run, Pallas kernels for 0% -> 2%
where the time goes in v1:
time: 138 us; the launch traced here: 137 us
  Pallas kernels  80 us (58%)
  starting transfers between devices  30.3 us (22%)
  waiting for transfers between devices  22 us (16%)
  local copies, waits for them, and re-layouts  3.35 us (2%)
    pallas_call x1, Pallas kernels, pack(): pl.pallas_call(pack_kernel, out_shape=shapes, in_specs=[SMEM, ANY], out_s...  36.9 us
    pallas_call x1, Pallas kernels, place(): pl.pallas_call(place_kernel, out_shape=jax.ShapeDtypeStruct((V, MEMBERS,...  36.9 us
    ppermute x9, starting transfers between devices, scatter(): lax.ppermute(chunks[s], 'member', ring(s))  14.5 us
    ppermute x9, waiting for transfers between devices, scatter(): lax.ppermute(chunks[s], 'member', ring(s))  13 us
    ppermute x3, starting transfers between devices, total(): parts = [lax.ppermute(x, 'space', space_shift(0, s, 0)) for s in (2, 1, 3)]  5.97 us
    ppermute x3, starting transfers between devices, total(): parts = [lax.ppermute(x, 'space', space_shift(s, 0, 0)) for s in (2, 1, 3)]  5.11 us
    ppermute x3, starting transfers between devices, total(): parts = [lax.ppermute(x, 'member', ring(s)) for s in (2, 1, 3)]  4.66 us
    ppermute x3, waiting for transfers between devices, total(): parts = [lax.ppermute(x, 'space', space_shift(0, s, 0)) for s in (2, 1, 3)]  3.96 us
  transfers between devices with their start and end apart: 19, of which 8 were waited for; matrix products, arithmetic and copies ran while one was open for 1% of the time, Pallas kernels for 2%

profile of v1, /device:TPU:0, one launch (start us, length us, event | category | flops | bytes accessed | tf_op | source)
XLA Modules:
  0.0 137.2 jit_solution(7588413062658340675)
XLA Ops:
  0.7 36.9 %pack.1 = (bf16[4,24,512]{2,1,0:T(8,128)(2,1)}, bf16[4,24,512]{2,1,0:T(8,128)(2,1)}, bf16[4,24,512]{2,1,0:T(8,128)(2,1)}, bf16[4,24,512]{2,1,0:T(8,128)(2,1)}, b...) custom-call(s32[1]{0:T(128)} %bitcast.me_ref, ...), custom_call_target="tpu_custom_call" | custom-call | tf_op jit(solution)/shard_map/pack/pallas_call | solution.py:53
  37.6 1.7 %collective-permute-start = (bf16[4,24,512]{2,1,0:T(8,128)(2,1)}, bf16[4,24,512]{2,1,0:T(8,128)(2,1)S(1)}, u32[]{:S(2)}, u32[]{:S(2)}) collective-permute-start(bf16[4,24,512]{2,1,0:T(8,128)(2,1)} %get-tuple-element.15), channel_id=1, source_target_pairs={{0,32},{32,64},{64,96},{96,0},{1,33},{33,65},{65,97},{97,1},{2,34}... | collective-permute-start | bytes 294920 | tf_op jit(solution)/shard_map/ppermute | solution.py:217
  39.3 2.9 %collective-permute-start.1 = (bf16[4,24,512]{2,1,0:T(8,128)(2,1)}, bf16[4,24,512]{2,1,0:T(8,128)(2,1)S(1)}, u32[]{:S(2)}, u32[]{:S(2)}) collective-permute-start(bf16[4,24,512]{2,1,0:T(8,128)(2,1)} %get-tuple-element.16), channel_id=1, source_target_pairs={{0,64},{32,96},{64,0},{96,32},{1,65},{33,97},{65,1},{97,33},{2,66}... | collective-permute-start | bytes 294920 | tf_op jit(solution)/shard_map/ppermute | solution.py:217
  42.2 1.3 collective-permute-start.2
  43.8 3.3 %collective-permute-done.1.c2.o2 = bf16[4,24,512]{2,1,0:T(8,128)(2,1)S(1)} collective-permute-done((bf16[4,24,512]{2,1,0:T(8,128)(2,1)}, bf16[4,24,512]{2,1,0:T(8,128)(2,1)S(1)}, u32[]{:S(2)}, u32[]{:S(2)}) %collective-permute-start.1) | collective-permute-done | bytes 98336 | tf_op jit(solution)/shard_map/ppermute | solution.py:217
  47.1 0.9 copy-done.1
  48.0 2.2 %observe.1 = f32[96,128]{1,0:T(8,128)S(1)} custom-call(s32[1]{0:T(128)} %bitcast.me_ref, s32[24]{0:T(128)S(1)} %reshape.11.slots_ref, bf16[4,24,512]{2,1,0:T(8,128)(2,1)S(1)} %copy-done.1, bf16[4,24,512]{2,1,0:T(8,128)(2,1)S(1)} %collective-permute-done.c1.o1, bf16[4,24,512]{2,1,0:T(8,128)(2,1)S(1)} %collective-permute-done.1.c2.o2, ...), custom_call_target="tpu_custom_call" | custom-call | tf_op jit(solution)/shard_map/observe/pallas_call | solution.py:91
  50.3 1.2 collective-permute-done.3
  51.5 2.6 %collective-permute-start.6 = (f32[96,128]{1,0:T(8,128)S(1)}, f32[96,128]{1,0:T(8,128)S(1)}, u32[]{:S(2)}, u32[]{:S(2)}) collective-permute-start(f32[96,128]{1,0:T(8,128)S(1)} %add.30), channel_id=1, source_target_pairs={{0,96},{32,0},{64,32},{96,64},{1,97},{33,1},{65,33},{97,65},{2,98}... | collective-permute-start | bytes 147464 | tf_op jit(solution)/shard_map/ppermute | solution.py:222
  54.1 2.0 %collective-permute-start.4 = (f32[96,128]{1,0:T(8,128)S(1)}, f32[96,128]{1,0:T(8,128)S(1)}, u32[]{:S(2)}, u32[]{:S(2)}) collective-permute-start(f32[96,128]{1,0:T(8,128)S(1)} %add.30), channel_id=1, source_target_pairs={{0,64},{32,96},{64,0},{96,32},{1,65},{33,97},{65,1},{97,33},{2,66}... | collective-permute-start | bytes 147464 | tf_op jit(solution)/shard_map/ppermute | solution.py:222
  56.2 3.8 %collective-permute-done.5 = f32[96,128]{1,0:T(8,128)S(1)} collective-permute-done((f32[96,128]{1,0:T(8,128)S(1)}, f32[96,128]{1,0:T(8,128)S(1)}, u32[]{:S(2)}, u32[]{:S(2)}) %collective-permute-start.5) | collective-permute-done | bytes 49184 | tf_op jit(solution)/shard_map/ppermute | solution.py:222
  60.0 4.1 %collective-permute-start.9 = (f32[96,128]{1,0:T(8,128)S(1)}, f32[96,128]{1,0:T(8,128)S(1)}, u32[]{:S(2)}, u32[]{:S(2)}) collective-permute-start(f32[96,128]{1,0:T(8,128)S(1)} %add_add_fusion.2), channel_id=1, source_target_pairs={{0,6},{1,7},{2,0},{3,1},{4,2},{5,3},{6,4},{7,5},{8,14},{9,15},{10,... | collective-permute-start | bytes 147464 | tf_op jit(solution)/shard_map/ppermute | solution.py:224
  64.1 1.9 %collective-permute-start.7 = (f32[96,128]{1,0:T(8,128)S(1)}, f32[96,128]{1,0:T(8,128)S(1)}, u32[]{:S(2)}, u32[]{:S(2)}) collective-permute-start(f32[96,128]{1,0:T(8,128)S(1)} %add_add_fusion.2), channel_id=1, source_target_pairs={{0,4},{1,5},{2,6},{3,7},{4,0},{5,1},{6,2},{7,3},{8,12},{9,13},{10,... | collective-permute-start | bytes 147464 | tf_op jit(solution)/shard_map/ppermute | solution.py:224
  66.0 4.0 %collective-permute-done.8 = f32[96,128]{1,0:T(8,128)S(1)} collective-permute-done((f32[96,128]{1,0:T(8,128)S(1)}, f32[96,128]{1,0:T(8,128)S(1)}, u32[]{:S(2)}, u32[]{:S(2)}) %collective-permute-start.8) | collective-permute-done | bytes 49184 | tf_op jit(solution)/shard_map/ppermute | solution.py:224
  69.9 2.8 %collective-permute-start.12 = (f32[96,128]{1,0:T(8,128)S(1)}, f32[96,128]{1,0:T(8,128)S(1)}, u32[]{:S(2)}, u32[]{:S(2)}) collective-permute-start(f32[96,128]{1,0:T(8,128)S(1)} %add_add_fusion.1), channel_id=1, source_target_pairs={{0,24},{1,25},{2,26},{3,27},{4,28},{5,29},{6,30},{7,31},{8,0},{9,1... | collective-permute-start | bytes 147464 | tf_op jit(solution)/shard_map/ppermute | solution.py:226
  72.8 2.3 %collective-permute-start.10 = (f32[96,128]{1,0:T(8,128)S(1)}, f32[96,128]{1,0:T(8,128)S(1)}, u32[]{:S(2)}, u32[]{:S(2)}) collective-permute-start(f32[96,128]{1,0:T(8,128)S(1)} %add_add_fusion.1), channel_id=1, source_target_pairs={{0,16},{1,17},{2,18},{3,19},{4,20},{5,21},{6,22},{7,23},{8,24},{9,... | collective-permute-start | bytes 147464 | tf_op jit(solution)/shard_map/ppermute | solution.py:226
  75.5 4.0 %collective-permute-start.14 = (bf16[8,24,512]{2,1,0:T(8,128)(2,1)S(1)}, bf16[8,24,512]{2,1,0:T(8,128)(2,1)S(1)}, u32[]{:S(2)}, u32[]{:S(2)}) collective-permute-start(bf16[8,24,512]{2,1,0:T(8,128)(2,1)S(1)} %copy-done.13), channel_id=1, source_target_pairs={{0,64},{32,96},{64,0},{96,32},{1,65},{33,97},{65,1},{97,33},{2,66}... | collective-permute-start | bytes 589832 | tf_op jit(solution)/shard_map/ppermute | solution.py:217
  80.2 3.4 %transform.1.w_ref = f32[96,96]{1,0:T(8,128)} custom-call(f32[96,128]{1,0:T(8,128)} %add_add_fusion.sums_ref), custom_call_target="tpu_custom_call" | custom-call | tf_op jit(solution)/shard_map/transform/pallas_call | solution.py:133
  83.6 1.7 %collective-permute-done.14.r2 = bf16[8,24,512]{2,1,0:T(8,128)(2,1)S(1)} collective-permute-done((bf16[8,24,512]{2,1,0:T(8,128)(2,1)S(1)}, bf16[8,24,512]{2,1,0:T(8,128)(2,1)S(1)}, u32[]{:S(2)}, u32[]{:S(2)}) %collective-permute-start.14) | collective-permute-done | bytes 196640 | tf_op jit(solution)/shard_map/ppermute | solution.py:217
  87.4 0.8 collective-permute-start.16
  88.3 2.9 %collective-permute-start.17 = (bf16[12,24,512]{2,1,0:T(8,128)(2,1)S(1)}, bf16[12,24,512]{2,1,0:T(8,128)(2,1)S(1)}, u32[]{:S(2)}, u32[]{:S(2)}) collective-permute-start(bf16[12,24,512]{2,1,0:T(8,128)(2,1)S(1)} %get-tuple-element.24), channel_id=1, source_target_pairs={{0,64},{32,96},{64,0},{96,32},{1,65},{33,97},{65,1},{97,33},{2,66}... | collective-permute-start | bytes 884744 | tf_op jit(solution)/shard_map/ppermute | solution.py:217
  91.5 4.7 %collective-permute-done.16.c1 = bf16[12,24,512]{2,1,0:T(8,128)(2,1)S(1)} collective-permute-done((bf16[12,24,512]{2,1,0:T(8,128)(2,1)S(1)}, bf16[12,24,512]{2,1,0:T(8,128)(2,1)S(1)}, u32[]{:S(2)}, u32[]{:S(2)}) %collective-permute-start.16) | collective-permute-done | bytes 294944 | tf_op jit(solution)/shard_map/ppermute | solution.py:217
  96.2 3.2 %collective-permute-done.17.c2 = bf16[12,24,512]{2,1,0:T(8,128)(2,1)S(1)} collective-permute-done((bf16[12,24,512]{2,1,0:T(8,128)(2,1)S(1)}, bf16[12,24,512]{2,1,0:T(8,128)(2,1)S(1)}, u32[]{:S(2)}, u32[]{:S(2)}) %collective-permute-start.17) | collective-permute-done | bytes 294944 | tf_op jit(solution)/shard_map/ppermute | solution.py:217
  100.3 36.9 %place.1 = bf16[12,24,2048]{2,1,0:T(8,128)(2,1)} custom-call(s32[1]{0:T(128)} %bitcast.me_ref, bf16[12,24,512]{2,1,0:T(8,128)(2,1)} %copy-done.3, bf16[12,24,512]{2,1,0:T(8,128)(2,1)} %copy-done.6, bf16[12,24,512]{2,1,0:T(8,128)(2,1)} %copy-done.7, bf16[12,24,512]{2,1,0:T(8,128)(2,1)} %copy-done.8), custom_call_target="tpu_custom_call" | custom-call | tf_op jit(solution)/shard_map/place/pallas_call | solution.py:192
  (56 shorter events, 4.8 us)
Async XLA Ops:
  0.6 42.9 %copy-start.9 = (f32[12,1,128]{2,1,0:T(1,128)S(1)}, f32[12,1,128]{2,1,0:T(1,128)}, u32[]{:S(2)}) copy-start(f32[12,1,128]{2,1,0:T(1,128)} %param.7) | copy-start | bytes 18436
  0.6 42.9 %copy-start.10 = (f32[12,1,128]{2,1,0:T(1,128)S(1)}, f32[12,1,128]{2,1,0:T(1,128)}, u32[]{:S(2)}) copy-start(f32[12,1,128]{2,1,0:T(1,128)} %param.6) | copy-start | bytes 18436
  0.7 42.9 %copy-start.11 = (s32[12,1,2]{0,2,1:T(2,128)S(1)}, s32[12,1,2]{0,2,1:T(2,128)}, u32[]{:S(2)}) copy-start(s32[12,1,2]{0,2,1:T(2,128)} %param.9) | copy-start | bytes 292
  0.7 46.4 %copy-start = (bf16[12,1,2,128,128]{4,3,2,1,0:T(8,128)(2,1)S(1)}, bf16[12,1,2,128,128]{4,3,2,1,0:T(8,128)(2,1)}, u32[]{:S(2)}) copy-start(bf16[12,1,2,128,128]{4,3,2,1,0:T(8,128)(2,1)} %param.8) | copy-start | bytes 2359300
  37.6 6.2 %collective-permute-start = (bf16[4,24,512]{2,1,0:T(8,128)(2,1)}, bf16[4,24,512]{2,1,0:T(8,128)(2,1)S(1)}, u32[]{:S(2)}, u32[]{:S(2)}) collective-permute-start(bf16[4,24,512]{2,1,0:T(8,128)(2,1)} %get-tuple-element.15), channel_id=1, source_target_pairs={{0,32},{32,64},{64,96},{96,0},{1,33},{33,65},{65,97},{97,1},{2,34}... | collective-permute-start | bytes 294920 | tf_op jit(solution)/shard_map/ppermute | solution.py:217
  39.3 7.7 %collective-permute-start.1 = (bf16[4,24,512]{2,1,0:T(8,128)(2,1)}, bf16[4,24,512]{2,1,0:T(8,128)(2,1)S(1)}, u32[]{:S(2)}, u32[]{:S(2)}) collective-permute-start(bf16[4,24,512]{2,1,0:T(8,128)(2,1)} %get-tuple-element.16), channel_id=1, source_target_pairs={{0,64},{32,96},{64,0},{96,32},{1,65},{33,97},{65,1},{97,33},{2,66}... | collective-permute-start | bytes 294920 | tf_op jit(solution)/shard_map/ppermute | solution.py:217
  42.2 4.8 %collective-permute-start.2 = (bf16[4,24,512]{2,1,0:T(8,128)(2,1)}, bf16[4,24,512]{2,1,0:T(8,128)(2,1)S(1)}, u32[]{:S(2)}, u32[]{:S(2)}) collective-permute-start(bf16[4,24,512]{2,1,0:T(8,128)(2,1)} %get-tuple-element.17), channel_id=1, source_target_pairs={{0,96},{32,0},{64,32},{96,64},{1,97},{33,1},{65,33},{97,65},{2,98}... | collective-permute-start | bytes 294920 | tf_op jit(solution)/shard_map/ppermute | solution.py:217
  48.0 37.3 %copy-start.2 = (bf16[4,24,512]{2,1,0:T(8,128)(2,1)S(1)}, bf16[4,24,512]{2,1,0:T(8,128)(2,1)}, u32[]{:S(2)}) copy-start(bf16[4,24,512]{2,1,0:T(8,128)(2,1)} %get-tuple-element.14.c0.o0) | copy-start | bytes 294916
  50.2 1.3 collective-permute-start.3
  51.5 4.7 %collective-permute-start.6 = (f32[96,128]{1,0:T(8,128)S(1)}, f32[96,128]{1,0:T(8,128)S(1)}, u32[]{:S(2)}, u32[]{:S(2)}) collective-permute-start(f32[96,128]{1,0:T(8,128)S(1)} %add.30), channel_id=1, source_target_pairs={{0,96},{32,0},{64,32},{96,64},{1,97},{33,1},{65,33},{97,65},{2,98}... | collective-permute-start | bytes 147464 | tf_op jit(solution)/shard_map/ppermute | solution.py:222
  54.1 5.8 %collective-permute-start.5 = (f32[96,128]{1,0:T(8,128)S(1)}, f32[96,128]{1,0:T(8,128)S(1)}, u32[]{:S(2)}, u32[]{:S(2)}) collective-permute-start(f32[96,128]{1,0:T(8,128)S(1)} %add.30), channel_id=1, source_target_pairs={{0,32},{32,64},{64,96},{96,0},{1,33},{33,65},{65,97},{97,1},{2,34}... | collective-permute-start | bytes 147464 | tf_op jit(solution)/shard_map/ppermute | solution.py:222
  54.1 5.8 %collective-permute-start.4 = (f32[96,128]{1,0:T(8,128)S(1)}, f32[96,128]{1,0:T(8,128)S(1)}, u32[]{:S(2)}, u32[]{:S(2)}) collective-permute-start(f32[96,128]{1,0:T(8,128)S(1)} %add.30), channel_id=1, source_target_pairs={{0,64},{32,96},{64,0},{96,32},{1,65},{33,97},{65,1},{97,33},{2,66}... | collective-permute-start | bytes 147464 | tf_op jit(solution)/shard_map/ppermute | solution.py:222
  60.0 6.0 %collective-permute-start.9 = (f32[96,128]{1,0:T(8,128)S(1)}, f32[96,128]{1,0:T(8,128)S(1)}, u32[]{:S(2)}, u32[]{:S(2)}) collective-permute-start(f32[96,128]{1,0:T(8,128)S(1)} %add_add_fusion.2), channel_id=1, source_target_pairs={{0,6},{1,7},{2,0},{3,1},{4,2},{5,3},{6,4},{7,5},{8,14},{9,15},{10,... | collective-permute-start | bytes 147464 | tf_op jit(solution)/shard_map/ppermute | solution.py:224
  64.1 5.8 %collective-permute-start.8 = (f32[96,128]{1,0:T(8,128)S(1)}, f32[96,128]{1,0:T(8,128)S(1)}, u32[]{:S(2)}, u32[]{:S(2)}) collective-permute-start(f32[96,128]{1,0:T(8,128)S(1)} %add_add_fusion.2), channel_id=1, source_target_pairs={{0,2},{1,3},{2,4},{3,5},{4,6},{5,7},{6,0},{7,1},{8,10},{9,11},{10,... | collective-permute-start | bytes 147464 | tf_op jit(solution)/shard_map/ppermute | solution.py:224
  64.1 5.8 %collective-permute-start.7 = (f32[96,128]{1,0:T(8,128)S(1)}, f32[96,128]{1,0:T(8,128)S(1)}, u32[]{:S(2)}, u32[]{:S(2)}) collective-permute-start(f32[96,128]{1,0:T(8,128)S(1)} %add_add_fusion.2), channel_id=1, source_target_pairs={{0,4},{1,5},{2,6},{3,7},{4,0},{5,1},{6,2},{7,3},{8,12},{9,13},{10,... | collective-permute-start | bytes 147464 | tf_op jit(solution)/shard_map/ppermute | solution.py:224
  69.9 9.6 %collective-permute-start.12 = (f32[96,128]{1,0:T(8,128)S(1)}, f32[96,128]{1,0:T(8,128)S(1)}, u32[]{:S(2)}, u32[]{:S(2)}) collective-permute-start(f32[96,128]{1,0:T(8,128)S(1)} %add_add_fusion.1), channel_id=1, source_target_pairs={{0,24},{1,25},{2,26},{3,27},{4,28},{5,29},{6,30},{7,31},{8,0},{9,1... | collective-permute-start | bytes 147464 | tf_op jit(solution)/shard_map/ppermute | solution.py:226
  72.8 6.8 %collective-permute-start.11 = (f32[96,128]{1,0:T(8,128)S(1)}, f32[96,128]{1,0:T(8,128)S(1)}, u32[]{:S(2)}, u32[]{:S(2)}) collective-permute-start(f32[96,128]{1,0:T(8,128)S(1)} %add_add_fusion.1), channel_id=1, source_target_pairs={{0,8},{1,9},{2,10},{3,11},{4,12},{5,13},{6,14},{7,15},{8,16},{9,17... | collective-permute-start | bytes 147464 | tf_op jit(solution)/shard_map/ppermute | solution.py:226
  72.8 6.8 %collective-permute-start.10 = (f32[96,128]{1,0:T(8,128)S(1)}, f32[96,128]{1,0:T(8,128)S(1)}, u32[]{:S(2)}, u32[]{:S(2)}) collective-permute-start(f32[96,128]{1,0:T(8,128)S(1)} %add_add_fusion.1), channel_id=1, source_target_pairs={{0,16},{1,17},{2,18},{3,19},{4,20},{5,21},{6,22},{7,23},{8,24},{9,... | collective-permute-start | bytes 147464 | tf_op jit(solution)/shard_map/ppermute | solution.py:226
  75.1 8.6 %collective-permute-start.13 = (bf16[8,24,512]{2,1,0:T(8,128)(2,1)S(1)}, bf16[8,24,512]{2,1,0:T(8,128)(2,1)S(1)}, u32[]{:S(2)}, u32[]{:S(2)}) collective-permute-start(bf16[8,24,512]{2,1,0:T(8,128)(2,1)S(1)} %copy-done.14), channel_id=1, source_target_pairs={{0,32},{32,64},{64,96},{96,0},{1,33},{33,65},{65,97},{97,1},{2,34}... | collective-permute-start | bytes 589832 | tf_op jit(solution)/shard_map/ppermute | solution.py:217
  75.5 9.7 %collective-permute-start.14 = (bf16[8,24,512]{2,1,0:T(8,128)(2,1)S(1)}, bf16[8,24,512]{2,1,0:T(8,128)(2,1)S(1)}, u32[]{:S(2)}, u32[]{:S(2)}) collective-permute-start(bf16[8,24,512]{2,1,0:T(8,128)(2,1)S(1)} %copy-done.13), channel_id=1, source_target_pairs={{0,64},{32,96},{64,0},{96,32},{1,65},{33,97},{65,1},{97,33},{2,66}... | collective-permute-start | bytes 589832 | tf_op jit(solution)/shard_map/ppermute | solution.py:217
  79.5 5.7 %collective-permute-start.15 = (bf16[8,24,512]{2,1,0:T(8,128)(2,1)S(1)}, bf16[8,24,512]{2,1,0:T(8,128)(2,1)S(1)}, u32[]{:S(2)}, u32[]{:S(2)}) collective-permute-start(bf16[8,24,512]{2,1,0:T(8,128)(2,1)S(1)} %copy-done.12), channel_id=1, source_target_pairs={{0,96},{32,0},{64,32},{96,64},{1,97},{33,1},{65,33},{97,65},{2,98}... | collective-permute-start | bytes 589832 | tf_op jit(solution)/shard_map/ppermute | solution.py:217
  87.4 8.8 %collective-permute-start.16 = (bf16[12,24,512]{2,1,0:T(8,128)(2,1)S(1)}, bf16[12,24,512]{2,1,0:T(8,128)(2,1)S(1)}, u32[]{:S(2)}, u32[]{:S(2)}) collective-permute-start(bf16[12,24,512]{2,1,0:T(8,128)(2,1)S(1)} %get-tuple-element.23), channel_id=1, source_target_pairs={{0,32},{32,64},{64,96},{96,0},{1,33},{33,65},{65,97},{97,1},{2,34}... | collective-permute-start | bytes 884744 | tf_op jit(solution)/shard_map/ppermute | solution.py:217
  88.3 11.1 %collective-permute-start.17 = (bf16[12,24,512]{2,1,0:T(8,128)(2,1)S(1)}, bf16[12,24,512]{2,1,0:T(8,128)(2,1)S(1)}, u32[]{:S(2)}, u32[]{:S(2)}) collective-permute-start(bf16[12,24,512]{2,1,0:T(8,128)(2,1)S(1)} %get-tuple-element.24), channel_id=1, source_target_pairs={{0,64},{32,96},{64,0},{96,32},{1,65},{33,97},{65,1},{97,33},{2,66}... | collective-permute-start | bytes 884744 | tf_op jit(solution)/shard_map/ppermute | solution.py:217
  91.2 8.4 %collective-permute-start.18 = (bf16[12,24,512]{2,1,0:T(8,128)(2,1)S(1)}, bf16[12,24,512]{2,1,0:T(8,128)(2,1)S(1)}, u32[]{:S(2)}, u32[]{:S(2)}) collective-permute-start(bf16[12,24,512]{2,1,0:T(8,128)(2,1)S(1)} %get-tuple-element.25), channel_id=1, source_target_pairs={{0,96},{32,0},{64,32},{96,64},{1,97},{33,1},{65,33},{97,65},{2,98}... | collective-permute-start | bytes 884744 | tf_op jit(solution)/shard_map/ppermute | solution.py:217
  (10 other events, 130.8 us)

commit v2 on v1

--- a/solution.py
+++ b/solution.py
@@ -3,6 +3,7 @@
 from jax import lax
 from jax.experimental import pallas as pl
 from jax.experimental.pallas import tpu as pltpu
+from jax.sharding import Mesh
 from jax.sharding import PartitionSpec as P
 
 K = 96
@@ -14,6 +15,8 @@
 BLOCKS = 12
 NNZ = 2
 NS_ITERS = 4
+HALF = K // 2
+CHIPS = 64
 
 EXACT = lax.Precision.HIGHEST
 VMEM = pl.BlockSpec(memory_space=pltpu.VMEM)
@@ -54,11 +57,42 @@
         pack_kernel,
         out_shape=shapes,
         in_specs=[SMEM, ANY],
-        out_specs=[ANY] * len(shapes),
+        out_specs=[VMEM] * len(shapes),
         scratch_shapes=[pltpu.SemaphoreType.DMA((2 * GROUPS,))],
         name="pack",
     )(me, prior)
     return outs[:GROUPS], outs[GROUPS:]
+
+
+def indices():
+    row = lax.broadcasted_iota(jnp.int32, (HALF, 128), 0)
+    lane = lax.broadcasted_iota(jnp.int32, (HALF, 128), 1)
+    return row, lane
+
+
+def fold(gram):
+    row, lane = indices()
+    top, low = gram[:HALF], gram[HALF:]
+    second = pltpu.roll(low, 128 - HALF, 1)
+    diagonal = jnp.sum(jnp.where(lane == row, second, 0.0), axis=1, keepdims=True)
+    tail = jnp.sum(jnp.where(lane == HALF, second, 0.0), axis=1, keepdims=True)
+    out = jnp.where((lane < HALF) & (lane > row), second, top)
+    out = jnp.where(lane == K + 1, tail, out)
+    return jnp.where(lane == K + 2, diagonal, out)
+
+
+def unfold(folded):
+    row, lane = indices()
+    turned = jnp.concatenate([folded, jnp.zeros((128 - HALF, 128), jnp.float32)], axis=0).T
+    flipped = turned[:HALF]
+    first = jnp.where(lane <= row, folded, flipped)
+    diagonal = folded[:, K + 2 : K + 3]
+    second = jnp.where(lane < row, flipped, jnp.where(lane == row, diagonal, folded))
+    top = jnp.where(lane < HALF, first, folded)
+    low = jnp.where(lane < HALF, turned[HALF:K], pltpu.roll(second, HALF, 1))
+    gram = jnp.concatenate([top, low], axis=0)[:, :K]
+    projected = jnp.concatenate([folded[:, K : K + 1], folded[:, K + 1 : K + 2]], axis=0)
+    return gram, projected
 
 
 def observe_kernel(me_ref, slots_ref, c0, c1, c2, c3, op_ref, y_ref, var_ref, out_ref, state, spread, scaled):
@@ -82,15 +116,16 @@
         spread[:K, lanes] = dev
         spread[K : K + 1, lanes] = y_ref[b : b + 1, :] - mean
         scaled[:, lanes] = dev / var_ref[b : b + 1, :]
-    out_ref[...] = lax.dot_general(
+    gram = lax.dot_general(
         scaled[...], spread[...], (((1,), (1,)), ((), ())), precision=EXACT, preferred_element_type=jnp.float32
     )
+    out_ref[...] = fold(gram)
 
 
 def observe(me, slots, chunks, op, values, variances):
     return pl.pallas_call(
         observe_kernel,
-        out_shape=jax.ShapeDtypeStruct((K, 128), jnp.float32),
+        out_shape=jax.ShapeDtypeStruct((HALF, 128), jnp.float32),
         in_specs=[SMEM, SMEM] + [VMEM] * 7,
         out_specs=VMEM,
         scratch_shapes=[
@@ -103,40 +138,51 @@
     )(me, slots, *chunks, op, values, variances)
 
 
-def exact_dot(a, b):
-    return jnp.dot(a, b, precision=EXACT, preferred_element_type=jnp.float32)
-
-
-def weights_kernel(sums_ref, weights_ref):
-    sums = sums_ref[...]
+def split(a):
+    high = a.astype(jnp.bfloat16)
+    return high, (a - high.astype(jnp.float32)).astype(jnp.bfloat16)
+
+
+def fine_dot(a, b):
+    a_high, a_low = split(a)
+    b_high, b_low = split(b)
+    small = jnp.dot(a_high, b_low, preferred_element_type=jnp.float32)
+    small += jnp.dot(a_low, b_high, preferred_element_type=jnp.float32)
+    return small + jnp.dot(a_high, b_high, preferred_element_type=jnp.float32)
+
+
+def transform_kernel(core_ref, mine_ref, other_ref, weights_ref):
+    first = core_ref[0] == 0
+    mine, other = mine_ref[...], other_ref[...]
+    folded = jnp.concatenate([jnp.where(first, mine, other), jnp.where(first, other, mine)], axis=0)
+    gram, projected = unfold(folded)
     row = lax.broadcasted_iota(jnp.int32, (K, K), 0)
     col = lax.broadcasted_iota(jnp.int32, (K, K), 1)
     eye = jnp.where(row == col, 1.0, 0.0).astype(jnp.float32)
-    system = sums[:, :K] + (K - 1.0) * eye
-    projected = sums[:, K : K + 1]
+    system = gram + (K - 1.0) * eye
     frob = jnp.sqrt(jnp.sum(system * system, keepdims=True))
     root = system / frob
     inverse = None
     for step in range(NS_ITERS):
-        product = root if inverse is None else exact_dot(inverse, root)
+        product = root if inverse is None else fine_dot(inverse, root)
         factor = 1.5 * eye - 0.5 * product
         if step < NS_ITERS - 1:
-            root = exact_dot(root, factor)
-        inverse = factor if inverse is None else exact_dot(factor, inverse)
+            root = fine_dot(root, factor)
+        inverse = factor if inverse is None else fine_dot(factor, inverse)
     inverse_root = inverse / jnp.sqrt(frob)
-    covariance = exact_dot(inverse_root, inverse_root)
-    mean_shift = exact_dot(covariance, projected)
+    halfway = jnp.sum(inverse_root * projected, axis=0, keepdims=True)
+    mean_shift = jnp.sum(inverse_root * halfway, axis=1, keepdims=True)
     weights_ref[...] = mean_shift + (K - 1.0) ** 0.5 * inverse_root
 
 
-def make_weights(sums):
-    return pl.pallas_call(
-        weights_kernel,
+def transform(core, mine, other):
+    return pl.pallas_call(
+        transform_kernel,
         out_shape=jax.ShapeDtypeStruct((K, K), jnp.float32),
-        in_specs=[VMEM],
+        in_specs=[SMEM, VMEM, VMEM],
         out_specs=VMEM,
         name="transform",
-    )(sums)
+    )(core, mine, other)
 
 
 def analyse_kernel(me_ref, w_ref, o0, o1, o2, o3, r0, r1, r2, r3, a0, a1, a2, a3, turned):
@@ -192,7 +238,7 @@
     return pl.pallas_call(
         place_kernel,
         out_shape=jax.ShapeDtypeStruct((V, MEMBERS, GROUPS * TILE), jnp.bfloat16),
-        in_specs=[SMEM] + [ANY] * GROUPS,
+        in_specs=[SMEM] + [VMEM] * GROUPS,
         out_specs=ANY,
         scratch_shapes=[pltpu.SemaphoreType.DMA((GROUPS,))],
         name="place",
@@ -203,51 +249,45 @@
     return [(i, (i + shift) % GROUPS) for i in range(GROUPS)]
 
 
-def space_shift(dx, dz, dc):
-    pairs = []
-    for x in range(4):
-        for z in range(4):
-            for c in range(2):
-                to = ((x + dx) % 4) * 8 + ((z + dz) % 4) * 2 + (c + dc) % 2
-                pairs.append((x * 8 + z * 2 + c, to))
-    return pairs
-
-
 def scatter(chunks):
     return [chunks[0]] + [lax.ppermute(chunks[s], "member", ring(s)) for s in range(1, GROUPS)]
 
 
-def total(x):
-    x = x + lax.ppermute(x, "space", space_shift(0, 0, 1))
-    parts = [lax.ppermute(x, "member", ring(s)) for s in (2, 1, 3)]
-    x = (x + parts[0]) + (parts[1] + parts[2])
-    parts = [lax.ppermute(x, "space", space_shift(0, s, 0)) for s in (2, 1, 3)]
-    x = (x + parts[0]) + (parts[1] + parts[2])
-    parts = [lax.ppermute(x, "space", space_shift(s, 0, 0)) for s in (2, 1, 3)]
-    return (x + parts[0]) + (parts[1] + parts[2])
+def swap(x):
+    return lax.ppermute(x, "core", [(0, 1), (1, 0)])
+
+
+def total(core, folded):
+    first = core[0] == 0
+    top, low = folded[: HALF // 2], folded[HALF // 2 :]
+    chip = jnp.where(first, top, low) + swap(jnp.where(first, low, top))
+    copies = jnp.broadcast_to(chip[None], (CHIPS, HALF // 2, 128))
+    mine = jnp.sum(lax.all_to_all(copies, ("member", "x", "z"), 0, 0, tiled=True), axis=0)
+    return mine, swap(mine)
 
 
 def body(prior, readings, error_spread, mapping, slots):
     me = lax.axis_index("member").astype(jnp.int32).reshape(1)
+    core = lax.axis_index("core").astype(jnp.int32).reshape(1)
     observed_out, rest_out = pack(me, jnp.transpose(prior, (1, 0, 2)))
     observed = scatter(observed_out)
     rest = scatter(rest_out)
-    sums = total(
-        observe(me, slots.reshape(-1), observed, mapping[:, 0], readings[:, 0], error_spread[:, 0])
+    folded = observe(me, slots.reshape(-1), observed, mapping[:, 0], readings[:, 0], error_spread[:, 0])
+    weights = transform(core, *total(core, folded))
+    out = place(me, scatter(analyse(me, weights, observed, rest)))
+    return (jnp.transpose(out, (1, 0, 2)), weights)
+
+
+def solution(mesh):
+    devices = mesh.devices.reshape(GROUPS, 4, 4, 2)
+    axes = Mesh(devices, ("member", "x", "z", "core"))
+    space = ("x", "z", "core")
+    in_specs = (
+        P("member", None, space),
+        P(space, "member", None),
+        P(space, "member", None),
+        P(space, "member", None, None, None),
+        P(space, "member", None),
     )
-    weights = make_weights(sums)
-    chunks = analyse(me, weights, observed, rest)
-    out = place(me, scatter(chunks))
-    return (jnp.transpose(out, (1, 0, 2)), weights)
-
-
-def solution(mesh):
-    in_specs = (
-        P("member", None, "space"),
-        P("space", "member", None),
-        P("space", "member", None),
-        P("space", "member", None, None, None),
-        P("space", "member", None),
-    )
-    out_specs = (P("member", None, "space"), P())
-    return jax.shard_map(body, mesh=mesh, in_specs=in_specs, out_specs=out_specs, check_vma=False)
+    out_specs = (P("member", None, space), P())
+    return jax.shard_map(body, mesh=axes, in_specs=in_specs, out_specs=out_specs, check_vma=False)

time: 138 us -> 73 us (0.53)
  Pallas kernels: 80 us -> 10.6 us
  waiting for transfers between devices: 22 us -> 30 us
  starting transfers between devices: 30.3 us -> 26.2 us
  local copies, waits for them, and re-layouts: 3.35 us -> 4.86 us
    pallas_call x1, Pallas kernels: 36.9 us -> 2.27 us  [place(): pl.pallas_call(place_kernel, out_shape=jax.ShapeDtypeStruct((V, MEMBERS,...]
    pallas_call x1, Pallas kernels: 36.9 us -> 2.49 us  [pack(): pl.pallas_call(pack_kernel, out_shape=shapes, in_specs=[SMEM, ANY], out_s...]
    ppermute x10 -> x2, starting transfers between devices: 15.8 us -> 0.17 us  [swap(): return lax.ppermute(x, 'core', [(0, 1), (1, 0)])]
    all_to_all x0 -> x1, starting transfers between devices: none -> 10.9 us  [total(): lax.all_to_all(copies, ('member', 'x', 'z'), 0, 0, tiled=True)]
    all_to_all x0 -> x1, waiting for transfers between devices: none -> 10.4 us  [total(): lax.all_to_all(copies, ('member', 'x', 'z'), 0, 0, tiled=True)]
    ppermute x10 -> x2, waiting for transfers between devices: 8.97 us -> 2.33 us  [swap(): return lax.ppermute(x, 'core', [(0, 1), (1, 0)])]
    ppermute x9, waiting for transfers between devices: 13 us -> 17.2 us  [scatter(): lax.ppermute(chunks[s], 'member', ring(s))]
    unnamed x32 -> x36, local copies, waits for them, and re-layouts: 3.27 us -> 3.85 us
  transfers between devices with their start and end apart: 19 -> 12, of which waited for: 8 -> 6; matrix products, arithmetic and copies ran while one was open for 1% -> 0% of each run, Pallas kernels for 2% -> 4%
where the time goes in v2:
time: 73 us; the launch traced here: 72.6 us
  waiting for transfers between devices  30 us (41%)
  starting transfers between devices  26.2 us (36%)
  Pallas kernels  10.6 us (15%)
  local copies, waits for them, and re-layouts  4.86 us (7%)
  between operations  0.83 us (1%)
    ppermute x9, waiting for transfers between devices, scatter(): lax.ppermute(chunks[s], 'member', ring(s))  17.2 us
    ppermute x9, starting transfers between devices, scatter(): lax.ppermute(chunks[s], 'member', ring(s))  15.1 us
    all_to_all x1, starting transfers between devices, total(): lax.all_to_all(copies, ('member', 'x', 'z'), 0, 0, tiled=True)  10.9 us
    all_to_all x1, waiting for transfers between devices, total(): lax.all_to_all(copies, ('member', 'x', 'z'), 0, 0, tiled=True)  10.4 us
    unnamed x36, local copies, waits for them, and re-layouts  3.85 us
    pallas_call x1, Pallas kernels, transform(): pl.pallas_call(transform_kernel, out_shape=jax.ShapeDtypeStruct((K, K), j...  2.88 us
    pallas_call x1, Pallas kernels, pack(): pl.pallas_call(pack_kernel, out_shape=shapes, in_specs=[SMEM, ANY], out_s...  2.49 us
    pallas_call x1, Pallas kernels, observe(): pl.pallas_call(observe_kernel, out_shape=jax.ShapeDtypeStruct((HALF, 128)...  2.36 us
  transfers between devices with their start and end apart: 12, of which 6 were waited for; matrix products, arithmetic and copies ran while one was open for 0% of the time, Pallas kernels for 4%

profile of v2, /device:TPU:0, one launch (start us, length us, event | category | flops | bytes accessed | tf_op | source)
XLA Modules:
  0.0 72.6 jit_solution(6145599608218239792)
XLA Ops:
  0.7 2.5 %pack.1 = (bf16[4,24,512]{2,1,0:T(8,128)(2,1)}, bf16[4,24,512]{2,1,0:T(8,128)(2,1)}, bf16[4,24,512]{2,1,0:T(8,128)(2,1)}, bf16[4,24,512]{2,1,0:T(8,128)(2,1)}, b...) custom-call(s32[1]{0:T(128)} %bitcast.me_ref, ...), custom_call_target="tpu_custom_call" | custom-call | tf_op jit(solution)/shard_map/pack/pallas_call | solution.py:56
  3.2 1.7 %collective-permute-start = (bf16[4,24,512]{2,1,0:T(8,128)(2,1)}, bf16[4,24,512]{2,1,0:T(8,128)(2,1)S(1)}, u32[]{:S(2)}, u32[]{:S(2)}) collective-permute-start(bf16[4,24,512]{2,1,0:T(8,128)(2,1)} %get-tuple-element.15), channel_id=1, source_target_pairs={{0,32},{32,64},{64,96},{96,0},{1,33},{33,65},{65,97},{97,1},{2,34}... | collective-permute-start | bytes 294920 | tf_op jit(solution)/shard_map/ppermute | solution.py:253
  4.9 2.9 %collective-permute-start.1 = (bf16[4,24,512]{2,1,0:T(8,128)(2,1)}, bf16[4,24,512]{2,1,0:T(8,128)(2,1)S(1)}, u32[]{:S(2)}, u32[]{:S(2)}) collective-permute-start(bf16[4,24,512]{2,1,0:T(8,128)(2,1)} %get-tuple-element.16), channel_id=1, source_target_pairs={{0,64},{32,96},{64,0},{96,32},{1,65},{33,97},{65,1},{97,33},{2,66}... | collective-permute-start | bytes 294920 | tf_op jit(solution)/shard_map/ppermute | solution.py:253
  7.8 1.3 %collective-permute-start.2 = (bf16[4,24,512]{2,1,0:T(8,128)(2,1)}, bf16[4,24,512]{2,1,0:T(8,128)(2,1)S(1)}, u32[]{:S(2)}, u32[]{:S(2)}) collective-permute-start(bf16[4,24,512]{2,1,0:T(8,128)(2,1)} %get-tuple-element.17), channel_id=1, source_target_pairs={{0,96},{32,0},{64,32},{96,64},{1,97},{33,1},{65,33},{97,65},{2,98}... | collective-permute-start | bytes 294920 | tf_op jit(solution)/shard_map/ppermute | solution.py:253
  9.4 3.3 %collective-permute-done.1.c2.o2 = bf16[4,24,512]{2,1,0:T(8,128)(2,1)S(1)} collective-permute-done((bf16[4,24,512]{2,1,0:T(8,128)(2,1)}, bf16[4,24,512]{2,1,0:T(8,128)(2,1)S(1)}, u32[]{:S(2)}, u32[]{:S(2)}) %collective-permute-start.1) | collective-permute-done | bytes 98336 | tf_op jit(solution)/shard_map/ppermute | solution.py:253
  12.6 0.9 %copy-done.1 = bf16[4,24,512]{2,1,0:T(8,128)(2,1)S(1)} copy-done((bf16[4,24,512]{2,1,0:T(8,128)(2,1)S(1)}, bf16[4,24,512]{2,1,0:T(8,128)(2,1)}, u32[]{:S(2)}) %copy-start.1) | copy-done | bytes 98328
  13.5 2.4 %observe.1 = f32[48,128]{1,0:T(8,128)S(1)} custom-call(s32[1]{0:T(128)} %bitcast.me_ref, s32[24]{0:T(128)S(1)} %reshape.16.slots_ref, bf16[4,24,512]{2,1,0:T(8,128)(2,1)S(1)} %copy-done.1, bf16[4,24,512]{2,1,0:T(8,128)(2,1)S(1)} %collective-permute-done.c1.o1, bf16[4,24,512]{2,1,0:T(8,128)(2,1)S(1)} %collective-permute-done.1.c2.o2, ...), custom_call_target="tpu_custom_call" | custom-call | tf_op jit(solution)/shard_map/observe/pallas_call | solution.py:126
  16.0 1.2 %collective-permute-done.3 = f32[24,128]{1,0:T(8,128)S(1)} collective-permute-done((f32[24,128]{1,0:T(8,128)S(1)}, f32[24,128]{1,0:T(8,128)S(1)}, u32[]{:S(2)}, u32[]{:S(2)}) %collective-permute-start.3) | collective-permute-done | bytes 12320 | tf_op jit(solution)/shard_map/ppermute | solution.py:257
  17.2 0.9 %broadcast_in_dim.2 = f32[64,24,128]{2,1,0:T(8,128)} broadcast(f32[24,128]{1,0:T(8,128)S(1)} %select_add_fusion), dimensions={1,2} | broadcast | bytes 798720 | tf_op jit(solution)/shard_map/broadcast_in_dim | solution.py:264
  18.1 10.9 %all-to-all-start = ((f32[64,24,128]{2,1,0:T(8,128)}), f32[64,24,128]{2,1,0:T(8,128)S(1)}, u32[]{:S(2)}, u32[]{:S(2)}) async-start(f32[64,24,128]{2,1,0:T(8,128)} %broadcast_in_dim.2), calls=%async_computation | async-start | bytes 1572864 | tf_op jit(solution)/shard_map/all_to_all | solution.py:265
  29.1 1.6 %collective-permute-start.5 = (bf16[8,24,512]{2,1,0:T(8,128)(2,1)S(1)}, bf16[8,24,512]{2,1,0:T(8,128)(2,1)S(1)}, u32[]{:S(2)}, u32[]{:S(2)}) collective-permute-start(bf16[8,24,512]{2,1,0:T(8,128)(2,1)S(1)} %copy-done.16), channel_id=1, source_target_pairs={{0,32},{32,64},{64,96},{96,0},{1,33},{33,65},{65,97},{97,1},{2,34}... | collective-permute-start | bytes 589832 | tf_op jit(solution)/shard_map/ppermute | solution.py:253
  30.7 2.9 %collective-permute-start.6 = (bf16[8,24,512]{2,1,0:T(8,128)(2,1)S(1)}, bf16[8,24,512]{2,1,0:T(8,128)(2,1)S(1)}, u32[]{:S(2)}, u32[]{:S(2)}) collective-permute-start(bf16[8,24,512]{2,1,0:T(8,128)(2,1)S(1)} %copy-done.15), channel_id=1, source_target_pairs={{0,64},{32,96},{64,0},{96,32},{1,65},{33,97},{65,1},{97,33},{2,66}... | collective-permute-start | bytes 589832 | tf_op jit(solution)/shard_map/ppermute | solution.py:253
  33.6 1.4 %collective-permute-start.7 = (bf16[8,24,512]{2,1,0:T(8,128)(2,1)S(1)}, bf16[8,24,512]{2,1,0:T(8,128)(2,1)S(1)}, u32[]{:S(2)}, u32[]{:S(2)}) collective-permute-start(bf16[8,24,512]{2,1,0:T(8,128)(2,1)S(1)} %copy-done.14), channel_id=1, source_target_pairs={{0,96},{32,0},{64,32},{96,64},{1,97},{33,1},{65,33},{97,65},{2,98}... | collective-permute-start | bytes 589832 | tf_op jit(solution)/shard_map/ppermute | solution.py:253
  34.9 10.4 %all-to-all-done = f32[64,24,128]{2,1,0:T(8,128)S(1)} async-done(((f32[64,24,128]{2,1,0:T(8,128)}), f32[64,24,128]{2,1,0:T(8,128)S(1)}, u32[]{:S(2)}, u32[]{:S(2)}) %all-to-all-start) | async-done | bytes 786464 | tf_op jit(solution)/shard_map/all_to_all | solution.py:265
  45.6 1.2 %collective-permute-done.4.other_ref = f32[24,128]{1,0:T(8,128)S(1)} collective-permute-done((f32[24,128]{1,0:T(8,128)S(1)}, f32[24,128]{1,0:T(8,128)S(1)}, u32[]{:S(2)}, u32[]{:S(2)}) %collective-permute-start.4) | collective-permute-done | bytes 12320 | tf_op jit(solution)/shard_map/ppermute | solution.py:257
  47.4 2.9 %transform.1.w_ref = f32[96,96]{1,0:T(8,128)} custom-call(s32[1]{0:T(128)} %bitcast.1.core_ref, f32[24,128]{1,0:T(8,128)} %copy-done.9, f32[24,128]{1,0:T(8,128)} %copy-done.10), custom_call_target="tpu_custom_call" | custom-call | tf_op jit(solution)/shard_map/transform/pallas_call | solution.py:179
  50.3 0.8 %copy-done.4 = f32[96,96]{1,0:T(8,128)S(1)} copy-done((f32[96,96]{1,0:T(8,128)S(1)}, f32[96,96]{1,0:T(8,128)}, u32[]{:S(2)}) %copy-start.4) | copy-done | bytes 36888
  51.1 0.6 analyse.1
  51.7 0.7 copy-done.3
  52.6 2.0 %collective-permute-start.9 = (bf16[12,24,512]{2,1,0:T(8,128)(2,1)S(1)}, bf16[12,24,512]{2,1,0:T(8,128)(2,1)S(1)}, u32[]{:S(2)}, u32[]{:S(2)}) collective-permute-start(bf16[12,24,512]{2,1,0:T(8,128)(2,1)S(1)} %get-tuple-element.24), channel_id=1, source_target_pairs={{0,64},{32,96},{64,0},{96,32},{1,65},{33,97},{65,1},{97,33},{2,66}... | collective-permute-start | bytes 884744 | tf_op jit(solution)/shard_map/ppermute | solution.py:253
  54.7 1.0 %collective-permute-start.10 = (bf16[12,24,512]{2,1,0:T(8,128)(2,1)S(1)}, bf16[12,24,512]{2,1,0:T(8,128)(2,1)S(1)}, u32[]{:S(2)}, u32[]{:S(2)}) collective-permute-start(bf16[12,24,512]{2,1,0:T(8,128)(2,1)S(1)} %get-tuple-element.25), channel_id=1, source_target_pairs={{0,96},{32,0},{64,32},{96,64},{1,97},{33,1},{65,33},{97,65},{2,98}... | collective-permute-start | bytes 884744 | tf_op jit(solution)/shard_map/ppermute | solution.py:253
  55.7 13.3 %collective-permute-done.8.c1 = bf16[12,24,512]{2,1,0:T(8,128)(2,1)S(1)} collective-permute-done((bf16[12,24,512]{2,1,0:T(8,128)(2,1)S(1)}, bf16[12,24,512]{2,1,0:T(8,128)(2,1)S(1)}, u32[]{:S(2)}, u32[]{:S(2)}) %collective-permute-start.8) | collective-permute-done | bytes 294944 | tf_op jit(solution)/shard_map/ppermute | solution.py:253
  69.0 0.6 collective-permute-done.10.c3
  70.4 2.3 %place.1 = bf16[12,24,2048]{2,1,0:T(8,128)(2,1)} custom-call(s32[1]{0:T(128)} %bitcast.me_ref, bf16[12,24,512]{2,1,0:T(8,128)(2,1)} %copy-done.3, bf16[12,24,512]{2,1,0:T(8,128)(2,1)} %copy-done.6, bf16[12,24,512]{2,1,0:T(8,128)(2,1)} %copy-done.7, bf16[12,24,512]{2,1,0:T(8,128)(2,1)} %copy-done.8), custom_call_target="tpu_custom_call" | custom-call | tf_op jit(solution)/shard_map/place/pallas_call | solution.py:238
  (46 shorter events, 2.1 us)
Async XLA Ops:
  0.6 8.5 %copy-start.11 = (f32[12,1,128]{2,1,0:T(1,128)S(1)}, f32[12,1,128]{2,1,0:T(1,128)}, u32[]{:S(2)}) copy-start(f32[12,1,128]{2,1,0:T(1,128)} %param.7) | copy-start | bytes 18436
  0.6 8.5 %copy-start.12 = (f32[12,1,128]{2,1,0:T(1,128)S(1)}, f32[12,1,128]{2,1,0:T(1,128)}, u32[]{:S(2)}) copy-start(f32[12,1,128]{2,1,0:T(1,128)} %param.6) | copy-start | bytes 18436
  0.7 8.5 %copy-start.13 = (s32[12,1,2]{0,2,1:T(2,128)S(1)}, s32[12,1,2]{0,2,1:T(2,128)}, u32[]{:S(2)}) copy-start(s32[12,1,2]{0,2,1:T(2,128)} %param.9) | copy-start | bytes 292
  0.7 12.0 %copy-start = (bf16[12,1,2,128,128]{4,3,2,1,0:T(8,128)(2,1)S(1)}, bf16[12,1,2,128,128]{4,3,2,1,0:T(8,128)(2,1)}, u32[]{:S(2)}) copy-start(bf16[12,1,2,128,128]{4,3,2,1,0:T(8,128)(2,1)} %param.8) | copy-start | bytes 2359300
  3.2 6.2 %collective-permute-start = (bf16[4,24,512]{2,1,0:T(8,128)(2,1)}, bf16[4,24,512]{2,1,0:T(8,128)(2,1)S(1)}, u32[]{:S(2)}, u32[]{:S(2)}) collective-permute-start(bf16[4,24,512]{2,1,0:T(8,128)(2,1)} %get-tuple-element.15), channel_id=1, source_target_pairs={{0,32},{32,64},{64,96},{96,0},{1,33},{33,65},{65,97},{97,1},{2,34}... | collective-permute-start | bytes 294920 | tf_op jit(solution)/shard_map/ppermute | solution.py:253
  4.9 7.7 %collective-permute-start.1 = (bf16[4,24,512]{2,1,0:T(8,128)(2,1)}, bf16[4,24,512]{2,1,0:T(8,128)(2,1)S(1)}, u32[]{:S(2)}, u32[]{:S(2)}) collective-permute-start(bf16[4,24,512]{2,1,0:T(8,128)(2,1)} %get-tuple-element.16), channel_id=1, source_target_pairs={{0,64},{32,96},{64,0},{96,32},{1,65},{33,97},{65,1},{97,33},{2,66}... | collective-permute-start | bytes 294920 | tf_op jit(solution)/shard_map/ppermute | solution.py:253
  7.8 4.8 %collective-permute-start.2 = (bf16[4,24,512]{2,1,0:T(8,128)(2,1)}, bf16[4,24,512]{2,1,0:T(8,128)(2,1)S(1)}, u32[]{:S(2)}, u32[]{:S(2)}) collective-permute-start(bf16[4,24,512]{2,1,0:T(8,128)(2,1)} %get-tuple-element.17), channel_id=1, source_target_pairs={{0,96},{32,0},{64,32},{96,64},{1,97},{33,1},{65,33},{97,65},{2,98}... | collective-permute-start | bytes 294920 | tf_op jit(solution)/shard_map/ppermute | solution.py:253
  12.6 0.9 %copy-start.1 = (bf16[4,24,512]{2,1,0:T(8,128)(2,1)S(1)}, bf16[4,24,512]{2,1,0:T(8,128)(2,1)}, u32[]{:S(2)}) copy-start(bf16[4,24,512]{2,1,0:T(8,128)(2,1)} %get-tuple-element.14.c0.o0) | copy-start | bytes 294916
  15.9 1.3 %collective-permute-start.3 = (f32[24,128]{1,0:T(8,128)S(1)}, f32[24,128]{1,0:T(8,128)S(1)}, u32[]{:S(2)}, u32[]{:S(2)}) collective-permute-start(f32[24,128]{1,0:T(8,128)S(1)} %slice_select_fusion), channel_id=1, source_target_pairs={{0,1},{1,0},{2,3},{3,2},{4,5},{5,4},{6,7},{7,6},{8,9},{9,8},{10,11... | collective-permute-start | bytes 36872 | tf_op jit(solution)/shard_map/ppermute | solution.py:257
  17.2 11.9 %copy-start.16 = (bf16[8,24,512]{2,1,0:T(8,128)(2,1)S(1)}, bf16[8,24,512]{2,1,0:T(8,128)(2,1)}, u32[]{:S(2)}) copy-start(bf16[8,24,512]{2,1,0:T(8,128)(2,1)} %get-tuple-element.19) | copy-start | bytes 589828
  17.2 13.5 %copy-start.15 = (bf16[8,24,512]{2,1,0:T(8,128)(2,1)S(1)}, bf16[8,24,512]{2,1,0:T(8,128)(2,1)}, u32[]{:S(2)}) copy-start(bf16[8,24,512]{2,1,0:T(8,128)(2,1)} %get-tuple-element.20) | copy-start | bytes 589828
  17.2 16.4 %copy-start.14 = (bf16[8,24,512]{2,1,0:T(8,128)(2,1)S(1)}, bf16[8,24,512]{2,1,0:T(8,128)(2,1)}, u32[]{:S(2)}) copy-start(bf16[8,24,512]{2,1,0:T(8,128)(2,1)} %get-tuple-element.21) | copy-start | bytes 589828
  18.1 32.1 %copy-start.2 = (bf16[4,24,512]{2,1,0:T(8,128)(2,1)S(1)}, bf16[4,24,512]{2,1,0:T(8,128)(2,1)}, u32[]{:S(2)}) copy-start(bf16[4,24,512]{2,1,0:T(8,128)(2,1)} %get-tuple-element.14.c0.o0) | copy-start | bytes 294916
  18.1 32.1 %copy-start.5 = (bf16[8,24,512]{2,1,0:T(8,128)(2,1)S(1)}, bf16[8,24,512]{2,1,0:T(8,128)(2,1)}, u32[]{:S(2)}) copy-start(bf16[8,24,512]{2,1,0:T(8,128)(2,1)} %get-tuple-element.18.r0) | copy-start | bytes 589828
  18.1 27.3 %all-to-all-start = ((f32[64,24,128]{2,1,0:T(8,128)}), f32[64,24,128]{2,1,0:T(8,128)S(1)}, u32[]{:S(2)}, u32[]{:S(2)}) async-start(f32[64,24,128]{2,1,0:T(8,128)} %broadcast_in_dim.2), calls=%async_computation | async-start | bytes 1572864 | tf_op jit(solution)/shard_map/all_to_all | solution.py:265
  29.1 21.2 %collective-permute-start.5 = (bf16[8,24,512]{2,1,0:T(8,128)(2,1)S(1)}, bf16[8,24,512]{2,1,0:T(8,128)(2,1)S(1)}, u32[]{:S(2)}, u32[]{:S(2)}) collective-permute-start(bf16[8,24,512]{2,1,0:T(8,128)(2,1)S(1)} %copy-done.16), channel_id=1, source_target_pairs={{0,32},{32,64},{64,96},{96,0},{1,33},{33,65},{65,97},{97,1},{2,34}... | collective-permute-start | bytes 589832 | tf_op jit(solution)/shard_map/ppermute | solution.py:253
  30.7 19.5 %collective-permute-start.6 = (bf16[8,24,512]{2,1,0:T(8,128)(2,1)S(1)}, bf16[8,24,512]{2,1,0:T(8,128)(2,1)S(1)}, u32[]{:S(2)}, u32[]{:S(2)}) collective-permute-start(bf16[8,24,512]{2,1,0:T(8,128)(2,1)S(1)} %copy-done.15), channel_id=1, source_target_pairs={{0,64},{32,96},{64,0},{96,32},{1,65},{33,97},{65,1},{97,33},{2,66}... | collective-permute-start | bytes 589832 | tf_op jit(solution)/shard_map/ppermute | solution.py:253
  33.6 16.6 %collective-permute-start.7 = (bf16[8,24,512]{2,1,0:T(8,128)(2,1)S(1)}, bf16[8,24,512]{2,1,0:T(8,128)(2,1)S(1)}, u32[]{:S(2)}, u32[]{:S(2)}) collective-permute-start(bf16[8,24,512]{2,1,0:T(8,128)(2,1)S(1)} %copy-done.14), channel_id=1, source_target_pairs={{0,96},{32,0},{64,32},{96,64},{1,97},{33,1},{65,33},{97,65},{2,98}... | collective-permute-start | bytes 589832 | tf_op jit(solution)/shard_map/ppermute | solution.py:253
  45.5 1.3 %copy-start.9 = (f32[24,128]{1,0:T(8,128)}, f32[24,128]{1,0:T(8,128)S(1)}, u32[]{:S(2)}) copy-start(f32[24,128]{1,0:T(8,128)S(1)} %reduce_sum.9.mine_ref) | copy-start | bytes 36868
  45.5 1.3 %collective-permute-start.4 = (f32[24,128]{1,0:T(8,128)S(1)}, f32[24,128]{1,0:T(8,128)S(1)}, u32[]{:S(2)}, u32[]{:S(2)}) collective-permute-start(f32[24,128]{1,0:T(8,128)S(1)} %reduce_sum.9.mine_ref), channel_id=1, source_target_pairs={{0,1},{1,0},{2,3},{3,2},{4,5},{5,4},{6,7},{7,6},{8,9},{9,8},{10,11... | collective-permute-start | bytes 36872 | tf_op jit(solution)/shard_map/ppermute | solution.py:257
  52.4 16.6 %collective-permute-start.8 = (bf16[12,24,512]{2,1,0:T(8,128)(2,1)S(1)}, bf16[12,24,512]{2,1,0:T(8,128)(2,1)S(1)}, u32[]{:S(2)}, u32[]{:S(2)}) collective-permute-start(bf16[12,24,512]{2,1,0:T(8,128)(2,1)S(1)} %get-tuple-element.23), channel_id=1, source_target_pairs={{0,32},{32,64},{64,96},{96,0},{1,33},{33,65},{65,97},{97,1},{2,34}... | collective-permute-start | bytes 884744 | tf_op jit(solution)/shard_map/ppermute | solution.py:253
  52.6 16.4 %collective-permute-start.9 = (bf16[12,24,512]{2,1,0:T(8,128)(2,1)S(1)}, bf16[12,24,512]{2,1,0:T(8,128)(2,1)S(1)}, u32[]{:S(2)}, u32[]{:S(2)}) collective-permute-start(bf16[12,24,512]{2,1,0:T(8,128)(2,1)S(1)} %get-tuple-element.24), channel_id=1, source_target_pairs={{0,64},{32,96},{64,0},{96,32},{1,65},{33,97},{65,1},{97,33},{2,66}... | collective-permute-start | bytes 884744 | tf_op jit(solution)/shard_map/ppermute | solution.py:253
  54.7 15.0 %collective-permute-start.10 = (bf16[12,24,512]{2,1,0:T(8,128)(2,1)S(1)}, bf16[12,24,512]{2,1,0:T(8,128)(2,1)S(1)}, u32[]{:S(2)}, u32[]{:S(2)}) collective-permute-start(bf16[12,24,512]{2,1,0:T(8,128)(2,1)S(1)} %get-tuple-element.25), channel_id=1, source_target_pairs={{0,96},{32,0},{64,32},{96,64},{1,97},{33,1},{65,33},{97,65},{2,98}... | collective-permute-start | bytes 884744 | tf_op jit(solution)/shard_map/ppermute | solution.py:253
  69.0 0.8 %copy-start.7 = (bf16[12,24,512]{2,1,0:T(8,128)(2,1)}, bf16[12,24,512]{2,1,0:T(8,128)(2,1)S(1)}, u32[]{:S(2)}) copy-start(bf16[12,24,512]{2,1,0:T(8,128)(2,1)S(1)} %collective-permute-done.9.c2) | copy-start | bytes 884740
  (5 other events, 3.5 us)

commit v3 on v2

--- a/solution.py
+++ b/solution.py
@@ -1,3 +1,5 @@
+import functools
+
 import jax
 import jax.numpy as jnp
 from jax import lax
@@ -16,13 +18,13 @@
 NNZ = 2
 NS_ITERS = 4
 HALF = K // 2
-CHIPS = 64
+PLANE = 16
 
 EXACT = lax.Precision.HIGHEST
 VMEM = pl.BlockSpec(memory_space=pltpu.VMEM)
 SMEM = pl.BlockSpec(memory_space=pltpu.SMEM)
 ANY = pl.BlockSpec(memory_space=pl.ANY)
-ROOM = pltpu.CompilerParams(vmem_limit_bytes=48 * 1024 * 1024)
+ROOM = pltpu.CompilerParams(vmem_limit_bytes=8 * 1024 * 1024)
 
 
 def group_from(me, shift):
@@ -59,6 +61,7 @@
         in_specs=[SMEM, ANY],
         out_specs=[VMEM] * len(shapes),
         scratch_shapes=[pltpu.SemaphoreType.DMA((2 * GROUPS,))],
+        compiler_params=ROOM,
         name="pack",
     )(me, prior)
     return outs[:GROUPS], outs[GROUPS:]
@@ -181,6 +184,7 @@
         out_shape=jax.ShapeDtypeStruct((K, K), jnp.float32),
         in_specs=[SMEM, VMEM, VMEM],
         out_specs=VMEM,
+        compiler_params=ROOM,
         name="transform",
     )(core, mine, other)
 
@@ -222,27 +226,30 @@
     )(me, weights, *observed, *rest)
 
 
-def place_kernel(me_ref, c0, c1, c2, c3, out_ref, sems):
-    me = me_ref[0]
-    copies = []
-    for s, chunk in enumerate((c0, c1, c2, c3)):
-        cells = pl.ds(pl.multiple_of(group_from(me, s) * TILE, TILE), TILE)
-        copies.append(pltpu.make_async_copy(chunk, out_ref.at[:, :, cells], sems.at[s]))
-    for copy in copies:
-        copy.start()
-    for copy in copies:
-        copy.wait()
+def place_kernel(shift, me_ref, chunk, *refs):
+    out_ref, sem = refs[-2:]
+    cells = pl.ds(pl.multiple_of(group_from(me_ref[0], shift) * TILE, TILE), TILE)
+    copy = pltpu.make_async_copy(chunk, out_ref.at[:, :, cells], sem)
+    copy.start()
+    copy.wait()
 
 
 def place(me, chunks):
-    return pl.pallas_call(
-        place_kernel,
-        out_shape=jax.ShapeDtypeStruct((V, MEMBERS, GROUPS * TILE), jnp.bfloat16),
-        in_specs=[SMEM] + [VMEM] * GROUPS,
-        out_specs=ANY,
-        scratch_shapes=[pltpu.SemaphoreType.DMA((GROUPS,))],
-        name="place",
-    )(me, *chunks)
+    out = []
+    for shift, chunk in enumerate(chunks):
+        out = [
+            pl.pallas_call(
+                functools.partial(place_kernel, shift),
+                out_shape=jax.ShapeDtypeStruct((V, MEMBERS, GROUPS * TILE), jnp.bfloat16),
+                in_specs=[SMEM, VMEM] + [ANY] * len(out),
+                out_specs=ANY,
+                scratch_shapes=[pltpu.SemaphoreType.DMA],
+                input_output_aliases={2: 0} if out else {},
+                compiler_params=ROOM,
+                name="place",
+            )(me, chunk, *out)
+        ]
+    return out[0]
 
 
 def ring(shift):
@@ -261,8 +268,10 @@
     first = core[0] == 0
     top, low = folded[: HALF // 2], folded[HALF // 2 :]
     chip = jnp.where(first, top, low) + swap(jnp.where(first, low, top))
-    copies = jnp.broadcast_to(chip[None], (CHIPS, HALF // 2, 128))
-    mine = jnp.sum(lax.all_to_all(copies, ("member", "x", "z"), 0, 0, tiled=True), axis=0)
+    parts = [lax.ppermute(chip, "member", ring(s)) for s in (2, 1, 3)]
+    chip = (chip + parts[0]) + (parts[1] + parts[2])
+    copies = jnp.broadcast_to(chip[None], (PLANE, HALF // 2, 128))
+    mine = jnp.sum(lax.all_to_all(copies, ("x", "z"), 0, 0, tiled=True), axis=0)
     return mine, swap(mine)
 
 

time: 73 us -> 64.5 us (0.88)
  waiting for transfers between devices: 30 us -> 24.2 us
  Pallas kernels: 10.6 us -> 8.27 us
  local copies, waits for them, and re-layouts: 4.86 us -> 2.96 us
  starting transfers between devices: 26.2 us -> 27.8 us
    all_to_all x1, waiting for transfers between devices: 10.4 us -> 3.31 us  [total(): mine = jnp.sum(lax.all_to_all(copies, ('x', 'z'), 0, 0, tiled=True), axis=0)]
    ppermute x0 -> x3, starting transfers between devices: none -> 4.61 us  [total(): parts = [lax.ppermute(chip, 'member', ring(s)) for s in (2, 1, 3)]]
    ppermute x0 -> x3, waiting for transfers between devices: none -> 3.15 us  [total(): parts = [lax.ppermute(chip, 'member', ring(s)) for s in (2, 1, 3)]]
    all_to_all x1, starting transfers between devices: 10.9 us -> 7.88 us  [total(): mine = jnp.sum(lax.all_to_all(copies, ('x', 'z'), 0, 0, tiled=True), axis=0)]
    pallas_call x1, Pallas kernels: 2.49 us -> 0.25 us  [pack(): pl.pallas_call(pack_kernel, out_shape=shapes, in_specs=[SMEM, ANY], out_s...]
    ppermute x9, waiting for transfers between devices: 17.2 us -> 15.4 us  [scatter(): lax.ppermute(chunks[s], 'member', ring(s))]
    unnamed x36 -> x14, local copies, waits for them, and re-layouts: 3.85 us -> 2.18 us
    pallas_call x1 -> x4, Pallas kernels: 2.27 us -> 2.89 us  [place(): pl.pallas_call(functools.partial(place_kernel, shift), out_shape=jax.Shap...]
  transfers between devices with their start and end apart: 12 -> 15, of which waited for: 6 -> 9; matrix products, arithmetic and copies ran while one was open for 0% -> 0% of each run, Pallas kernels for 4% -> 7%
where the time goes in v3:
time: 64.5 us; the launch traced here: 64 us
  starting transfers between devices  27.8 us (43%)
  waiting for transfers between devices  24.2 us (38%)
  Pallas kernels  8.27 us (13%)
  local copies, waits for them, and re-layouts  2.96 us (5%)
  between operations  0.79 us (1%)
    ppermute x9, waiting for transfers between devices, scatter(): lax.ppermute(chunks[s], 'member', ring(s))  15.4 us
    ppermute x9, starting transfers between devices, scatter(): lax.ppermute(chunks[s], 'member', ring(s))  15.1 us
    all_to_all x1, starting transfers between devices, total(): mine = jnp.sum(lax.all_to_all(copies, ('x', 'z'), 0, 0, tiled=True), axis=0)  7.88 us
    ppermute x3, starting transfers between devices, total(): parts = [lax.ppermute(chip, 'member', ring(s)) for s in (2, 1, 3)]  4.61 us
    all_to_all x1, waiting for transfers between devices, total(): mine = jnp.sum(lax.all_to_all(copies, ('x', 'z'), 0, 0, tiled=True), axis=0)  3.31 us
    ppermute x3, waiting for transfers between devices, total(): parts = [lax.ppermute(chip, 'member', ring(s)) for s in (2, 1, 3)]  3.15 us
    pallas_call x4, Pallas kernels, place(): pl.pallas_call(functools.partial(place_kernel, shift), out_shape=jax.Shap...  2.89 us
    pallas_call x1, Pallas kernels, observe(): pl.pallas_call(observe_kernel, out_shape=jax.ShapeDtypeStruct((HALF, 128)...  2.35 us
  transfers between devices with their start and end apart: 15, of which 9 were waited for; matrix products, arithmetic and copies ran while one was open for 0% of the time, Pallas kernels for 7%

profile of v3, /device:TPU:0, one launch (start us, length us, event | category | flops | bytes accessed | tf_op | source)
XLA Modules:
  0.0 64.0 jit_solution(7587739173524838363)
XLA Ops:
  0.7 1.3 %copy-done = bf16[24,12,2048]{2,0,1:T(8,128)(2,1)S(1)} copy-done((bf16[24,12,2048]{2,0,1:T(8,128)(2,1)S(1)}, bf16[24,12,2048]{2,0,1:T(8,128)(2,1)}, u32[]{:S(2)}) %copy-start) | copy-done | bytes 1179672
  2.2 1.7 %collective-permute-start = (bf16[4,24,512]{2,1,0:T(8,128)(2,1)S(1)}, bf16[4,24,512]{2,1,0:T(8,128)(2,1)S(1)}, u32[]{:S(2)}, u32[]{:S(2)}) collective-permute-start(bf16[4,24,512]{2,1,0:T(8,128)(2,1)S(1)} %get-tuple-element.15), channel_id=1, source_target_pairs={{0,32},{32,64},{64,96},{96,0},{1,33},{33,65},{65,97},{97,1},{2,34}... | collective-permute-start | bytes 294920 | tf_op jit(solution)/shard_map/ppermute | solution.py:260
  3.9 2.9 %collective-permute-start.1 = (bf16[4,24,512]{2,1,0:T(8,128)(2,1)S(1)}, bf16[4,24,512]{2,1,0:T(8,128)(2,1)S(1)}, u32[]{:S(2)}, u32[]{:S(2)}) collective-permute-start(bf16[4,24,512]{2,1,0:T(8,128)(2,1)S(1)} %get-tuple-element.16), channel_id=1, source_target_pairs={{0,64},{32,96},{64,0},{96,32},{1,65},{33,97},{65,1},{97,33},{2,66}... | collective-permute-start | bytes 294920 | tf_op jit(solution)/shard_map/ppermute | solution.py:260
  6.8 1.3 %collective-permute-start.2 = (bf16[4,24,512]{2,1,0:T(8,128)(2,1)S(1)}, bf16[4,24,512]{2,1,0:T(8,128)(2,1)S(1)}, u32[]{:S(2)}, u32[]{:S(2)}) collective-permute-start(bf16[4,24,512]{2,1,0:T(8,128)(2,1)S(1)} %get-tuple-element.17), channel_id=1, source_target_pairs={{0,96},{32,0},{64,32},{96,64},{1,97},{33,1},{65,33},{97,65},{2,98}... | collective-permute-start | bytes 294920 | tf_op jit(solution)/shard_map/ppermute | solution.py:260
  8.4 3.1 %collective-permute-done.1.c2.o2 = bf16[4,24,512]{2,1,0:T(8,128)(2,1)S(1)} collective-permute-done((bf16[4,24,512]{2,1,0:T(8,128)(2,1)S(1)}, bf16[4,24,512]{2,1,0:T(8,128)(2,1)S(1)}, u32[]{:S(2)}, u32[]{:S(2)}) %collective-permute-start.1) | collective-permute-done | bytes 98336 | tf_op jit(solution)/shard_map/ppermute | solution.py:260
  11.4 2.4 %observe.1 = f32[48,128]{1,0:T(8,128)S(1)} custom-call(s32[1]{0:T(128)} %bitcast.me_ref, s32[24]{0:T(128)S(1)} %reshape.16.slots_ref, bf16[4,24,512]{2,1,0:T(8,128)(2,1)S(1)} %get-tuple-element.14.c0.o0, bf16[4,24,512]{2,1,0:T(8,128)(2,1)S(1)} %collective-permute-done.c1.o1, bf16[4,24,512]{2,1,0:T(8,128)(2,1)S(1)} %collective-permute-done.1.c2.o2, ...), custom_call_target="tpu_custom_call" | custom-call | tf_op jit(solution)/shard_map/observe/pallas_call | solution.py:129
  13.9 1.2 %collective-permute-done.3 = f32[24,128]{1,0:T(8,128)S(1)} collective-permute-done((f32[24,128]{1,0:T(8,128)S(1)}, f32[24,128]{1,0:T(8,128)S(1)}, u32[]{:S(2)}, u32[]{:S(2)}) %collective-permute-start.3) | collective-permute-done | bytes 12320 | tf_op jit(solution)/shard_map/ppermute | solution.py:264
  15.1 2.6 %collective-permute-start.6 = (f32[24,128]{1,0:T(8,128)S(1)}, f32[24,128]{1,0:T(8,128)S(1)}, u32[]{:S(2)}, u32[]{:S(2)}) collective-permute-start(f32[24,128]{1,0:T(8,128)S(1)} %select_add_fusion), channel_id=1, source_target_pairs={{0,96},{32,0},{64,32},{96,64},{1,97},{33,1},{65,33},{97,65},{2,98}... | collective-permute-start | bytes 36872 | tf_op jit(solution)/shard_map/ppermute | solution.py:271
  17.7 2.0 %collective-permute-start.4 = (f32[24,128]{1,0:T(8,128)S(1)}, f32[24,128]{1,0:T(8,128)S(1)}, u32[]{:S(2)}, u32[]{:S(2)}) collective-permute-start(f32[24,128]{1,0:T(8,128)S(1)} %select_add_fusion), channel_id=1, source_target_pairs={{0,64},{32,96},{64,0},{96,32},{1,65},{33,97},{65,1},{97,33},{2,66}... | collective-permute-start | bytes 36872 | tf_op jit(solution)/shard_map/ppermute | solution.py:271
  19.7 2.9 %collective-permute-done.5 = f32[24,128]{1,0:T(8,128)S(1)} collective-permute-done((f32[24,128]{1,0:T(8,128)S(1)}, f32[24,128]{1,0:T(8,128)S(1)}, u32[]{:S(2)}, u32[]{:S(2)}) %collective-permute-start.5) | collective-permute-done | bytes 12320 | tf_op jit(solution)/shard_map/ppermute | solution.py:271
  23.6 7.9 %all-to-all-start = ((f32[16,24,128]{2,1,0:T(8,128)}), f32[16,24,128]{2,1,0:T(8,128)S(1)}, u32[]{:S(2)}, u32[]{:S(2)}) async-start(f32[16,24,128]{2,1,0:T(8,128)} %broadcast_in_dim.2), calls=%async_computation | async-start | bytes 393216 | tf_op jit(solution)/shard_map/all_to_all | solution.py:274
  31.4 0.8 %collective-permute-start.8 = (bf16[8,24,512]{2,1,0:T(8,128)(2,1)S(1)}, bf16[8,24,512]{2,1,0:T(8,128)(2,1)S(1)}, u32[]{:S(2)}, u32[]{:S(2)}) collective-permute-start(bf16[8,24,512]{2,1,0:T(8,128)(2,1)S(1)} %get-tuple-element.19), channel_id=1, source_target_pairs={{0,32},{32,64},{64,96},{96,0},{1,33},{33,65},{65,97},{97,1},{2,34}... | collective-permute-start | bytes 589832 | tf_op jit(solution)/shard_map/ppermute | solution.py:260
  32.2 4.0 %collective-permute-start.9 = (bf16[8,24,512]{2,1,0:T(8,128)(2,1)S(1)}, bf16[8,24,512]{2,1,0:T(8,128)(2,1)S(1)}, u32[]{:S(2)}, u32[]{:S(2)}) collective-permute-start(bf16[8,24,512]{2,1,0:T(8,128)(2,1)S(1)} %get-tuple-element.20), channel_id=1, source_target_pairs={{0,64},{32,96},{64,0},{96,32},{1,65},{33,97},{65,1},{97,33},{2,66}... | collective-permute-start | bytes 589832 | tf_op jit(solution)/shard_map/ppermute | solution.py:260
  36.2 3.3 %all-to-all-done = f32[16,24,128]{2,1,0:T(8,128)S(1)} async-done(((f32[16,24,128]{2,1,0:T(8,128)}), f32[16,24,128]{2,1,0:T(8,128)S(1)}, u32[]{:S(2)}, u32[]{:S(2)}) %all-to-all-start) | async-done | bytes 196640 | tf_op jit(solution)/shard_map/all_to_all | solution.py:274
  39.6 1.2 %collective-permute-done.7.other_ref = f32[24,128]{1,0:T(8,128)S(1)} collective-permute-done((f32[24,128]{1,0:T(8,128)S(1)}, f32[24,128]{1,0:T(8,128)S(1)}, u32[]{:S(2)}, u32[]{:S(2)}) %collective-permute-start.7) | collective-permute-done | bytes 12320 | tf_op jit(solution)/shard_map/ppermute | solution.py:264
  40.8 2.2 %transform.1.w_ref = f32[96,96]{1,0:T(8,128)} custom-call(s32[1]{0:T(128)} %bitcast.1.core_ref, f32[24,128]{1,0:T(8,128)S(1)} %reduce_sum.9.mine_ref, f32[24,128]{1,0:T(8,128)S(1)} %collective-permute-done.7.other_ref), custom_call_target="tpu_custom_call" | custom-call | tf_op jit(solution)/shard_map/transform/pallas_call | solution.py:182
  43.4 0.8 %copy-done.2 = f32[96,96]{1,0:T(8,128)S(1)} copy-done((f32[96,96]{1,0:T(8,128)S(1)}, f32[96,96]{1,0:T(8,128)}, u32[]{:S(2)}) %copy-start.2) | copy-done | bytes 36888
  45.4 3.7 %collective-permute-start.12 = (bf16[12,24,512]{2,1,0:T(8,128)(2,1)S(1)}, bf16[12,24,512]{2,1,0:T(8,128)(2,1)S(1)}, u32[]{:S(2)}, u32[]{:S(2)}) collective-permute-start(bf16[12,24,512]{2,1,0:T(8,128)(2,1)S(1)} %get-tuple-element.23), channel_id=1, source_target_pairs={{0,64},{32,96},{64,0},{96,32},{1,65},{33,97},{65,1},{97,33},{2,66}... | collective-permute-start | bytes 884744 | tf_op jit(solution)/shard_map/ppermute | solution.py:260
  49.2 0.7 %place.4.refs_0_ = bf16[12,24,2048]{2,1,0:T(8,128)(2,1)} custom-call(s32[1]{0:T(128)} %bitcast.me_ref, bf16[12,24,512]{2,1,0:T(8,128)(2,1)S(1)} %get-tuple-element.25.chunk), custom_call_target="tpu_custom_call" | custom-call | tf_op jit(solution)/shard_map/place/pallas_call | solution.py:241
  49.9 5.1 %collective-permute-done.13.chunk = bf16[12,24,512]{2,1,0:T(8,128)(2,1)S(1)} collective-permute-done((bf16[12,24,512]{2,1,0:T(8,128)(2,1)S(1)}, bf16[12,24,512]{2,1,0:T(8,128)(2,1)S(1)}, u32[]{:S(2)}, u32[]{:S(2)}) %collective-permute-start.13) | collective-permute-done | bytes 294944 | tf_op jit(solution)/shard_map/ppermute | solution.py:260
  55.0 0.7 %place.5.refs_0_ = bf16[12,24,2048]{2,1,0:T(8,128)(2,1)} custom-call(s32[1]{0:T(128)} %bitcast.me_ref, bf16[12,24,512]{2,1,0:T(8,128)(2,1)S(1)} %collective-permute-done.13.chunk, bf16[12,24,2048]{2,1,0:T(8,128)(2,1)} %place.4.refs_0_), custom_call_target="tpu_custom_call", output_to_operand_aliasing={{}: (2, {})} | custom-call | tf_op jit(solution)/shard_map/place/pallas_call | solution.py:241
  55.8 6.8 %collective-permute-done.12.chunk = bf16[12,24,512]{2,1,0:T(8,128)(2,1)S(1)} collective-permute-done((bf16[12,24,512]{2,1,0:T(8,128)(2,1)S(1)}, bf16[12,24,512]{2,1,0:T(8,128)(2,1)S(1)}, u32[]{:S(2)}, u32[]{:S(2)}) %collective-permute-start.12) | collective-permute-done | bytes 294944 | tf_op jit(solution)/shard_map/ppermute | solution.py:260
  62.5 0.7 %place.6.refs_0_ = bf16[12,24,2048]{2,1,0:T(8,128)(2,1)} custom-call(s32[1]{0:T(128)} %bitcast.me_ref, bf16[12,24,512]{2,1,0:T(8,128)(2,1)S(1)} %collective-permute-done.12.chunk, bf16[12,24,2048]{2,1,0:T(8,128)(2,1)} %place.5.refs_0_), custom_call_target="tpu_custom_call", output_to_operand_aliasing={{}: (2, {})} | custom-call | tf_op jit(solution)/shard_map/place/pallas_call | solution.py:241
  63.3 0.7 %place.7 = bf16[12,24,2048]{2,1,0:T(8,128)(2,1)} custom-call(s32[1]{0:T(128)} %bitcast.me_ref, bf16[12,24,512]{2,1,0:T(8,128)(2,1)S(1)} %collective-permute-done.11.chunk, bf16[12,24,2048]{2,1,0:T(8,128)(2,1)} %place.6.refs_0_), custom_call_target="tpu_custom_call", output_to_operand_aliasing={{}: (2, {})} | custom-call | tf_op jit(solution)/shard_map/place/pallas_call | solution.py:241
  (34 shorter events, 3.3 us)
Async XLA Ops:
  0.6 7.5 %copy-start.3 = (f32[12,1,128]{2,1,0:T(1,128)S(1)}, f32[12,1,128]{2,1,0:T(1,128)}, u32[]{:S(2)}) copy-start(f32[12,1,128]{2,1,0:T(1,128)} %param.7) | copy-start | bytes 18436
  0.6 7.5 %copy-start.5 = (s32[12,1,2]{0,2,1:T(2,128)S(1)}, s32[12,1,2]{0,2,1:T(2,128)}, u32[]{:S(2)}) copy-start(s32[12,1,2]{0,2,1:T(2,128)} %param.9) | copy-start | bytes 292
  0.7 1.3 %copy-start = (bf16[24,12,2048]{2,0,1:T(8,128)(2,1)S(1)}, bf16[24,12,2048]{2,0,1:T(8,128)(2,1)}, u32[]{:S(2)}) copy-start(bf16[24,12,2048]{2,0,1:T(8,128)(2,1)} %param.5) | copy-start | bytes 3538948
  1.9 6.2 %copy-start.4 = (f32[12,1,128]{2,1,0:T(1,128)S(1)}, f32[12,1,128]{2,1,0:T(1,128)}, u32[]{:S(2)}) copy-start(f32[12,1,128]{2,1,0:T(1,128)} %param.6) | copy-start | bytes 18436
  1.9 9.5 %copy-start.1 = (bf16[12,1,2,128,128]{4,3,2,1,0:T(8,128)(2,1)S(1)}, bf16[12,1,2,128,128]{4,3,2,1,0:T(8,128)(2,1)}, u32[]{:S(2)}) copy-start(bf16[12,1,2,128,128]{4,3,2,1,0:T(8,128)(2,1)} %param.8) | copy-start | bytes 2359300
  2.2 6.2 %collective-permute-start = (bf16[4,24,512]{2,1,0:T(8,128)(2,1)S(1)}, bf16[4,24,512]{2,1,0:T(8,128)(2,1)S(1)}, u32[]{:S(2)}, u32[]{:S(2)}) collective-permute-start(bf16[4,24,512]{2,1,0:T(8,128)(2,1)S(1)} %get-tuple-element.15), channel_id=1, source_target_pairs={{0,32},{32,64},{64,96},{96,0},{1,33},{33,65},{65,97},{97,1},{2,34}... | collective-permute-start | bytes 294920 | tf_op jit(solution)/shard_map/ppermute | solution.py:260
  3.9 7.5 %collective-permute-start.1 = (bf16[4,24,512]{2,1,0:T(8,128)(2,1)S(1)}, bf16[4,24,512]{2,1,0:T(8,128)(2,1)S(1)}, u32[]{:S(2)}, u32[]{:S(2)}) collective-permute-start(bf16[4,24,512]{2,1,0:T(8,128)(2,1)S(1)} %get-tuple-element.16), channel_id=1, source_target_pairs={{0,64},{32,96},{64,0},{96,32},{1,65},{33,97},{65,1},{97,33},{2,66}... | collective-permute-start | bytes 294920 | tf_op jit(solution)/shard_map/ppermute | solution.py:260
  6.8 4.6 %collective-permute-start.2 = (bf16[4,24,512]{2,1,0:T(8,128)(2,1)S(1)}, bf16[4,24,512]{2,1,0:T(8,128)(2,1)S(1)}, u32[]{:S(2)}, u32[]{:S(2)}) collective-permute-start(bf16[4,24,512]{2,1,0:T(8,128)(2,1)S(1)} %get-tuple-element.17), channel_id=1, source_target_pairs={{0,96},{32,0},{64,32},{96,64},{1,97},{33,1},{65,33},{97,65},{2,98}... | collective-permute-start | bytes 294920 | tf_op jit(solution)/shard_map/ppermute | solution.py:260
  13.8 1.3 %collective-permute-start.3 = (f32[24,128]{1,0:T(8,128)S(1)}, f32[24,128]{1,0:T(8,128)S(1)}, u32[]{:S(2)}, u32[]{:S(2)}) collective-permute-start(f32[24,128]{1,0:T(8,128)S(1)} %slice_select_fusion), channel_id=1, source_target_pairs={{0,1},{1,0},{2,3},{3,2},{4,5},{5,4},{6,7},{7,6},{8,9},{9,8},{10,11... | collective-permute-start | bytes 36872 | tf_op jit(solution)/shard_map/ppermute | solution.py:264
  15.1 4.6 %collective-permute-start.6 = (f32[24,128]{1,0:T(8,128)S(1)}, f32[24,128]{1,0:T(8,128)S(1)}, u32[]{:S(2)}, u32[]{:S(2)}) collective-permute-start(f32[24,128]{1,0:T(8,128)S(1)} %select_add_fusion), channel_id=1, source_target_pairs={{0,96},{32,0},{64,32},{96,64},{1,97},{33,1},{65,33},{97,65},{2,98}... | collective-permute-start | bytes 36872 | tf_op jit(solution)/shard_map/ppermute | solution.py:271
  17.6 4.9 %collective-permute-start.5 = (f32[24,128]{1,0:T(8,128)S(1)}, f32[24,128]{1,0:T(8,128)S(1)}, u32[]{:S(2)}, u32[]{:S(2)}) collective-permute-start(f32[24,128]{1,0:T(8,128)S(1)} %select_add_fusion), channel_id=1, source_target_pairs={{0,32},{32,64},{64,96},{96,0},{1,33},{33,65},{65,97},{97,1},{2,34}... | collective-permute-start | bytes 36872 | tf_op jit(solution)/shard_map/ppermute | solution.py:271
  17.7 5.2 %collective-permute-start.4 = (f32[24,128]{1,0:T(8,128)S(1)}, f32[24,128]{1,0:T(8,128)S(1)}, u32[]{:S(2)}, u32[]{:S(2)}) collective-permute-start(f32[24,128]{1,0:T(8,128)S(1)} %select_add_fusion), channel_id=1, source_target_pairs={{0,64},{32,96},{64,0},{96,32},{1,65},{33,97},{65,1},{97,33},{2,66}... | collective-permute-start | bytes 36872 | tf_op jit(solution)/shard_map/ppermute | solution.py:271
  23.6 16.0 %all-to-all-start = ((f32[16,24,128]{2,1,0:T(8,128)}), f32[16,24,128]{2,1,0:T(8,128)S(1)}, u32[]{:S(2)}, u32[]{:S(2)}) async-start(f32[16,24,128]{2,1,0:T(8,128)} %broadcast_in_dim.2), calls=%async_computation | async-start | bytes 393216 | tf_op jit(solution)/shard_map/all_to_all | solution.py:274
  31.4 11.5 %collective-permute-start.8 = (bf16[8,24,512]{2,1,0:T(8,128)(2,1)S(1)}, bf16[8,24,512]{2,1,0:T(8,128)(2,1)S(1)}, u32[]{:S(2)}, u32[]{:S(2)}) collective-permute-start(bf16[8,24,512]{2,1,0:T(8,128)(2,1)S(1)} %get-tuple-element.19), channel_id=1, source_target_pairs={{0,32},{32,64},{64,96},{96,0},{1,33},{33,65},{65,97},{97,1},{2,34}... | collective-permute-start | bytes 589832 | tf_op jit(solution)/shard_map/ppermute | solution.py:260
  32.2 11.2 %collective-permute-start.9 = (bf16[8,24,512]{2,1,0:T(8,128)(2,1)S(1)}, bf16[8,24,512]{2,1,0:T(8,128)(2,1)S(1)}, u32[]{:S(2)}, u32[]{:S(2)}) collective-permute-start(bf16[8,24,512]{2,1,0:T(8,128)(2,1)S(1)} %get-tuple-element.20), channel_id=1, source_target_pairs={{0,64},{32,96},{64,0},{96,32},{1,65},{33,97},{65,1},{97,33},{2,66}... | collective-permute-start | bytes 589832 | tf_op jit(solution)/shard_map/ppermute | solution.py:260
  36.2 7.2 %collective-permute-start.10 = (bf16[8,24,512]{2,1,0:T(8,128)(2,1)S(1)}, bf16[8,24,512]{2,1,0:T(8,128)(2,1)S(1)}, u32[]{:S(2)}, u32[]{:S(2)}) collective-permute-start(bf16[8,24,512]{2,1,0:T(8,128)(2,1)S(1)} %get-tuple-element.21), channel_id=1, source_target_pairs={{0,96},{32,0},{64,32},{96,64},{1,97},{33,1},{65,33},{97,65},{2,98}... | collective-permute-start | bytes 589832 | tf_op jit(solution)/shard_map/ppermute | solution.py:260
  39.5 1.3 %collective-permute-start.7 = (f32[24,128]{1,0:T(8,128)S(1)}, f32[24,128]{1,0:T(8,128)S(1)}, u32[]{:S(2)}, u32[]{:S(2)}) collective-permute-start(f32[24,128]{1,0:T(8,128)S(1)} %reduce_sum.9.mine_ref), channel_id=1, source_target_pairs={{0,1},{1,0},{2,3},{3,2},{4,5},{5,4},{6,7},{7,6},{8,9},{9,8},{10,11... | collective-permute-start | bytes 36872 | tf_op jit(solution)/shard_map/ppermute | solution.py:264
  43.4 0.8 %copy-start.2 = (f32[96,96]{1,0:T(8,128)S(1)}, f32[96,96]{1,0:T(8,128)}, u32[]{:S(2)}) copy-start(f32[96,96]{1,0:T(8,128)} %transform.1.w_ref) | copy-start | bytes 110596
  44.8 10.2 %collective-permute-start.13 = (bf16[12,24,512]{2,1,0:T(8,128)(2,1)S(1)}, bf16[12,24,512]{2,1,0:T(8,128)(2,1)S(1)}, u32[]{:S(2)}, u32[]{:S(2)}) collective-permute-start(bf16[12,24,512]{2,1,0:T(8,128)(2,1)S(1)} %get-tuple-element.24), channel_id=1, source_target_pairs={{0,32},{32,64},{64,96},{96,0},{1,33},{33,65},{65,97},{97,1},{2,34}... | collective-permute-start | bytes 884744 | tf_op jit(solution)/shard_map/ppermute | solution.py:260
  45.4 17.1 %collective-permute-start.12 = (bf16[12,24,512]{2,1,0:T(8,128)(2,1)S(1)}, bf16[12,24,512]{2,1,0:T(8,128)(2,1)S(1)}, u32[]{:S(2)}, u32[]{:S(2)}) collective-permute-start(bf16[12,24,512]{2,1,0:T(8,128)(2,1)S(1)} %get-tuple-element.23), channel_id=1, source_target_pairs={{0,64},{32,96},{64,0},{96,32},{1,65},{33,97},{65,1},{97,33},{2,66}... | collective-permute-start | bytes 884744 | tf_op jit(solution)/shard_map/ppermute | solution.py:260
  49.2 14.1 %collective-permute-start.11 = (bf16[12,24,512]{2,1,0:T(8,128)(2,1)S(1)}, bf16[12,24,512]{2,1,0:T(8,128)(2,1)S(1)}, u32[]{:S(2)}, u32[]{:S(2)}) collective-permute-start(bf16[12,24,512]{2,1,0:T(8,128)(2,1)S(1)} %get-tuple-element.22), channel_id=1, source_target_pairs={{0,96},{32,0},{64,32},{96,64},{1,97},{33,1},{65,33},{97,65},{2,98}... | collective-permute-start | bytes 884744 | tf_op jit(solution)/shard_map/ppermute | solution.py:260

commit v4 on v2

--- a/solution.py
+++ b/solution.py
@@ -1,3 +1,5 @@
+import functools
+
 import jax
 import jax.numpy as jnp
 from jax import lax
@@ -16,13 +18,19 @@
 NNZ = 2
 NS_ITERS = 4
 HALF = K // 2
-CHIPS = 64
+PLANE = 16
+COLUMN = 8
+NEAR = 6
+COST = 40_000_000_000
+FAR = V - NEAR
+NEXT = NEAR - VOBS
 
 EXACT = lax.Precision.HIGHEST
 VMEM = pl.BlockSpec(memory_space=pltpu.VMEM)
 SMEM = pl.BlockSpec(memory_space=pltpu.SMEM)
+HBM = pl.BlockSpec(memory_space=pltpu.HBM)
 ANY = pl.BlockSpec(memory_space=pl.ANY)
-ROOM = pltpu.CompilerParams(vmem_limit_bytes=48 * 1024 * 1024)
+ROOM = pltpu.CompilerParams(vmem_limit_bytes=8 * 1024 * 1024)
 
 
 def group_from(me, shift):
@@ -35,15 +43,10 @@
 
 def pack_kernel(me_ref, prior_ref, *refs):
     outs, sems = refs[:-1], refs[-1]
-    me = me_ref[0]
     copies = []
     for s in range(GROUPS):
-        cells = pl.ds(pl.multiple_of(group_to(me, s) * TILE, TILE), TILE)
-        for part, rows in enumerate((pl.ds(0, VOBS), pl.ds(VOBS, V - VOBS))):
-            n = part * GROUPS + s
-            copies.append(
-                pltpu.make_async_copy(prior_ref.at[rows, :, cells], outs[n], sems.at[n])
-            )
+        cells = pl.ds(pl.multiple_of(group_to(me_ref[0], s) * TILE, TILE), TILE)
+        copies.append(pltpu.make_async_copy(prior_ref.at[pl.ds(0, VOBS), :, cells], outs[s], sems.at[s]))
     for copy in copies:
         copy.start()
     for copy in copies:
@@ -51,17 +54,45 @@
 
 
 def pack(me, prior):
-    shapes = [jax.ShapeDtypeStruct((VOBS, MEMBERS, TILE), prior.dtype)] * GROUPS
-    shapes += [jax.ShapeDtypeStruct((V - VOBS, MEMBERS, TILE), prior.dtype)] * GROUPS
-    outs = pl.pallas_call(
+    return pl.pallas_call(
         pack_kernel,
-        out_shape=shapes,
-        in_specs=[SMEM, ANY],
-        out_specs=[VMEM] * len(shapes),
-        scratch_shapes=[pltpu.SemaphoreType.DMA((2 * GROUPS,))],
+        out_shape=[jax.ShapeDtypeStruct((VOBS, MEMBERS, TILE), prior.dtype)] * GROUPS,
+        in_specs=[SMEM, HBM],
+        out_specs=[VMEM] * GROUPS,
+        scratch_shapes=[pltpu.SemaphoreType.DMA((GROUPS,))],
+        compiler_params=ROOM,
         name="pack",
     )(me, prior)
-    return outs[:GROUPS], outs[GROUPS:]
+
+
+def pack_bulk_kernel(me_ref, prior_ref, after_ref, *refs):
+    del after_ref
+    outs, sems = refs[:-1], refs[-1]
+    copies = []
+    for s in range(GROUPS):
+        cells = pl.ds(pl.multiple_of(group_to(me_ref[0], s) * TILE, TILE), TILE)
+        if NEXT:
+            copies.append((prior_ref.at[pl.ds(VOBS, NEXT), :, cells], outs[s].at[pl.ds(0, NEXT)]))
+        for c in range(GROUPS):
+            source = prior_ref.at[pl.ds(NEAR, FAR), :, pl.ds(c * TILE, TILE)]
+            copies.append((source, outs[s].at[pl.ds(NEXT + c * FAR, FAR)]))
+    copies = [pltpu.make_async_copy(*pair, sems.at[n]) for n, pair in enumerate(copies)]
+    for copy in copies:
+        copy.start()
+    for copy in copies:
+        copy.wait()
+
+
+def pack_bulk(me, prior, after):
+    return pl.pallas_call(
+        pack_bulk_kernel,
+        out_shape=[jax.ShapeDtypeStruct((NEXT + GROUPS * FAR, MEMBERS, TILE), prior.dtype)] * GROUPS,
+        in_specs=[SMEM, ANY, ANY],
+        out_specs=[VMEM] * GROUPS,
+        scratch_shapes=[pltpu.SemaphoreType.DMA((GROUPS * (GROUPS + 1),))],
+        compiler_params=ROOM,
+        name="pack_bulk",
+    )(me, prior, after)
 
 
 def indices():
@@ -151,10 +182,27 @@
     return small + jnp.dot(a_high, b_high, preferred_element_type=jnp.float32)
 
 
-def transform_kernel(core_ref, mine_ref, other_ref, weights_ref):
-    first = core_ref[0] == 0
-    mine, other = mine_ref[...], other_ref[...]
-    folded = jnp.concatenate([jnp.where(first, mine, other), jnp.where(first, other, mine)], axis=0)
+def spread_kernel(parts_ref, out_ref):
+    total = parts_ref[0]
+    for part in range(1, parts_ref.shape[0]):
+        total = total + parts_ref[part]
+    for copy in range(out_ref.shape[0]):
+        out_ref[copy] = total
+
+
+def spread_sum(parts, copies):
+    return pl.pallas_call(
+        spread_kernel,
+        out_shape=jax.ShapeDtypeStruct((copies, HALF, 128), jnp.float32),
+        in_specs=[VMEM],
+        out_specs=VMEM,
+        compiler_params=ROOM,
+        name="spread_sum",
+    )(parts)
+
+
+def transform_kernel(parts_ref, weights_ref, again_ref):
+    folded = parts_ref[...]
     gram, projected = unfold(folded)
     row = lax.broadcasted_iota(jnp.int32, (K, K), 0)
     col = lax.broadcasted_iota(jnp.int32, (K, K), 1)
@@ -172,77 +220,119 @@
     inverse_root = inverse / jnp.sqrt(frob)
     halfway = jnp.sum(inverse_root * projected, axis=0, keepdims=True)
     mean_shift = jnp.sum(inverse_root * halfway, axis=1, keepdims=True)
-    weights_ref[...] = mean_shift + (K - 1.0) ** 0.5 * inverse_root
-
-
-def transform(core, mine, other):
+    weights = mean_shift + (K - 1.0) ** 0.5 * inverse_root
+    weights_ref[...] = weights
+    again_ref[...] = weights
+
+
+def transform(parts):
     return pl.pallas_call(
         transform_kernel,
-        out_shape=jax.ShapeDtypeStruct((K, K), jnp.float32),
-        in_specs=[SMEM, VMEM, VMEM],
-        out_specs=VMEM,
+        out_shape=[jax.ShapeDtypeStruct((K, K), jnp.float32)] * 2,
+        in_specs=[VMEM],
+        out_specs=[VMEM] * 2,
+        compiler_params=ROOM,
+        cost_estimate=pl.CostEstimate(flops=COST, bytes_accessed=0, transcendentals=0),
         name="transform",
-    )(core, mine, other)
-
-
-def analyse_kernel(me_ref, w_ref, o0, o1, o2, o3, r0, r1, r2, r3, a0, a1, a2, a3, turned):
-    me = me_ref[0]
-
-    def regroup(x, which):
-        return jnp.concatenate(
-            [x[pl.ds(pl.multiple_of(which(me, s) * MEMBERS, 8), MEMBERS), :] for s in range(GROUPS)], axis=0
-        )
-
-    by_source = regroup(w_ref, group_from)
-    turned[...] = by_source.T
-    coeffs = regroup(turned, group_to).astype(jnp.bfloat16)
-    keep = 1.0 - jnp.sum(coeffs.astype(jnp.float32), axis=1, keepdims=True)
-    outs = (a0, a1, a2, a3)
-    for v in range(V):
-        src = (o0, o1, o2, o3) if v < VOBS else (r0, r1, r2, r3)
-        u = v if v < VOBS else v - VOBS
-        parts = [ref[u].astype(jnp.float32) for ref in src]
-        stacked = jnp.concatenate(parts, axis=0)
-        center = jnp.sum(stacked, axis=0, keepdims=True) * (1.0 / K)
-        mixed = jnp.dot(coeffs, stacked.astype(jnp.bfloat16), preferred_element_type=jnp.float32)
-        mixed = mixed + keep * center
-        for g in range(GROUPS):
-            outs[g][v] = mixed[g * MEMBERS : (g + 1) * MEMBERS].astype(jnp.bfloat16)
-
-
-def analyse(me, weights, observed, rest):
-    return pl.pallas_call(
-        analyse_kernel,
-        out_shape=[jax.ShapeDtypeStruct((V, MEMBERS, TILE), jnp.bfloat16)] * GROUPS,
+    )(parts)
+
+
+def regroup(x, me, which):
+    return jnp.concatenate(
+        [x[pl.ds(pl.multiple_of(which(me, s) * MEMBERS, 8), MEMBERS), :] for s in range(GROUPS)], axis=0
+    )
+
+
+def coefficients(me, w_ref, turned):
+    turned[...] = regroup(w_ref, me, group_from).T
+    coeffs = regroup(turned, me, group_to).astype(jnp.bfloat16)
+    return coeffs, 1.0 - jnp.sum(coeffs.astype(jnp.float32), axis=1, keepdims=True)
+
+
+def mix(coeffs, keep, parts):
+    stacked = jnp.concatenate([part.astype(jnp.float32) for part in parts], axis=0)
+    center = jnp.sum(stacked, axis=0, keepdims=True) * (1.0 / K)
+    mixed = jnp.dot(coeffs, stacked.astype(jnp.bfloat16), preferred_element_type=jnp.float32)
+    return mixed + keep * center
+
+
+def near_kernel(me_ref, w_ref, o0, o1, o2, o3, b0, b1, b2, b3, a0, a1, a2, a3, turned):
+    coeffs, keep = coefficients(me_ref[0], w_ref, turned)
+    for v in range(NEAR):
+        parts = [ref[v] for ref in (o0, o1, o2, o3)] if v < VOBS else [ref[v - VOBS] for ref in (b0, b1, b2, b3)]
+        mixed = mix(coeffs, keep, parts)
+        for g, out in enumerate((a0, a1, a2, a3)):
+            out[v] = mixed[g * MEMBERS : (g + 1) * MEMBERS].astype(jnp.bfloat16)
+
+
+def analyse_near(me, weights, observed, bulk):
+    return pl.pallas_call(
+        near_kernel,
+        out_shape=[jax.ShapeDtypeStruct((NEAR, MEMBERS, TILE), jnp.bfloat16)] * GROUPS,
         in_specs=[SMEM] + [VMEM] * 9,
         out_specs=[VMEM] * GROUPS,
         scratch_shapes=[pltpu.VMEM((K, K), jnp.float32)],
         compiler_params=ROOM,
-        name="analyse",
-    )(me, weights, *observed, *rest)
-
-
-def place_kernel(me_ref, c0, c1, c2, c3, out_ref, sems):
+        name="analyse_near",
+    )(me, weights, *observed, *bulk)
+
+
+def far_kernel(me_ref, w_ref, near_ref, b0, b1, b2, b3, out_ref, turned, result, sems):
     me = me_ref[0]
+    cells = pl.ds(pl.multiple_of(me * TILE, TILE), TILE)
+    copies = [pltpu.make_async_copy(near_ref, out_ref.at[pl.ds(0, NEAR), :, cells], sems.at[0])]
+    copies[0].start()
+    coeffs, keep = coefficients(me, w_ref, turned)
+    for v in range(FAR):
+        for c in range(GROUPS):
+            parts = [ref[NEXT + c * FAR + v] for ref in (b0, b1, b2, b3)]
+            mixed = mix(coeffs[:MEMBERS], keep[:MEMBERS], parts)
+            result[v, :, pl.ds(c * TILE, TILE)] = mixed.astype(jnp.bfloat16)
+        copies.append(pltpu.make_async_copy(result.at[v], out_ref.at[NEAR + v], sems.at[1 + v]))
+        copies[-1].start()
+    for copy in copies:
+        copy.wait()
+
+
+def analyse_far(me, weights, near, bulk):
+    return pl.pallas_call(
+        far_kernel,
+        out_shape=jax.ShapeDtypeStruct((V, MEMBERS, GROUPS * TILE), jnp.bfloat16),
+        in_specs=[SMEM] + [VMEM] * 6,
+        out_specs=ANY,
+        scratch_shapes=[
+            pltpu.VMEM((K, K), jnp.float32),
+            pltpu.VMEM((FAR, MEMBERS, GROUPS * TILE), jnp.bfloat16),
+            pltpu.SemaphoreType.DMA((1 + FAR,)),
+        ],
+        compiler_params=ROOM,
+        name="analyse_far",
+    )(me, weights, near, *bulk)
+
+
+def place_kernel(me_ref, c1, c2, c3, start_ref, out_ref, sems):
+    del start_ref
     copies = []
-    for s, chunk in enumerate((c0, c1, c2, c3)):
-        cells = pl.ds(pl.multiple_of(group_from(me, s) * TILE, TILE), TILE)
-        copies.append(pltpu.make_async_copy(chunk, out_ref.at[:, :, cells], sems.at[s]))
+    for s, chunk in enumerate((c1, c2, c3)):
+        cells = pl.ds(pl.multiple_of(group_from(me_ref[0], s + 1) * TILE, TILE), TILE)
+        copies.append(pltpu.make_async_copy(chunk, out_ref.at[pl.ds(0, NEAR), :, cells], sems.at[s]))
     for copy in copies:
         copy.start()
     for copy in copies:
         copy.wait()
 
 
-def place(me, chunks):
+def place(me, chunks, out):
     return pl.pallas_call(
         place_kernel,
-        out_shape=jax.ShapeDtypeStruct((V, MEMBERS, GROUPS * TILE), jnp.bfloat16),
-        in_specs=[SMEM] + [VMEM] * GROUPS,
+        out_shape=jax.ShapeDtypeStruct(out.shape, out.dtype),
+        in_specs=[SMEM] + [VMEM] * (GROUPS - 1) + [ANY],
         out_specs=ANY,
-        scratch_shapes=[pltpu.SemaphoreType.DMA((GROUPS,))],
+        scratch_shapes=[pltpu.SemaphoreType.DMA((GROUPS - 1,))],
+        input_output_aliases={GROUPS: 0},
+        compiler_params=ROOM,
         name="place",
-    )(me, *chunks)
+    )(me, *chunks, out)
 
 
 def ring(shift):
@@ -253,28 +343,30 @@
     return [chunks[0]] + [lax.ppermute(chunks[s], "member", ring(s)) for s in range(1, GROUPS)]
 
 
-def swap(x):
-    return lax.ppermute(x, "core", [(0, 1), (1, 0)])
-
-
-def total(core, folded):
-    first = core[0] == 0
-    top, low = folded[: HALF // 2], folded[HALF // 2 :]
-    chip = jnp.where(first, top, low) + swap(jnp.where(first, low, top))
-    copies = jnp.broadcast_to(chip[None], (CHIPS, HALF // 2, 128))
-    mine = jnp.sum(lax.all_to_all(copies, ("member", "x", "z"), 0, 0, tiled=True), axis=0)
-    return mine, swap(mine)
+def exchange(copies, axes):
+    return lax.all_to_all(copies, axes, 0, 0, tiled=True)
+
+
+def total(folded):
+    copies = exchange(spread_sum(folded[None], PLANE), ("x", "z"))
+    copies = exchange(spread_sum(copies, COLUMN), ("member", "core"))
+    return spread_sum(copies, 1)[0]
 
 
 def body(prior, readings, error_spread, mapping, slots):
-    me = lax.axis_index("member").astype(jnp.int32).reshape(1)
-    core = lax.axis_index("core").astype(jnp.int32).reshape(1)
-    observed_out, rest_out = pack(me, jnp.transpose(prior, (1, 0, 2)))
-    observed = scatter(observed_out)
-    rest = scatter(rest_out)
+    member = lax.axis_index("member").astype(jnp.int32)
+    me = member.reshape(1)
+    prior = jnp.transpose(prior, (1, 0, 2))
+    packed = pack(me, prior)
+    observed = scatter(packed)
+    bulk = scatter(pack_bulk(me, prior, packed[0]))
     folded = observe(me, slots.reshape(-1), observed, mapping[:, 0], readings[:, 0], error_spread[:, 0])
-    weights = transform(core, *total(core, folded))
-    out = place(me, scatter(analyse(me, weights, observed, rest)))
+    folded = lax.fori_loop(0, jnp.where(member < GROUPS, 1, 2), lambda i, x: total(x), folded)
+    weights, again = transform(folded)
+    near = analyse_near(me, again, observed, bulk)
+    arrived = scatter(near)
+    out = analyse_far(me, again, near[0], bulk)
+    out = place(me, arrived[1:], out)
     return (jnp.transpose(out, (1, 0, 2)), weights)
 
 

time: 73 us -> 60.3 us (0.83)
  waiting for transfers between devices: 30 us -> 12.4 us
  blocking collectives: 0 us -> 16.8 us
  starting transfers between devices: 26.2 us -> 16.9 us
  local copies, waits for them, and re-layouts: 4.86 us -> 3.43 us
  Pallas kernels: 10.6 us -> 9.68 us
    all_to_all x0 -> x1, blocking collectives: none -> 16.8 us  [exchange(): return lax.all_to_all(copies, axes, 0, 0, tiled=True)]
    ppermute x9, waiting for transfers between devices: 17.2 us -> 5.54 us  [scatter(): lax.ppermute(chunks[s], 'member', ring(s))]
    all_to_all x1, starting transfers between devices: 10.9 us -> 4.09 us  [exchange(): return lax.all_to_all(copies, axes, 0, 0, tiled=True)]
    all_to_all x1, waiting for transfers between devices: 10.4 us -> 6.84 us  [exchange(): return lax.all_to_all(copies, axes, 0, 0, tiled=True)]
    ppermute x2 -> x0, waiting for transfers between devices: 2.33 us -> none  [swap(): return lax.ppermute(x, 'core', [(0, 1), (1, 0)])]
    ppermute x9, starting transfers between devices: 15.1 us -> 12.8 us  [scatter(): lax.ppermute(chunks[s], 'member', ring(s))]
    pallas_call x4 -> x9, Pallas kernels: 8.26 us -> 7.33 us  [the longest x1 2.16 us: transform(): pl.pallas_call(transform_kernel, out_shape=[jax.ShapeDtypeStruct((K, K),...]
    broadcast_in_dim x1 -> x0, local copies, waits for them, and re-layouts: 0.93 us -> none  [total(): copies = jnp.broadcast_to(chip[None], (CHIPS, HALF // 2, 128))]
  transfers between devices with their start and end apart: 12 -> 10, of which waited for: 6 -> 3; matrix products, arithmetic and copies ran while one was open for 0% -> 0% of each run, Pallas kernels for 4% -> 14%
where the time goes in v4:
time: 60.3 us; the launch traced here: 59.9 us
  starting transfers between devices  16.9 us (28%)
  blocking collectives  16.8 us (28%)
  waiting for transfers between devices  12.4 us (21%)
  Pallas kernels  9.68 us (16%)
  local copies, waits for them, and re-layouts  3.43 us (6%)
  between operations  0.73 us (1%)
    all_to_all x1, blocking collectives, exchange(): return lax.all_to_all(copies, axes, 0, 0, tiled=True)  16.8 us
    ppermute x9, starting transfers between devices, scatter(): lax.ppermute(chunks[s], 'member', ring(s))  12.8 us
    all_to_all x1, waiting for transfers between devices, exchange(): return lax.all_to_all(copies, axes, 0, 0, tiled=True)  6.84 us
    ppermute x9, waiting for transfers between devices, scatter(): lax.ppermute(chunks[s], 'member', ring(s))  5.54 us
    all_to_all x1, starting transfers between devices, exchange(): return lax.all_to_all(copies, axes, 0, 0, tiled=True)  4.09 us
    unnamed x14, local copies, waits for them, and re-layouts  3.35 us
    pallas_call x1, Pallas kernels, observe(): pl.pallas_call(observe_kernel, out_shape=jax.ShapeDtypeStruct((HALF, 128)...  2.35 us
    pallas_call x1, Pallas kernels, transform(): pl.pallas_call(transform_kernel, out_shape=[jax.ShapeDtypeStruct((K, K),...  2.16 us
  transfers between devices with their start and end apart: 10, of which 3 were waited for; matrix products, arithmetic and copies ran while one was open for 0% of the time, Pallas kernels for 14%

profile of v4, /device:TPU:0, one launch (start us, length us, event | category | flops | bytes accessed | tf_op | source)
XLA Modules:
  0.0 59.9 jit_solution(18219825340220684549)
XLA Ops:
  0.6 1.3 %copy-done = bf16[24,12,2048]{2,0,1:T(8,128)(2,1)S(1)} copy-done((bf16[24,12,2048]{2,0,1:T(8,128)(2,1)S(1)}, bf16[24,12,2048]{2,0,1:T(8,128)(2,1)}, u32[]{:S(2)}) %copy-start) | copy-done | bytes 1179672
  2.0 1.7 %collective-permute-start = (bf16[4,24,512]{2,1,0:T(8,128)(2,1)S(1)}, bf16[4,24,512]{2,1,0:T(8,128)(2,1)S(1)}, u32[]{:S(2)}, u32[]{:S(2)}) collective-permute-start(bf16[4,24,512]{2,1,0:T(8,128)(2,1)S(1)} %get-tuple-element.35), channel_id=1, source_target_pairs={{0,32},{32,64},{64,96},{96,0},{1,33},{33,65},{65,97},{97,1},{2,34}... | collective-permute-start | bytes 294920 | tf_op jit(solution)/shard_map/ppermute | solution.py:343
  3.7 2.9 %collective-permute-start.1 = (bf16[4,24,512]{2,1,0:T(8,128)(2,1)S(1)}, bf16[4,24,512]{2,1,0:T(8,128)(2,1)S(1)}, u32[]{:S(2)}, u32[]{:S(2)}) collective-permute-start(bf16[4,24,512]{2,1,0:T(8,128)(2,1)S(1)} %get-tuple-element.36), channel_id=1, source_target_pairs={{0,64},{32,96},{64,0},{96,32},{1,65},{33,97},{65,1},{97,33},{2,66}... | collective-permute-start | bytes 294920 | tf_op jit(solution)/shard_map/ppermute | solution.py:343
  6.7 1.3 %collective-permute-start.2 = (bf16[4,24,512]{2,1,0:T(8,128)(2,1)S(1)}, bf16[4,24,512]{2,1,0:T(8,128)(2,1)S(1)}, u32[]{:S(2)}, u32[]{:S(2)}) collective-permute-start(bf16[4,24,512]{2,1,0:T(8,128)(2,1)S(1)} %get-tuple-element.37), channel_id=1, source_target_pairs={{0,96},{32,0},{64,32},{96,64},{1,97},{33,1},{65,33},{97,65},{2,98}... | collective-permute-start | bytes 294920 | tf_op jit(solution)/shard_map/ppermute | solution.py:343
  8.0 1.7 %pack_bulk.1 = (bf16[26,24,512]{2,1,0:T(8,128)(2,1)S(1)}, bf16[26,24,512]{2,1,0:T(8,128)(2,1)}, bf16[26,24,512]{2,1,0:T(8,128)(2,1)}, bf16[26,24,512]{2,1,0:T(8,128)(2,1)S(1)}) custom-call(s32[1]{0:T(128)} %bitcast.2.me_ref, bf16[12,24,2048]{2,1,0:T(8,128)(2,1)S(1)} %bitcast.17, bf16[4,24,512]{2,1,0:T(8,128)(2,1)S(1)} %get-tuple-element.34.c0.after_ref.o0), custom_call_target="tpu_custom_call" | custom-call | tf_op jit(solution)/shard_map/pack_bulk/pallas_call | solution.py:87
  9.7 0.8 %copy-done.2 = bf16[26,24,512]{2,1,0:T(8,128)(2,1)} copy-done((bf16[26,24,512]{2,1,0:T(8,128)(2,1)}, bf16[26,24,512]{2,1,0:T(8,128)(2,1)S(1)}, u32[]{:S(2)}) %copy-start.2) | copy-done | bytes 639000
  10.5 0.7 %collective-permute-start.3 = (bf16[26,24,512]{2,1,0:T(8,128)(2,1)}, bf16[26,24,512]{2,1,0:T(8,128)(2,1)S(1)}, u32[]{:S(2)}, u32[]{:S(2)}) collective-permute-start(bf16[26,24,512]{2,1,0:T(8,128)(2,1)} %get-tuple-element.41), channel_id=1, source_target_pairs={{0,32},{32,64},{64,96},{96,0},{1,33},{33,65},{65,97},{97,1},{2,34}... | collective-permute-start | bytes 1916936 | tf_op jit(solution)/shard_map/ppermute | solution.py:343
  11.2 0.8 %collective-permute-start.4 = (bf16[26,24,512]{2,1,0:T(8,128)(2,1)}, bf16[26,24,512]{2,1,0:T(8,128)(2,1)S(1)}, u32[]{:S(2)}, u32[]{:S(2)}) collective-permute-start(bf16[26,24,512]{2,1,0:T(8,128)(2,1)} %get-tuple-element.42), channel_id=1, source_target_pairs={{0,64},{32,96},{64,0},{96,32},{1,65},{33,97},{65,1},{97,33},{2,66}... | collective-permute-start | bytes 1916936 | tf_op jit(solution)/shard_map/ppermute | solution.py:343
  12.2 2.0 %collective-permute-start.5 = (bf16[26,24,512]{2,1,0:T(8,128)(2,1)}, bf16[26,24,512]{2,1,0:T(8,128)(2,1)S(1)}, u32[]{:S(2)}, u32[]{:S(2)}) collective-permute-start(bf16[26,24,512]{2,1,0:T(8,128)(2,1)} %copy-done.2), channel_id=1, source_target_pairs={{0,96},{32,0},{64,32},{96,64},{1,97},{33,1},{65,33},{97,65},{2,98}... | collective-permute-start | bytes 1916936 | tf_op jit(solution)/shard_map/ppermute | solution.py:343
  14.2 1.1 %copy-done.1 = bf16[12,1,2,128,128]{4,3,2,1,0:T(8,128)(2,1)S(1)} copy-done((bf16[12,1,2,128,128]{4,3,2,1,0:T(8,128)(2,1)S(1)}, bf16[12,1,2,128,128]{4,3,2,1,0:T(8,128)(2,1)}, u32[]{:S(2)}) %copy-start.1) | copy-done | bytes 786456
  15.3 2.4 %observe.1 = f32[48,128]{1,0:T(8,128)S(1)} custom-call(s32[1]{0:T(128)} %bitcast.2.me_ref, s32[24]{0:T(128)S(1)} %reshape.11.slots_ref, bf16[4,24,512]{2,1,0:T(8,128)(2,1)S(1)} %get-tuple-element.34.c0.after_ref.o0, bf16[4,24,512]{2,1,0:T(8,128)(2,1)S(1)} %collective-permute-done.c1.o1, bf16[4,24,512]{2,1,0:T(8,128)(2,1)S(1)} %collective-permute-done.1.c2.o2, ...), custom_call_target="tpu_custom_call" | custom-call | tf_op jit(solution)/shard_map/observe/pallas_call | solution.py:157
  17.6 28.5 %while.10 = (s32[]{:T(128)}, f32[48,128]{1,0:T(8,128)S(1)}, s32[]{:T(128)}, s32[]{:T(128)}) while((s32[]{:T(128)}, f32[48,128]{1,0:T(8,128)S(1)}, s32[]{:T(128)}, s32[]{:T(128)}) %tuple.23), condition=%wide.region_1.2_spmd, body=%wide.region_0.1_spmd.sunk | while | flops 2 | bytes 1376341 | solution.py:364
  17.7 16.8 %all_to_all.12.parts_ref = f32[16,48,128]{2,1,0:T(8,128)S(1)} all-to-all(f32[16,48,128]{2,1,0:T(8,128)S(1)} %spread_sum.3), channel_id=1, replica_groups=mesh['member'=4,'x'=4,'z'=4,'core'=2] {'x','z'}, dimensions={0} | all-to-all | bytes 786432 | tf_op jit(solution)/shard_map/while/body/all_to_all | solution.py:347
  34.5 0.7 %spread_sum.4 = f32[8,48,128]{2,1,0:T(8,128)} custom-call(f32[16,48,128]{2,1,0:T(8,128)S(1)} %all_to_all.12.parts_ref), custom_call_target="tpu_custom_call" | custom-call | tf_op jit(solution)/shard_map/while/body/spread_sum/pallas_call | solution.py:194
  35.2 4.1 %all-to-all-start.1 = ((f32[8,48,128]{2,1,0:T(8,128)}), f32[8,48,128]{2,1,0:T(8,128)S(1)}, u32[]{:S(2)}, u32[]{:S(2)}) async-start(f32[8,48,128]{2,1,0:T(8,128)} %spread_sum.4), calls=%async_computation.1 | async-start | bytes 393216 | tf_op jit(solution)/shard_map/while/body/all_to_all | solution.py:347
  39.3 6.8 %all-to-all-done.1.parts_ref = f32[8,48,128]{2,1,0:T(8,128)S(1)} async-done(((f32[8,48,128]{2,1,0:T(8,128)}), f32[8,48,128]{2,1,0:T(8,128)S(1)}, u32[]{:S(2)}, u32[]{:S(2)}) %all-to-all-start.1) | async-done | bytes 196640 | tf_op jit(solution)/shard_map/while/body/all_to_all | solution.py:347
  46.2 2.2 %transform.1 = (f32[96,96]{1,0:T(8,128)}, f32[96,96]{1,0:T(8,128)S(1)}) custom-call(f32[48,128]{1,0:T(8,128)S(1)} %get-tuple-element.38.parts_ref), custom_call_target="tpu_custom_call" | custom-call | flops 40000000000 | tf_op jit(solution)/shard_map/transform/pallas_call | solution.py:229
  48.8 0.6 %collective-permute-start.6 = (bf16[6,24,512]{2,1,0:T(8,128)(2,1)S(1)}, bf16[6,24,512]{2,1,0:T(8,128)(2,1)S(1)}, u32[]{:S(2)}, u32[]{:S(2)}) collective-permute-start(bf16[6,24,512]{2,1,0:T(8,128)(2,1)S(1)} %get-tuple-element.44), channel_id=1, source_target_pairs={{0,32},{32,64},{64,96},{96,0},{1,33},{33,65},{65,97},{97,1},{2,34}... | collective-permute-start | bytes 442376 | tf_op jit(solution)/shard_map/ppermute | solution.py:343
  49.4 2.1 %collective-permute-start.7 = (bf16[6,24,512]{2,1,0:T(8,128)(2,1)S(1)}, bf16[6,24,512]{2,1,0:T(8,128)(2,1)S(1)}, u32[]{:S(2)}, u32[]{:S(2)}) collective-permute-start(bf16[6,24,512]{2,1,0:T(8,128)(2,1)S(1)} %get-tuple-element.45), channel_id=1, source_target_pairs={{0,64},{32,96},{64,0},{96,32},{1,65},{33,97},{65,1},{97,33},{2,66}... | collective-permute-start | bytes 442376 | tf_op jit(solution)/shard_map/ppermute | solution.py:343
  51.5 0.7 %collective-permute-start.8 = (bf16[6,24,512]{2,1,0:T(8,128)(2,1)S(1)}, bf16[6,24,512]{2,1,0:T(8,128)(2,1)S(1)}, u32[]{:S(2)}, u32[]{:S(2)}) collective-permute-start(bf16[6,24,512]{2,1,0:T(8,128)(2,1)S(1)} %get-tuple-element.46), channel_id=1, source_target_pairs={{0,96},{32,0},{64,32},{96,64},{1,97},{33,1},{65,33},{97,65},{2,98}... | collective-permute-start | bytes 442376 | tf_op jit(solution)/shard_map/ppermute | solution.py:343
  52.2 1.4 %analyse_far.1.start_ref = bf16[12,24,2048]{2,1,0:T(8,128)(2,1)} custom-call(s32[1]{0:T(128)} %bitcast.2.me_ref, f32[96,96]{1,0:T(8,128)S(1)} %get-tuple-element.39.w_ref, bf16[6,24,512]{2,1,0:T(8,128)(2,1)S(1)} %get-tuple-element.47.near_ref, bf16[26,24,512]{2,1,0:T(8,128)(2,1)S(1)} %get-tuple-element.40.b0, ...), custom_call_target="tpu_custom_call" | custom-call | tf_op jit(solution)/shard_map/analyse_far/pallas_call | solution.py:298
  53.6 4.9 %collective-permute-done.6.c1 = bf16[6,24,512]{2,1,0:T(8,128)(2,1)S(1)} collective-permute-done((bf16[6,24,512]{2,1,0:T(8,128)(2,1)S(1)}, bf16[6,24,512]{2,1,0:T(8,128)(2,1)S(1)}, u32[]{:S(2)}, u32[]{:S(2)}) %collective-permute-start.6) | collective-permute-done | bytes 147488 | tf_op jit(solution)/shard_map/ppermute | solution.py:343
  58.5 0.6 %collective-permute-done.8.c3 = bf16[6,24,512]{2,1,0:T(8,128)(2,1)S(1)} collective-permute-done((bf16[6,24,512]{2,1,0:T(8,128)(2,1)S(1)}, bf16[6,24,512]{2,1,0:T(8,128)(2,1)S(1)}, u32[]{:S(2)}, u32[]{:S(2)}) %collective-permute-start.8) | collective-permute-done | bytes 147488 | tf_op jit(solution)/shard_map/ppermute | solution.py:343
  59.2 0.8 %place.1 = bf16[12,24,2048]{2,1,0:T(8,128)(2,1)} custom-call(s32[1]{0:T(128)} %bitcast.2.me_ref, bf16[6,24,512]{2,1,0:T(8,128)(2,1)S(1)} %collective-permute-done.6.c1, bf16[6,24,512]{2,1,0:T(8,128)(2,1)S(1)} %collective-permute-done.7.c2, bf16[6,24,512]{2,1,0:T(8,128)(2,1)S(1)} %collective-permute-done.8.c3, ...), custom_call_target="tpu_custom_call", output_to_operand_aliasing={{}: (4, {})} | custom-call | tf_op jit(solution)/shard_map/place/pallas_call | solution.py:326
  (23 shorter events, 0.8 us)
Async XLA Ops:
  0.6 1.3 %copy-start = (bf16[24,12,2048]{2,0,1:T(8,128)(2,1)S(1)}, bf16[24,12,2048]{2,0,1:T(8,128)(2,1)}, u32[]{:S(2)}) copy-start(bf16[24,12,2048]{2,0,1:T(8,128)(2,1)} %param.7) | copy-start | bytes 3538948
  1.9 10.1 %copy-start.3 = (f32[12,1,128]{2,1,0:T(1,128)S(1)}, f32[12,1,128]{2,1,0:T(1,128)}, u32[]{:S(2)}) copy-start(f32[12,1,128]{2,1,0:T(1,128)} %param.9) | copy-start | bytes 18436
  1.9 10.1 %copy-start.4 = (f32[12,1,128]{2,1,0:T(1,128)S(1)}, f32[12,1,128]{2,1,0:T(1,128)}, u32[]{:S(2)}) copy-start(f32[12,1,128]{2,1,0:T(1,128)} %param.8) | copy-start | bytes 18436
  1.9 10.1 %copy-start.5 = (s32[12,1,2]{0,2,1:T(2,128)S(1)}, s32[12,1,2]{0,2,1:T(2,128)}, u32[]{:S(2)}) copy-start(s32[12,1,2]{0,2,1:T(2,128)} %param.11) | copy-start | bytes 292
  2.0 10.2 %collective-permute-start = (bf16[4,24,512]{2,1,0:T(8,128)(2,1)S(1)}, bf16[4,24,512]{2,1,0:T(8,128)(2,1)S(1)}, u32[]{:S(2)}, u32[]{:S(2)}) collective-permute-start(bf16[4,24,512]{2,1,0:T(8,128)(2,1)S(1)} %get-tuple-element.35), channel_id=1, source_target_pairs={{0,32},{32,64},{64,96},{96,0},{1,33},{33,65},{65,97},{97,1},{2,34}... | collective-permute-start | bytes 294920 | tf_op jit(solution)/shard_map/ppermute | solution.py:343
  3.7 10.4 %collective-permute-start.1 = (bf16[4,24,512]{2,1,0:T(8,128)(2,1)S(1)}, bf16[4,24,512]{2,1,0:T(8,128)(2,1)S(1)}, u32[]{:S(2)}, u32[]{:S(2)}) collective-permute-start(bf16[4,24,512]{2,1,0:T(8,128)(2,1)S(1)} %get-tuple-element.36), channel_id=1, source_target_pairs={{0,64},{32,96},{64,0},{96,32},{1,65},{33,97},{65,1},{97,33},{2,66}... | collective-permute-start | bytes 294920 | tf_op jit(solution)/shard_map/ppermute | solution.py:343
  6.7 7.5 %collective-permute-start.2 = (bf16[4,24,512]{2,1,0:T(8,128)(2,1)S(1)}, bf16[4,24,512]{2,1,0:T(8,128)(2,1)S(1)}, u32[]{:S(2)}, u32[]{:S(2)}) collective-permute-start(bf16[4,24,512]{2,1,0:T(8,128)(2,1)S(1)} %get-tuple-element.37), channel_id=1, source_target_pairs={{0,96},{32,0},{64,32},{96,64},{1,97},{33,1},{65,33},{97,65},{2,98}... | collective-permute-start | bytes 294920 | tf_op jit(solution)/shard_map/ppermute | solution.py:343
  9.7 0.9 %copy-start.2 = (bf16[26,24,512]{2,1,0:T(8,128)(2,1)}, bf16[26,24,512]{2,1,0:T(8,128)(2,1)S(1)}, u32[]{:S(2)}) copy-start(bf16[26,24,512]{2,1,0:T(8,128)(2,1)S(1)} %get-tuple-element.43) | copy-start | bytes 1916932
  10.5 37.8 %collective-permute-start.3 = (bf16[26,24,512]{2,1,0:T(8,128)(2,1)}, bf16[26,24,512]{2,1,0:T(8,128)(2,1)S(1)}, u32[]{:S(2)}, u32[]{:S(2)}) collective-permute-start(bf16[26,24,512]{2,1,0:T(8,128)(2,1)} %get-tuple-element.41), channel_id=1, source_target_pairs={{0,32},{32,64},{64,96},{96,0},{1,33},{33,65},{65,97},{97,1},{2,34}... | collective-permute-start | bytes 1916936 | tf_op jit(solution)/shard_map/ppermute | solution.py:343
  11.2 37.1 %collective-permute-start.4 = (bf16[26,24,512]{2,1,0:T(8,128)(2,1)}, bf16[26,24,512]{2,1,0:T(8,128)(2,1)S(1)}, u32[]{:S(2)}, u32[]{:S(2)}) collective-permute-start(bf16[26,24,512]{2,1,0:T(8,128)(2,1)} %get-tuple-element.42), channel_id=1, source_target_pairs={{0,64},{32,96},{64,0},{96,32},{1,65},{33,97},{65,1},{97,33},{2,66}... | collective-permute-start | bytes 1916936 | tf_op jit(solution)/shard_map/ppermute | solution.py:343
  12.2 36.2 %collective-permute-start.5 = (bf16[26,24,512]{2,1,0:T(8,128)(2,1)}, bf16[26,24,512]{2,1,0:T(8,128)(2,1)S(1)}, u32[]{:S(2)}, u32[]{:S(2)}) collective-permute-start(bf16[26,24,512]{2,1,0:T(8,128)(2,1)} %copy-done.2), channel_id=1, source_target_pairs={{0,96},{32,0},{64,32},{96,64},{1,97},{33,1},{65,33},{97,65},{2,98}... | collective-permute-start | bytes 1916936 | tf_op jit(solution)/shard_map/ppermute | solution.py:343
  14.1 1.1 %copy-start.1 = (bf16[12,1,2,128,128]{4,3,2,1,0:T(8,128)(2,1)S(1)}, bf16[12,1,2,128,128]{4,3,2,1,0:T(8,128)(2,1)}, u32[]{:S(2)}) copy-start(bf16[12,1,2,128,128]{4,3,2,1,0:T(8,128)(2,1)} %param.10) | copy-start | bytes 2359300
  35.2 10.9 %all-to-all-start.1 = ((f32[8,48,128]{2,1,0:T(8,128)}), f32[8,48,128]{2,1,0:T(8,128)S(1)}, u32[]{:S(2)}, u32[]{:S(2)}) async-start(f32[8,48,128]{2,1,0:T(8,128)} %spread_sum.4), calls=%async_computation.1 | async-start | bytes 393216 | tf_op jit(solution)/shard_map/while/body/all_to_all | solution.py:347
  48.8 9.8 %collective-permute-start.6 = (bf16[6,24,512]{2,1,0:T(8,128)(2,1)S(1)}, bf16[6,24,512]{2,1,0:T(8,128)(2,1)S(1)}, u32[]{:S(2)}, u32[]{:S(2)}) collective-permute-start(bf16[6,24,512]{2,1,0:T(8,128)(2,1)S(1)} %get-tuple-element.44), channel_id=1, source_target_pairs={{0,32},{32,64},{64,96},{96,0},{1,33},{33,65},{65,97},{97,1},{2,34}... | collective-permute-start | bytes 442376 | tf_op jit(solution)/shard_map/ppermute | solution.py:343
  49.4 9.1 %collective-permute-start.7 = (bf16[6,24,512]{2,1,0:T(8,128)(2,1)S(1)}, bf16[6,24,512]{2,1,0:T(8,128)(2,1)S(1)}, u32[]{:S(2)}, u32[]{:S(2)}) collective-permute-start(bf16[6,24,512]{2,1,0:T(8,128)(2,1)S(1)} %get-tuple-element.45), channel_id=1, source_target_pairs={{0,64},{32,96},{64,0},{96,32},{1,65},{33,97},{65,1},{97,33},{2,66}... | collective-permute-start | bytes 442376 | tf_op jit(solution)/shard_map/ppermute | solution.py:343
  51.5 7.7 %collective-permute-start.8 = (bf16[6,24,512]{2,1,0:T(8,128)(2,1)S(1)}, bf16[6,24,512]{2,1,0:T(8,128)(2,1)S(1)}, u32[]{:S(2)}, u32[]{:S(2)}) collective-permute-start(bf16[6,24,512]{2,1,0:T(8,128)(2,1)S(1)} %get-tuple-element.46), channel_id=1, source_target_pairs={{0,96},{32,0},{64,32},{96,64},{1,97},{33,1},{65,33},{97,65},{2,98}... | collective-permute-start | bytes 442376 | tf_op jit(solution)/shard_map/ppermute | solution.py:343

commit v5 on v4

--- a/solution.py
+++ b/solution.py
@@ -69,13 +69,12 @@
     del after_ref
     outs, sems = refs[:-1], refs[-1]
     copies = []
-    for s in range(GROUPS):
+    for s, out in enumerate(outs, 1):
         cells = pl.ds(pl.multiple_of(group_to(me_ref[0], s) * TILE, TILE), TILE)
-        if NEXT:
-            copies.append((prior_ref.at[pl.ds(VOBS, NEXT), :, cells], outs[s].at[pl.ds(0, NEXT)]))
+        copies.append((prior_ref.at[pl.ds(VOBS, NEXT), :, cells], out.at[pl.ds(0, NEXT)]))
         for c in range(GROUPS):
             source = prior_ref.at[pl.ds(NEAR, FAR), :, pl.ds(c * TILE, TILE)]
-            copies.append((source, outs[s].at[pl.ds(NEXT + c * FAR, FAR)]))
+            copies.append((source, out.at[pl.ds(NEXT + c * FAR, FAR)]))
     copies = [pltpu.make_async_copy(*pair, sems.at[n]) for n, pair in enumerate(copies)]
     for copy in copies:
         copy.start()
@@ -86,10 +85,10 @@
 def pack_bulk(me, prior, after):
     return pl.pallas_call(
         pack_bulk_kernel,
-        out_shape=[jax.ShapeDtypeStruct((NEXT + GROUPS * FAR, MEMBERS, TILE), prior.dtype)] * GROUPS,
+        out_shape=[jax.ShapeDtypeStruct((NEXT + GROUPS * FAR, MEMBERS, TILE), prior.dtype)] * (GROUPS - 1),
         in_specs=[SMEM, ANY, ANY],
-        out_specs=[VMEM] * GROUPS,
-        scratch_shapes=[pltpu.SemaphoreType.DMA((GROUPS * (GROUPS + 1),))],
+        out_specs=[HBM] * (GROUPS - 1),
+        scratch_shapes=[pltpu.SemaphoreType.DMA(((GROUPS - 1) * (GROUPS + 1),))],
         compiler_params=ROOM,
         name="pack_bulk",
     )(me, prior, after)
@@ -256,28 +255,30 @@
     return mixed + keep * center
 
 
-def near_kernel(me_ref, w_ref, o0, o1, o2, o3, b0, b1, b2, b3, a0, a1, a2, a3, turned):
+def near_kernel(me_ref, w_ref, prior_ref, o1, o2, o3, b1, b2, b3, a0, a1, a2, a3, turned):
     coeffs, keep = coefficients(me_ref[0], w_ref, turned)
+    cells = pl.ds(pl.multiple_of(me_ref[0] * TILE, TILE), TILE)
     for v in range(NEAR):
-        parts = [ref[v] for ref in (o0, o1, o2, o3)] if v < VOBS else [ref[v - VOBS] for ref in (b0, b1, b2, b3)]
+        parts = [ref[v] for ref in (o1, o2, o3)] if v < VOBS else [ref[v - VOBS] for ref in (b1, b2, b3)]
+        parts = [prior_ref[v, :, cells]] + parts
         mixed = mix(coeffs, keep, parts)
         for g, out in enumerate((a0, a1, a2, a3)):
             out[v] = mixed[g * MEMBERS : (g + 1) * MEMBERS].astype(jnp.bfloat16)
 
 
-def analyse_near(me, weights, observed, bulk):
+def analyse_near(me, weights, prior, observed, bulk):
     return pl.pallas_call(
         near_kernel,
         out_shape=[jax.ShapeDtypeStruct((NEAR, MEMBERS, TILE), jnp.bfloat16)] * GROUPS,
-        in_specs=[SMEM] + [VMEM] * 9,
+        in_specs=[SMEM] + [VMEM] * 8,
         out_specs=[VMEM] * GROUPS,
         scratch_shapes=[pltpu.VMEM((K, K), jnp.float32)],
         compiler_params=ROOM,
         name="analyse_near",
-    )(me, weights, *observed, *bulk)
-
-
-def far_kernel(me_ref, w_ref, near_ref, b0, b1, b2, b3, out_ref, turned, result, sems):
+    )(me, weights, prior, *observed, *bulk)
+
+
+def far_kernel(me_ref, w_ref, near_ref, prior_ref, b1, b2, b3, out_ref, turned, result, sems):
     me = me_ref[0]
     cells = pl.ds(pl.multiple_of(me * TILE, TILE), TILE)
     copies = [pltpu.make_async_copy(near_ref, out_ref.at[pl.ds(0, NEAR), :, cells], sems.at[0])]
@@ -285,16 +286,17 @@
     coeffs, keep = coefficients(me, w_ref, turned)
     for v in range(FAR):
         for c in range(GROUPS):
-            parts = [ref[NEXT + c * FAR + v] for ref in (b0, b1, b2, b3)]
+            lanes = pl.ds(c * TILE, TILE)
+            parts = [prior_ref[NEAR + v, :, lanes]] + [ref[NEXT + c * FAR + v] for ref in (b1, b2, b3)]
             mixed = mix(coeffs[:MEMBERS], keep[:MEMBERS], parts)
-            result[v, :, pl.ds(c * TILE, TILE)] = mixed.astype(jnp.bfloat16)
+            result[v, :, lanes] = mixed.astype(jnp.bfloat16)
         copies.append(pltpu.make_async_copy(result.at[v], out_ref.at[NEAR + v], sems.at[1 + v]))
         copies[-1].start()
     for copy in copies:
         copy.wait()
 
 
-def analyse_far(me, weights, near, bulk):
+def analyse_far(me, weights, near, prior, bulk):
     return pl.pallas_call(
         far_kernel,
         out_shape=jax.ShapeDtypeStruct((V, MEMBERS, GROUPS * TILE), jnp.bfloat16),
@@ -307,7 +309,7 @@
         ],
         compiler_params=ROOM,
         name="analyse_far",
-    )(me, weights, near, *bulk)
+    )(me, weights, near, prior, *bulk)
 
 
 def place_kernel(me_ref, c1, c2, c3, start_ref, out_ref, sems):
@@ -340,7 +342,7 @@
 
 
 def scatter(chunks):
-    return [chunks[0]] + [lax.ppermute(chunks[s], "member", ring(s)) for s in range(1, GROUPS)]
+    return [lax.ppermute(chunk, "member", ring(s)) for s, chunk in enumerate(chunks, 1)]
 
 
 def exchange(copies, axes):
@@ -358,15 +360,16 @@
     me = member.reshape(1)
     prior = jnp.transpose(prior, (1, 0, 2))
     packed = pack(me, prior)
-    observed = scatter(packed)
+    observed = scatter(packed[1:])
     bulk = scatter(pack_bulk(me, prior, packed[0]))
-    folded = observe(me, slots.reshape(-1), observed, mapping[:, 0], readings[:, 0], error_spread[:, 0])
-    folded = lax.fori_loop(0, jnp.where(member < GROUPS, 1, 2), lambda i, x: total(x), folded)
+    folded = observe(
+        me, slots.reshape(-1), [packed[0]] + observed, mapping[:, 0], readings[:, 0], error_spread[:, 0]
+    )
+    folded = lax.cond(member < GROUPS, total, lambda x: x, folded)
     weights, again = transform(folded)
-    near = analyse_near(me, again, observed, bulk)
-    arrived = scatter(near)
-    out = analyse_far(me, again, near[0], bulk)
-    out = place(me, arrived[1:], out)
+    near = analyse_near(me, again, prior, observed, bulk)
+    arrived = scatter(near[1:])
+    out = place(me, arrived, analyse_far(me, again, near[0], prior, bulk))
     return (jnp.transpose(out, (1, 0, 2)), weights)
 
 

time: 60.3 us -> 57.6 us (0.955)
  blocking collectives: 16.8 us -> 27.5 us
  waiting for transfers between devices: 12.4 us -> 5.17 us
  starting transfers between devices: 16.9 us -> 13.1 us
  Pallas kernels: 9.68 us -> 8.52 us
  local copies, waits for them, and re-layouts: 3.43 us -> 2.3 us
    all_to_all x1 -> x2, blocking collectives: 16.8 us -> 27.5 us  [exchange(): return lax.all_to_all(copies, axes, 0, 0, tiled=True)]
    all_to_all x1 -> x0, waiting for transfers between devices: 6.84 us -> none  [exchange(): return lax.all_to_all(copies, axes, 0, 0, tiled=True)]
    all_to_all x1 -> x0, starting transfers between devices: 4.09 us -> none  [exchange(): return lax.all_to_all(copies, axes, 0, 0, tiled=True)]
    unnamed x14 -> x16, local copies, waits for them, and re-layouts: 3.35 us -> 2.22 us
    pallas_call x3, Pallas kernels: 0.76 us -> 0.07 us  [spread_sum(): pl.pallas_call(spread_kernel, out_shape=jax.ShapeDtypeStruct((copies, HAL...]
  transfers between devices with their start and end apart: 10 -> 9, of which waited for: 3 -> 3; matrix products, arithmetic and copies ran while one was open for 0% -> 0% of each run, Pallas kernels for 14% -> 13%
where the time goes in v5:
time: 57.6 us; the launch traced here: 57.4 us
  blocking collectives  27.5 us (48%)
  starting transfers between devices  13.1 us (23%)
  Pallas kernels  8.52 us (15%)
  waiting for transfers between devices  5.17 us (9%)
  local copies, waits for them, and re-layouts  2.3 us (4%)
  between operations  0.74 us (1%)
    all_to_all x2, blocking collectives, exchange(): return lax.all_to_all(copies, axes, 0, 0, tiled=True)  27.5 us
    ppermute x9, starting transfers between devices, scatter(): lax.ppermute(chunk, 'member', ring(s))  13.1 us
    ppermute x9, waiting for transfers between devices, scatter(): lax.ppermute(chunk, 'member', ring(s))  5.17 us
    pallas_call x1, Pallas kernels, observe(): pl.pallas_call(observe_kernel, out_shape=jax.ShapeDtypeStruct((HALF, 128)...  2.36 us
    unnamed x16, local copies, waits for them, and re-layouts  2.22 us
    pallas_call x1, Pallas kernels, transform(): pl.pallas_call(transform_kernel, out_shape=[jax.ShapeDtypeStruct((K, K),...  2.16 us
    pallas_call x1, Pallas kernels, analyse_far(): pl.pallas_call(far_kernel, out_shape=jax.ShapeDtypeStruct((V, MEMBERS, GR...  1.43 us
    pallas_call x1, Pallas kernels, pack_bulk(): pl.pallas_call(pack_bulk_kernel, out_shape=[jax.ShapeDtypeStruct((NEXT +...  1.16 us
  transfers between devices with their start and end apart: 9, of which 3 were waited for; matrix products, arithmetic and copies ran while one was open for 0% of the time, Pallas kernels for 13%

profile of v5, /device:TPU:0, one launch (start us, length us, event | category | flops | bytes accessed | tf_op | source)
XLA Modules:
  0.0 57.4 jit_solution(589703735367932211)
XLA Ops:
  0.6 1.3 %copy-done = bf16[24,12,2048]{2,0,1:T(8,128)(2,1)S(1)} copy-done((bf16[24,12,2048]{2,0,1:T(8,128)(2,1)S(1)}, bf16[24,12,2048]{2,0,1:T(8,128)(2,1)}, u32[]{:S(2)}) %copy-start) | copy-done | bytes 1179672
  1.9 0.1 pack.1
  2.0 1.7 %collective-permute-start = (bf16[4,24,512]{2,1,0:T(8,128)(2,1)S(1)}, bf16[4,24,512]{2,1,0:T(8,128)(2,1)S(1)}, u32[]{:S(2)}, u32[]{:S(2)}) collective-permute-start(bf16[4,24,512]{2,1,0:T(8,128)(2,1)S(1)} %get-tuple-element.21), channel_id=1, source_target_pairs={{0,32},{32,64},{64,96},{96,0},{1,33},{33,65},{65,97},{97,1},{2,34}... | collective-permute-start | bytes 294920 | tf_op jit(solution)/shard_map/ppermute | solution.py:345
  3.8 2.9 %collective-permute-start.1 = (bf16[4,24,512]{2,1,0:T(8,128)(2,1)S(1)}, bf16[4,24,512]{2,1,0:T(8,128)(2,1)S(1)}, u32[]{:S(2)}, u32[]{:S(2)}) collective-permute-start(bf16[4,24,512]{2,1,0:T(8,128)(2,1)S(1)} %get-tuple-element.22), channel_id=1, source_target_pairs={{0,64},{32,96},{64,0},{96,32},{1,65},{33,97},{65,1},{97,33},{2,66}... | collective-permute-start | bytes 294920 | tf_op jit(solution)/shard_map/ppermute | solution.py:345
  6.7 1.3 %collective-permute-start.2 = (bf16[4,24,512]{2,1,0:T(8,128)(2,1)S(1)}, bf16[4,24,512]{2,1,0:T(8,128)(2,1)S(1)}, u32[]{:S(2)}, u32[]{:S(2)}) collective-permute-start(bf16[4,24,512]{2,1,0:T(8,128)(2,1)S(1)} %get-tuple-element.23), channel_id=1, source_target_pairs={{0,96},{32,0},{64,32},{96,64},{1,97},{33,1},{65,33},{97,65},{2,98}... | collective-permute-start | bytes 294920 | tf_op jit(solution)/shard_map/ppermute | solution.py:345
  8.0 1.2 %pack_bulk.1 = (bf16[26,24,512]{2,1,0:T(8,128)(2,1)}, bf16[26,24,512]{2,1,0:T(8,128)(2,1)}, bf16[26,24,512]{2,1,0:T(8,128)(2,1)S(1)}) custom-call(s32[1]{0:T(128)} %bitcast.2.me_ref, bf16[12,24,2048]{2,1,0:T(8,128)(2,1)S(1)} %bitcast.13, bf16[4,24,512]{2,1,0:T(8,128)(2,1)S(1)} %get-tuple-element.20.c0.after_ref), custom_call_target="tpu_custom_call" | custom-call | tf_op jit(solution)/shard_map/pack_bulk/pallas_call | solution.py:86
  9.2 0.8 %copy-done.3 = bf16[26,24,512]{2,1,0:T(8,128)(2,1)} copy-done((bf16[26,24,512]{2,1,0:T(8,128)(2,1)}, bf16[26,24,512]{2,1,0:T(8,128)(2,1)S(1)}, u32[]{:S(2)}) %copy-start.3) | copy-done | bytes 639000
  10.0 0.7 %collective-permute-start.3 = (bf16[26,24,512]{2,1,0:T(8,128)(2,1)}, bf16[26,24,512]{2,1,0:T(8,128)(2,1)S(1)}, u32[]{:S(2)}, u32[]{:S(2)}) collective-permute-start(bf16[26,24,512]{2,1,0:T(8,128)(2,1)} %get-tuple-element.25), channel_id=1, source_target_pairs={{0,32},{32,64},{64,96},{96,0},{1,33},{33,65},{65,97},{97,1},{2,34}... | collective-permute-start | bytes 1916936 | tf_op jit(solution)/shard_map/ppermute | solution.py:345
  10.7 0.8 %collective-permute-start.4 = (bf16[26,24,512]{2,1,0:T(8,128)(2,1)}, bf16[26,24,512]{2,1,0:T(8,128)(2,1)S(1)}, u32[]{:S(2)}, u32[]{:S(2)}) collective-permute-start(bf16[26,24,512]{2,1,0:T(8,128)(2,1)} %get-tuple-element.26), channel_id=1, source_target_pairs={{0,64},{32,96},{64,0},{96,32},{1,65},{33,97},{65,1},{97,33},{2,66}... | collective-permute-start | bytes 1916936 | tf_op jit(solution)/shard_map/ppermute | solution.py:345
  11.5 0.1 copy.9
  11.7 2.0 %collective-permute-start.5 = (bf16[26,24,512]{2,1,0:T(8,128)(2,1)}, bf16[26,24,512]{2,1,0:T(8,128)(2,1)S(1)}, u32[]{:S(2)}, u32[]{:S(2)}) collective-permute-start(bf16[26,24,512]{2,1,0:T(8,128)(2,1)} %copy-done.3), channel_id=1, source_target_pairs={{0,96},{32,0},{64,32},{96,64},{1,97},{33,1},{65,33},{97,65},{2,98}... | collective-permute-start | bytes 1916936 | tf_op jit(solution)/shard_map/ppermute | solution.py:345
  13.7 2.4 %observe.1 = f32[48,128]{1,0:T(8,128)S(1)} custom-call(s32[1]{0:T(128)} %bitcast.2.me_ref, s32[24]{0:T(128)S(1)} %reshape.11.slots_ref, bf16[4,24,512]{2,1,0:T(8,128)(2,1)S(1)} %get-tuple-element.20.c0.after_ref, bf16[4,24,512]{2,1,0:T(8,128)(2,1)S(1)} %collective-permute-done.c1.o1, bf16[4,24,512]{2,1,0:T(8,128)(2,1)S(1)} %collective-permute-done.1.c2.o2, ...), custom_call_target="tpu_custom_call" | custom-call | tf_op jit(solution)/shard_map/observe/pallas_call | solution.py:156
  16.1 27.6 %conditional.1 = (f32[48,128]{1,0:T(8,128)S(1)}) conditional(s32[]{:T(128)} %convert_element_type.3, f32[48,128]{1,0:T(8,128)S(1)} %observe.1, f32[48,128]{1,0:T(8,128)S(1)} %observe.1), branch_computations={%region_0.0_spmd, %region_1.0_spmd} | conditional | bytes 1179656 | solution.py:368
  16.1 16.8 %all_to_all.8.parts_ref = f32[16,48,128]{2,1,0:T(8,128)S(1)} all-to-all(f32[16,48,128]{2,1,0:T(8,128)S(1)} %spread_sum.3), channel_id=1, replica_groups=mesh['member'=4,'x'=4,'z'=4,'core'=2] {'x','z'}, dimensions={0} | all-to-all | bytes 786432 | tf_op jit(solution)/shard_map/cond/branch_1_fun/all_to_all | solution.py:349
  32.9 10.7 %all_to_all.9.parts_ref = f32[8,48,128]{2,1,0:T(8,128)S(1)} all-to-all(f32[8,48,128]{2,1,0:T(8,128)S(1)} %spread_sum.4), channel_id=1, replica_groups=mesh['member'=4,'x'=4,'z'=4,'core'=2] {'member','core'}, dimensions={0} | all-to-all | bytes 393216 | tf_op jit(solution)/shard_map/cond/branch_1_fun/all_to_all | solution.py:349
  43.7 2.2 %transform.1 = (f32[96,96]{1,0:T(8,128)}, f32[96,96]{1,0:T(8,128)S(1)}) custom-call(f32[48,128]{1,0:T(8,128)S(1)} %get-tuple-element.35.parts_ref), custom_call_target="tpu_custom_call" | custom-call | flops 40000000000 | tf_op jit(solution)/shard_map/transform/pallas_call | solution.py:228
  45.9 0.4 analyse_near.1
  46.3 0.6 %collective-permute-start.6 = (bf16[6,24,512]{2,1,0:T(8,128)(2,1)S(1)}, bf16[6,24,512]{2,1,0:T(8,128)(2,1)S(1)}, u32[]{:S(2)}, u32[]{:S(2)}) collective-permute-start(bf16[6,24,512]{2,1,0:T(8,128)(2,1)S(1)} %get-tuple-element.28), channel_id=1, source_target_pairs={{0,32},{32,64},{64,96},{96,0},{1,33},{33,65},{65,97},{97,1},{2,34}... | collective-permute-start | bytes 442376 | tf_op jit(solution)/shard_map/ppermute | solution.py:345
  46.9 3.1 %collective-permute-start.7 = (bf16[6,24,512]{2,1,0:T(8,128)(2,1)S(1)}, bf16[6,24,512]{2,1,0:T(8,128)(2,1)S(1)}, u32[]{:S(2)}, u32[]{:S(2)}) collective-permute-start(bf16[6,24,512]{2,1,0:T(8,128)(2,1)S(1)} %get-tuple-element.29), channel_id=1, source_target_pairs={{0,64},{32,96},{64,0},{96,32},{1,65},{33,97},{65,1},{97,33},{2,66}... | collective-permute-start | bytes 442376 | tf_op jit(solution)/shard_map/ppermute | solution.py:345
  50.0 1.4 %analyse_far.1.start_ref = bf16[12,24,2048]{2,1,0:T(8,128)(2,1)} custom-call(s32[1]{0:T(128)} %bitcast.2.me_ref, f32[96,96]{1,0:T(8,128)S(1)} %get-tuple-element.24.w_ref, bf16[6,24,512]{2,1,0:T(8,128)(2,1)S(1)} %get-tuple-element.31.near_ref, bf16[12,24,2048]{2,1,0:T(8,128)(2,1)S(1)} %bitcast.15, bf16[26,24,512]{2,1,0:T(8,128)(2,1)S(1)} %collective-permute-done.3.b1, ...), custom_call_target="tpu_custom_call" | custom-call | tf_op jit(solution)/shard_map/analyse_far/pallas_call | solution.py:300
  51.5 2.5 %collective-permute-done.6.c1 = bf16[6,24,512]{2,1,0:T(8,128)(2,1)S(1)} collective-permute-done((bf16[6,24,512]{2,1,0:T(8,128)(2,1)S(1)}, bf16[6,24,512]{2,1,0:T(8,128)(2,1)S(1)}, u32[]{:S(2)}, u32[]{:S(2)}) %collective-permute-start.6) | collective-permute-done | bytes 147488 | tf_op jit(solution)/shard_map/ppermute | solution.py:345
  53.9 2.5 %collective-permute-done.7.c2 = bf16[6,24,512]{2,1,0:T(8,128)(2,1)S(1)} collective-permute-done((bf16[6,24,512]{2,1,0:T(8,128)(2,1)S(1)}, bf16[6,24,512]{2,1,0:T(8,128)(2,1)S(1)}, u32[]{:S(2)}, u32[]{:S(2)}) %collective-permute-start.7) | collective-permute-done | bytes 147488 | tf_op jit(solution)/shard_map/ppermute | solution.py:345
  56.5 0.2 collective-permute-done.8.c3
  56.6 0.8 %place.1 = bf16[12,24,2048]{2,1,0:T(8,128)(2,1)} custom-call(s32[1]{0:T(128)} %bitcast.2.me_ref, bf16[6,24,512]{2,1,0:T(8,128)(2,1)S(1)} %collective-permute-done.6.c1, bf16[6,24,512]{2,1,0:T(8,128)(2,1)S(1)} %collective-permute-done.7.c2, bf16[6,24,512]{2,1,0:T(8,128)(2,1)S(1)} %collective-permute-done.8.c3, ...), custom_call_target="tpu_custom_call", output_to_operand_aliasing={{}: (4, {})} | custom-call | tf_op jit(solution)/shard_map/place/pallas_call | solution.py:328
  (24 shorter events, 0.2 us)
Async XLA Ops:
  0.6 1.3 %copy-start = (bf16[24,12,2048]{2,0,1:T(8,128)(2,1)S(1)}, bf16[24,12,2048]{2,0,1:T(8,128)(2,1)}, u32[]{:S(2)}) copy-start(bf16[24,12,2048]{2,0,1:T(8,128)(2,1)} %param.7) | copy-start | bytes 3538948
  1.9 9.6 %copy-start.4 = (f32[12,1,128]{2,1,0:T(1,128)S(1)}, f32[12,1,128]{2,1,0:T(1,128)}, u32[]{:S(2)}) copy-start(f32[12,1,128]{2,1,0:T(1,128)} %param.9) | copy-start | bytes 18436
  1.9 9.6 %copy-start.5 = (f32[12,1,128]{2,1,0:T(1,128)S(1)}, f32[12,1,128]{2,1,0:T(1,128)}, u32[]{:S(2)}) copy-start(f32[12,1,128]{2,1,0:T(1,128)} %param.8) | copy-start | bytes 18436
  1.9 9.6 %copy-start.6 = (s32[12,1,2]{0,2,1:T(2,128)S(1)}, s32[12,1,2]{0,2,1:T(2,128)}, u32[]{:S(2)}) copy-start(s32[12,1,2]{0,2,1:T(2,128)} %param.11) | copy-start | bytes 292
  1.9 11.8 %copy-start.2 = (bf16[12,1,2,128,128]{4,3,2,1,0:T(8,128)(2,1)S(1)}, bf16[12,1,2,128,128]{4,3,2,1,0:T(8,128)(2,1)}, u32[]{:S(2)}) copy-start(bf16[12,1,2,128,128]{4,3,2,1,0:T(8,128)(2,1)} %param.10) | copy-start | bytes 2359300
  2.0 9.7 %collective-permute-start = (bf16[4,24,512]{2,1,0:T(8,128)(2,1)S(1)}, bf16[4,24,512]{2,1,0:T(8,128)(2,1)S(1)}, u32[]{:S(2)}, u32[]{:S(2)}) collective-permute-start(bf16[4,24,512]{2,1,0:T(8,128)(2,1)S(1)} %get-tuple-element.21), channel_id=1, source_target_pairs={{0,32},{32,64},{64,96},{96,0},{1,33},{33,65},{65,97},{97,1},{2,34}... | collective-permute-start | bytes 294920 | tf_op jit(solution)/shard_map/ppermute | solution.py:345
  3.8 9.9 %collective-permute-start.1 = (bf16[4,24,512]{2,1,0:T(8,128)(2,1)S(1)}, bf16[4,24,512]{2,1,0:T(8,128)(2,1)S(1)}, u32[]{:S(2)}, u32[]{:S(2)}) collective-permute-start(bf16[4,24,512]{2,1,0:T(8,128)(2,1)S(1)} %get-tuple-element.22), channel_id=1, source_target_pairs={{0,64},{32,96},{64,0},{96,32},{1,65},{33,97},{65,1},{97,33},{2,66}... | collective-permute-start | bytes 294920 | tf_op jit(solution)/shard_map/ppermute | solution.py:345
  6.7 7.0 %collective-permute-start.2 = (bf16[4,24,512]{2,1,0:T(8,128)(2,1)S(1)}, bf16[4,24,512]{2,1,0:T(8,128)(2,1)S(1)}, u32[]{:S(2)}, u32[]{:S(2)}) collective-permute-start(bf16[4,24,512]{2,1,0:T(8,128)(2,1)S(1)} %get-tuple-element.23), channel_id=1, source_target_pairs={{0,96},{32,0},{64,32},{96,64},{1,97},{33,1},{65,33},{97,65},{2,98}... | collective-permute-start | bytes 294920 | tf_op jit(solution)/shard_map/ppermute | solution.py:345
  9.2 0.8 %copy-start.3 = (bf16[26,24,512]{2,1,0:T(8,128)(2,1)}, bf16[26,24,512]{2,1,0:T(8,128)(2,1)S(1)}, u32[]{:S(2)}) copy-start(bf16[26,24,512]{2,1,0:T(8,128)(2,1)S(1)} %get-tuple-element.27) | copy-start | bytes 1916932
  10.0 35.8 %collective-permute-start.3 = (bf16[26,24,512]{2,1,0:T(8,128)(2,1)}, bf16[26,24,512]{2,1,0:T(8,128)(2,1)S(1)}, u32[]{:S(2)}, u32[]{:S(2)}) collective-permute-start(bf16[26,24,512]{2,1,0:T(8,128)(2,1)} %get-tuple-element.25), channel_id=1, source_target_pairs={{0,32},{32,64},{64,96},{96,0},{1,33},{33,65},{65,97},{97,1},{2,34}... | collective-permute-start | bytes 1916936 | tf_op jit(solution)/shard_map/ppermute | solution.py:345
  10.7 35.1 %collective-permute-start.4 = (bf16[26,24,512]{2,1,0:T(8,128)(2,1)}, bf16[26,24,512]{2,1,0:T(8,128)(2,1)S(1)}, u32[]{:S(2)}, u32[]{:S(2)}) collective-permute-start(bf16[26,24,512]{2,1,0:T(8,128)(2,1)} %get-tuple-element.26), channel_id=1, source_target_pairs={{0,64},{32,96},{64,0},{96,32},{1,65},{33,97},{65,1},{97,33},{2,66}... | collective-permute-start | bytes 1916936 | tf_op jit(solution)/shard_map/ppermute | solution.py:345
  11.7 34.1 %collective-permute-start.5 = (bf16[26,24,512]{2,1,0:T(8,128)(2,1)}, bf16[26,24,512]{2,1,0:T(8,128)(2,1)S(1)}, u32[]{:S(2)}, u32[]{:S(2)}) collective-permute-start(bf16[26,24,512]{2,1,0:T(8,128)(2,1)} %copy-done.3), channel_id=1, source_target_pairs={{0,96},{32,0},{64,32},{96,64},{1,97},{33,1},{65,33},{97,65},{2,98}... | collective-permute-start | bytes 1916936 | tf_op jit(solution)/shard_map/ppermute | solution.py:345
  43.7 2.2 %copy-start.1 = (bf16[24,12,2048]{2,0,1:T(8,128)(2,1)S(1)}, bf16[24,12,2048]{2,0,1:T(8,128)(2,1)}, u32[]{:S(2)}) copy-start(bf16[24,12,2048]{2,0,1:T(8,128)(2,1)} %param.7) | copy-start | bytes 3538948
  46.3 7.6 %collective-permute-start.6 = (bf16[6,24,512]{2,1,0:T(8,128)(2,1)S(1)}, bf16[6,24,512]{2,1,0:T(8,128)(2,1)S(1)}, u32[]{:S(2)}, u32[]{:S(2)}) collective-permute-start(bf16[6,24,512]{2,1,0:T(8,128)(2,1)S(1)} %get-tuple-element.28), channel_id=1, source_target_pairs={{0,32},{32,64},{64,96},{96,0},{1,33},{33,65},{65,97},{97,1},{2,34}... | collective-permute-start | bytes 442376 | tf_op jit(solution)/shard_map/ppermute | solution.py:345
  46.9 9.5 %collective-permute-start.7 = (bf16[6,24,512]{2,1,0:T(8,128)(2,1)S(1)}, bf16[6,24,512]{2,1,0:T(8,128)(2,1)S(1)}, u32[]{:S(2)}, u32[]{:S(2)}) collective-permute-start(bf16[6,24,512]{2,1,0:T(8,128)(2,1)S(1)} %get-tuple-element.29), channel_id=1, source_target_pairs={{0,64},{32,96},{64,0},{96,32},{1,65},{33,97},{65,1},{97,33},{2,66}... | collective-permute-start | bytes 442376 | tf_op jit(solution)/shard_map/ppermute | solution.py:345
  50.0 6.6 %collective-permute-start.8 = (bf16[6,24,512]{2,1,0:T(8,128)(2,1)S(1)}, bf16[6,24,512]{2,1,0:T(8,128)(2,1)S(1)}, u32[]{:S(2)}, u32[]{:S(2)}) collective-permute-start(bf16[6,24,512]{2,1,0:T(8,128)(2,1)S(1)} %get-tuple-element.30), channel_id=1, source_target_pairs={{0,96},{32,0},{64,32},{96,64},{1,97},{33,1},{65,33},{97,65},{2,98}... | collective-permute-start | bytes 442376 | tf_op jit(solution)/shard_map/ppermute | solution.py:345

commit v6 on v5

--- a/solution.py
+++ b/solution.py
@@ -125,31 +125,38 @@
     return gram, projected
 
 
-def observe_kernel(me_ref, slots_ref, c0, c1, c2, c3, op_ref, y_ref, var_ref, out_ref, state, spread, scaled):
+def split(a):
+    high = a.astype(jnp.bfloat16)
+    return high, (a - high.astype(jnp.float32)).astype(jnp.bfloat16)
+
+
+def dot_rows(a, b):
+    return lax.dot_general(a, b, (((1,), (1,)), ((), ())), preferred_element_type=jnp.float32)
+
+
+def observe_kernel(me_ref, slots_ref, c0, c1, c2, c3, op_ref, y_ref, var_ref, out_ref, state):
     me = me_ref[0]
     for s, chunk in enumerate((c0, c1, c2, c3)):
         rows = pl.ds(pl.multiple_of(group_from(me, s) * MEMBERS, 8), MEMBERS)
         for v in range(VOBS):
             for c in range(TILE // 128):
                 state[v * (TILE // 128) + c, rows, :] = chunk[v, :, c * 128 : (c + 1) * 128].astype(jnp.float32)
-    spread[K:, :] = jnp.zeros((128 - K, BLOCKS * 128), jnp.float32)
+    spread, scaled = [], []
+    projected = jnp.zeros((K, 128), jnp.float32)
     for b in range(BLOCKS):
-        pred = jnp.zeros((K, 128), jnp.float32)
-        for j in range(NNZ):
-            part = state[slots_ref[b * NNZ + j]].astype(jnp.bfloat16)
-            pred += lax.dot_general(
-                part, op_ref[b, j], (((1,), (1,)), ((), ())), preferred_element_type=jnp.float32
-            )
+        picked = [state[slots_ref[b * NNZ + j]].astype(jnp.bfloat16) for j in range(NNZ)]
+        mapping = jnp.concatenate([op_ref[b, j] for j in range(NNZ)], axis=1)
+        pred = dot_rows(jnp.concatenate(picked, axis=1), mapping)
         mean = jnp.sum(pred, axis=0, keepdims=True) * (1.0 / K)
-        dev = pred - mean
-        lanes = pl.ds(b * 128, 128)
-        spread[:K, lanes] = dev
-        spread[K : K + 1, lanes] = y_ref[b : b + 1, :] - mean
-        scaled[:, lanes] = dev / var_ref[b : b + 1, :]
-    gram = lax.dot_general(
-        scaled[...], spread[...], (((1,), (1,)), ((), ())), precision=EXACT, preferred_element_type=jnp.float32
-    )
-    out_ref[...] = fold(gram)
+        spread.append(pred - mean)
+        scaled.append(spread[-1] * (1.0 / var_ref[b : b + 1, :]))
+        projected += scaled[-1] * (y_ref[b : b + 1, :] - mean)
+    high, low = split(jnp.concatenate(scaled, axis=1))
+    spread_high, spread_low = split(jnp.concatenate(spread, axis=1))
+    both = dot_rows(jnp.concatenate([high, low], axis=0), spread_high)
+    gram = both[:K] + both[K:] + dot_rows(high, spread_low)
+    projected = jnp.sum(projected, axis=1, keepdims=True)
+    out_ref[...] = fold(jnp.concatenate([gram, projected, jnp.zeros((K, 127 - K), jnp.float32)], axis=1))
 
 
 def observe(me, slots, chunks, op, values, variances):
@@ -158,19 +165,10 @@
         out_shape=jax.ShapeDtypeStruct((HALF, 128), jnp.float32),
         in_specs=[SMEM, SMEM] + [VMEM] * 7,
         out_specs=VMEM,
-        scratch_shapes=[
-            pltpu.VMEM((VOBS * TILE // 128, K, 128), jnp.float32),
-            pltpu.VMEM((128, BLOCKS * 128), jnp.float32),
-            pltpu.VMEM((K, BLOCKS * 128), jnp.float32),
-        ],
+        scratch_shapes=[pltpu.VMEM((VOBS * TILE // 128, K, 128), jnp.float32)],
         compiler_params=ROOM,
         name="observe",
     )(me, slots, *chunks, op, values, variances)
-
-
-def split(a):
-    high = a.astype(jnp.bfloat16)
-    return high, (a - high.astype(jnp.float32)).astype(jnp.bfloat16)
 
 
 def fine_dot(a, b):
@@ -200,7 +198,7 @@
     )(parts)
 
 
-def transform_kernel(parts_ref, weights_ref, again_ref):
+def transform_kernel(parts_ref, weights_ref):
     folded = parts_ref[...]
     gram, projected = unfold(folded)
     row = lax.broadcasted_iota(jnp.int32, (K, K), 0)
@@ -219,17 +217,15 @@
     inverse_root = inverse / jnp.sqrt(frob)
     halfway = jnp.sum(inverse_root * projected, axis=0, keepdims=True)
     mean_shift = jnp.sum(inverse_root * halfway, axis=1, keepdims=True)
-    weights = mean_shift + (K - 1.0) ** 0.5 * inverse_root
-    weights_ref[...] = weights
-    again_ref[...] = weights
+    weights_ref[...] = mean_shift + (K - 1.0) ** 0.5 * inverse_root
 
 
 def transform(parts):
     return pl.pallas_call(
         transform_kernel,
-        out_shape=[jax.ShapeDtypeStruct((K, K), jnp.float32)] * 2,
+        out_shape=jax.ShapeDtypeStruct((K, K), jnp.float32),
         in_specs=[VMEM],
-        out_specs=[VMEM] * 2,
+        out_specs=VMEM,
         compiler_params=ROOM,
         cost_estimate=pl.CostEstimate(flops=COST, bytes_accessed=0, transcendentals=0),
         name="transform",
@@ -278,11 +274,15 @@
     )(me, weights, prior, *observed, *bulk)
 
 
-def far_kernel(me_ref, w_ref, near_ref, prior_ref, b1, b2, b3, out_ref, turned, result, sems):
+def far_kernel(me_ref, w_ref, near_ref, prior_ref, b1, b2, b3, out_ref, weights_ref, turned, result, sems):
     me = me_ref[0]
     cells = pl.ds(pl.multiple_of(me * TILE, TILE), TILE)
-    copies = [pltpu.make_async_copy(near_ref, out_ref.at[pl.ds(0, NEAR), :, cells], sems.at[0])]
-    copies[0].start()
+    copies = [
+        pltpu.make_async_copy(near_ref, out_ref.at[pl.ds(0, NEAR), :, cells], sems.at[0]),
+        pltpu.make_async_copy(w_ref, weights_ref, sems.at[1]),
+    ]
+    for copy in copies:
+        copy.start()
     coeffs, keep = coefficients(me, w_ref, turned)
     for v in range(FAR):
         for c in range(GROUPS):
@@ -290,7 +290,7 @@
             parts = [prior_ref[NEAR + v, :, lanes]] + [ref[NEXT + c * FAR + v] for ref in (b1, b2, b3)]
             mixed = mix(coeffs[:MEMBERS], keep[:MEMBERS], parts)
             result[v, :, lanes] = mixed.astype(jnp.bfloat16)
-        copies.append(pltpu.make_async_copy(result.at[v], out_ref.at[NEAR + v], sems.at[1 + v]))
+        copies.append(pltpu.make_async_copy(result.at[v], out_ref.at[NEAR + v], sems.at[2 + v]))
         copies[-1].start()
     for copy in copies:
         copy.wait()
@@ -299,13 +299,16 @@
 def analyse_far(me, weights, near, prior, bulk):
     return pl.pallas_call(
         far_kernel,
-        out_shape=jax.ShapeDtypeStruct((V, MEMBERS, GROUPS * TILE), jnp.bfloat16),
+        out_shape=[
+            jax.ShapeDtypeStruct((V, MEMBERS, GROUPS * TILE), jnp.bfloat16),
+            jax.ShapeDtypeStruct((K, K), jnp.float32),
+        ],
         in_specs=[SMEM] + [VMEM] * 6,
-        out_specs=ANY,
+        out_specs=[ANY, ANY],
         scratch_shapes=[
             pltpu.VMEM((K, K), jnp.float32),
             pltpu.VMEM((FAR, MEMBERS, GROUPS * TILE), jnp.bfloat16),
-            pltpu.SemaphoreType.DMA((1 + FAR,)),
+            pltpu.SemaphoreType.DMA((2 + FAR,)),
         ],
         compiler_params=ROOM,
         name="analyse_far",
@@ -366,11 +369,11 @@
         me, slots.reshape(-1), [packed[0]] + observed, mapping[:, 0], readings[:, 0], error_spread[:, 0]
     )
     folded = lax.cond(member < GROUPS, total, lambda x: x, folded)
-    weights, again = transform(folded)
-    near = analyse_near(me, again, prior, observed, bulk)
+    weights = transform(folded)
+    near = analyse_near(me, weights, prior, observed, bulk)
     arrived = scatter(near[1:])
-    out = place(me, arrived, analyse_far(me, again, near[0], prior, bulk))
-    return (jnp.transpose(out, (1, 0, 2)), weights)
+    out, weights = analyse_far(me, weights, near[0], prior, bulk)
+    return (jnp.transpose(place(me, arrived, out), (1, 0, 2)), weights)
 
 
 def solution(mesh):

time: 57.6 us -> 56.9 us (0.988)
  Pallas kernels: 8.52 us -> 7.01 us
  starting transfers between devices: 13.1 us -> 14 us
    pallas_call x1, Pallas kernels: 2.36 us -> 1.48 us  [observe(): pl.pallas_call(observe_kernel, out_shape=jax.ShapeDtypeStruct((HALF, 128)...]
    ppermute x9, starting transfers between devices: 13.1 us -> 14 us  [scatter(): lax.ppermute(chunk, 'member', ring(s))]
    pallas_call x2, Pallas kernels: 3.59 us -> 2.97 us  [the longest x1 1.53 us: transform(): pl.pallas_call(transform_kernel, out_shape=jax.ShapeDtypeStruct((K, K), j...]
  transfers between devices with their start and end apart: 9 -> 9, of which waited for: 3 -> 2; matrix products, arithmetic and copies ran while one was open for 0% -> 0% of each run, Pallas kernels for 13% -> 10%
where the time goes in v6:
time: 56.9 us; the launch traced here: 56.6 us
  blocking collectives  27.5 us (48%)
  starting transfers between devices  14 us (25%)
  Pallas kernels  7.01 us (12%)
  waiting for transfers between devices  5.01 us (9%)
  local copies, waits for them, and re-layouts  2.3 us (4%)
  between operations  0.77 us (1%)
    all_to_all x2, blocking collectives, exchange(): return lax.all_to_all(copies, axes, 0, 0, tiled=True)  27.5 us
    ppermute x9, starting transfers between devices, scatter(): lax.ppermute(chunk, 'member', ring(s))  14 us
    ppermute x9, waiting for transfers between devices, scatter(): lax.ppermute(chunk, 'member', ring(s))  5.01 us
    unnamed x16, local copies, waits for them, and re-layouts  2.22 us
    pallas_call x1, Pallas kernels, transform(): pl.pallas_call(transform_kernel, out_shape=jax.ShapeDtypeStruct((K, K), j...  1.53 us
    pallas_call x1, Pallas kernels, observe(): pl.pallas_call(observe_kernel, out_shape=jax.ShapeDtypeStruct((HALF, 128)...  1.48 us
    pallas_call x1, Pallas kernels, analyse_far(): pl.pallas_call(far_kernel, out_shape=[jax.ShapeDtypeStruct((V, MEMBERS, G...  1.44 us
    pallas_call x1, Pallas kernels, pack_bulk(): pl.pallas_call(pack_bulk_kernel, out_shape=[jax.ShapeDtypeStruct((NEXT +...  1.16 us
  transfers between devices with their start and end apart: 9, of which 2 were waited for; matrix products, arithmetic and copies ran while one was open for 0% of the time, Pallas kernels for 10%

profile of v6, /device:TPU:0, one launch (start us, length us, event | category | flops | bytes accessed | tf_op | source)
XLA Modules:
  0.0 56.6 jit_solution(11559244915934074201)
XLA Ops:
  0.6 1.3 %copy-done = bf16[24,12,2048]{2,0,1:T(8,128)(2,1)S(1)} copy-done((bf16[24,12,2048]{2,0,1:T(8,128)(2,1)S(1)}, bf16[24,12,2048]{2,0,1:T(8,128)(2,1)}, u32[]{:S(2)}) %copy-start) | copy-done | bytes 1179672
  1.9 0.1 pack.1
  2.0 1.7 %collective-permute-start = (bf16[4,24,512]{2,1,0:T(8,128)(2,1)S(1)}, bf16[4,24,512]{2,1,0:T(8,128)(2,1)S(1)}, u32[]{:S(2)}, u32[]{:S(2)}) collective-permute-start(bf16[4,24,512]{2,1,0:T(8,128)(2,1)S(1)} %get-tuple-element.21), channel_id=1, source_target_pairs={{0,32},{32,64},{64,96},{96,0},{1,33},{33,65},{65,97},{97,1},{2,34}... | collective-permute-start | bytes 294920 | tf_op jit(solution)/shard_map/ppermute | solution.py:348
  3.8 2.9 %collective-permute-start.1 = (bf16[4,24,512]{2,1,0:T(8,128)(2,1)S(1)}, bf16[4,24,512]{2,1,0:T(8,128)(2,1)S(1)}, u32[]{:S(2)}, u32[]{:S(2)}) collective-permute-start(bf16[4,24,512]{2,1,0:T(8,128)(2,1)S(1)} %get-tuple-element.22), channel_id=1, source_target_pairs={{0,64},{32,96},{64,0},{96,32},{1,65},{33,97},{65,1},{97,33},{2,66}... | collective-permute-start | bytes 294920 | tf_op jit(solution)/shard_map/ppermute | solution.py:348
  6.7 1.3 %collective-permute-start.2 = (bf16[4,24,512]{2,1,0:T(8,128)(2,1)S(1)}, bf16[4,24,512]{2,1,0:T(8,128)(2,1)S(1)}, u32[]{:S(2)}, u32[]{:S(2)}) collective-permute-start(bf16[4,24,512]{2,1,0:T(8,128)(2,1)S(1)} %get-tuple-element.23), channel_id=1, source_target_pairs={{0,96},{32,0},{64,32},{96,64},{1,97},{33,1},{65,33},{97,65},{2,98}... | collective-permute-start | bytes 294920 | tf_op jit(solution)/shard_map/ppermute | solution.py:348
  8.0 1.2 %pack_bulk.1 = (bf16[26,24,512]{2,1,0:T(8,128)(2,1)}, bf16[26,24,512]{2,1,0:T(8,128)(2,1)}, bf16[26,24,512]{2,1,0:T(8,128)(2,1)S(1)}) custom-call(s32[1]{0:T(128)} %bitcast.2.me_ref, bf16[12,24,2048]{2,1,0:T(8,128)(2,1)S(1)} %bitcast.13, bf16[4,24,512]{2,1,0:T(8,128)(2,1)S(1)} %get-tuple-element.20.c0.after_ref), custom_call_target="tpu_custom_call" | custom-call | tf_op jit(solution)/shard_map/pack_bulk/pallas_call | solution.py:86
  9.2 0.8 %copy-done.3 = bf16[26,24,512]{2,1,0:T(8,128)(2,1)} copy-done((bf16[26,24,512]{2,1,0:T(8,128)(2,1)}, bf16[26,24,512]{2,1,0:T(8,128)(2,1)S(1)}, u32[]{:S(2)}) %copy-start.3) | copy-done | bytes 639000
  10.0 0.7 %collective-permute-start.3 = (bf16[26,24,512]{2,1,0:T(8,128)(2,1)}, bf16[26,24,512]{2,1,0:T(8,128)(2,1)S(1)}, u32[]{:S(2)}, u32[]{:S(2)}) collective-permute-start(bf16[26,24,512]{2,1,0:T(8,128)(2,1)} %get-tuple-element.24), channel_id=1, source_target_pairs={{0,32},{32,64},{64,96},{96,0},{1,33},{33,65},{65,97},{97,1},{2,34}... | collective-permute-start | bytes 1916936 | tf_op jit(solution)/shard_map/ppermute | solution.py:348
  10.7 0.8 %collective-permute-start.4 = (bf16[26,24,512]{2,1,0:T(8,128)(2,1)}, bf16[26,24,512]{2,1,0:T(8,128)(2,1)S(1)}, u32[]{:S(2)}, u32[]{:S(2)}) collective-permute-start(bf16[26,24,512]{2,1,0:T(8,128)(2,1)} %get-tuple-element.25), channel_id=1, source_target_pairs={{0,64},{32,96},{64,0},{96,32},{1,65},{33,97},{65,1},{97,33},{2,66}... | collective-permute-start | bytes 1916936 | tf_op jit(solution)/shard_map/ppermute | solution.py:348
  11.5 0.1 copy.9
  11.6 0.1 reshape.11.slots_ref
  11.7 2.0 %collective-permute-start.5 = (bf16[26,24,512]{2,1,0:T(8,128)(2,1)}, bf16[26,24,512]{2,1,0:T(8,128)(2,1)S(1)}, u32[]{:S(2)}, u32[]{:S(2)}) collective-permute-start(bf16[26,24,512]{2,1,0:T(8,128)(2,1)} %copy-done.3), channel_id=1, source_target_pairs={{0,96},{32,0},{64,32},{96,64},{1,97},{33,1},{65,33},{97,65},{2,98}... | collective-permute-start | bytes 1916936 | tf_op jit(solution)/shard_map/ppermute | solution.py:348
  13.7 1.5 %observe.1 = f32[48,128]{1,0:T(8,128)S(1)} custom-call(s32[1]{0:T(128)} %bitcast.2.me_ref, s32[24]{0:T(128)S(1)} %reshape.11.slots_ref, bf16[4,24,512]{2,1,0:T(8,128)(2,1)S(1)} %get-tuple-element.20.c0.after_ref, bf16[4,24,512]{2,1,0:T(8,128)(2,1)S(1)} %collective-permute-done.c1.o1, bf16[4,24,512]{2,1,0:T(8,128)(2,1)S(1)} %collective-permute-done.1.c2.o2, ...), custom_call_target="tpu_custom_call" | custom-call | tf_op jit(solution)/shard_map/observe/pallas_call | solution.py:163
  15.2 27.6 %conditional.1 = (f32[48,128]{1,0:T(8,128)S(1)}) conditional(s32[]{:T(128)} %convert_element_type.3, f32[48,128]{1,0:T(8,128)S(1)} %observe.1, f32[48,128]{1,0:T(8,128)S(1)} %observe.1), branch_computations={%region_0.0_spmd, %region_1.0_spmd} | conditional | bytes 1179656 | solution.py:371
  15.2 16.8 %all_to_all.8.parts_ref = f32[16,48,128]{2,1,0:T(8,128)S(1)} all-to-all(f32[16,48,128]{2,1,0:T(8,128)S(1)} %spread_sum.3), channel_id=1, replica_groups=mesh['member'=4,'x'=4,'z'=4,'core'=2] {'x','z'}, dimensions={0} | all-to-all | bytes 786432 | tf_op jit(solution)/shard_map/cond/branch_1_fun/all_to_all | solution.py:352
  32.1 10.7 %all_to_all.9.parts_ref = f32[8,48,128]{2,1,0:T(8,128)S(1)} all-to-all(f32[8,48,128]{2,1,0:T(8,128)S(1)} %spread_sum.4), channel_id=1, replica_groups=mesh['member'=4,'x'=4,'z'=4,'core'=2] {'member','core'}, dimensions={0} | all-to-all | bytes 393216 | tf_op jit(solution)/shard_map/cond/branch_1_fun/all_to_all | solution.py:352
  42.8 1.5 %transform.1.w_ref = f32[96,96]{1,0:T(8,128)S(1)} custom-call(f32[48,128]{1,0:T(8,128)S(1)} %get-tuple-element.35.parts_ref), custom_call_target="tpu_custom_call" | custom-call | flops 40000000000 | tf_op jit(solution)/shard_map/transform/pallas_call | solution.py:224
  44.4 0.4 analyse_near.1
  44.8 0.9 %collective-permute-start.6 = (bf16[6,24,512]{2,1,0:T(8,128)(2,1)S(1)}, bf16[6,24,512]{2,1,0:T(8,128)(2,1)S(1)}, u32[]{:S(2)}, u32[]{:S(2)}) collective-permute-start(bf16[6,24,512]{2,1,0:T(8,128)(2,1)S(1)} %get-tuple-element.27), channel_id=1, source_target_pairs={{0,32},{32,64},{64,96},{96,0},{1,33},{33,65},{65,97},{97,1},{2,34}... | collective-permute-start | bytes 442376 | tf_op jit(solution)/shard_map/ppermute | solution.py:348
  45.7 3.7 %collective-permute-start.7 = (bf16[6,24,512]{2,1,0:T(8,128)(2,1)S(1)}, bf16[6,24,512]{2,1,0:T(8,128)(2,1)S(1)}, u32[]{:S(2)}, u32[]{:S(2)}) collective-permute-start(bf16[6,24,512]{2,1,0:T(8,128)(2,1)S(1)} %get-tuple-element.28), channel_id=1, source_target_pairs={{0,64},{32,96},{64,0},{96,32},{1,65},{33,97},{65,1},{97,33},{2,66}... | collective-permute-start | bytes 442376 | tf_op jit(solution)/shard_map/ppermute | solution.py:348
  49.4 1.4 %analyse_far.1 = (bf16[12,24,2048]{2,1,0:T(8,128)(2,1)}, f32[96,96]{1,0:T(8,128)}) custom-call(s32[1]{0:T(128)} %bitcast.2.me_ref, f32[96,96]{1,0:T(8,128)S(1)} %transform.1.w_ref, bf16[6,24,512]{2,1,0:T(8,128)(2,1)S(1)} %get-tuple-element.30.near_ref, bf16[12,24,2048]{2,1,0:T(8,128)(2,1)S(1)} %bitcast.15, ...), custom_call_target="tpu_custom_call" | custom-call | tf_op jit(solution)/shard_map/analyse_far/pallas_call | solution.py:300
  50.9 1.0 %collective-permute-done.6.c1 = bf16[6,24,512]{2,1,0:T(8,128)(2,1)S(1)} collective-permute-done((bf16[6,24,512]{2,1,0:T(8,128)(2,1)S(1)}, bf16[6,24,512]{2,1,0:T(8,128)(2,1)S(1)}, u32[]{:S(2)}, u32[]{:S(2)}) %collective-permute-start.6) | collective-permute-done | bytes 147488 | tf_op jit(solution)/shard_map/ppermute | solution.py:348
  51.9 4.0 %collective-permute-done.7.c2 = bf16[6,24,512]{2,1,0:T(8,128)(2,1)S(1)} collective-permute-done((bf16[6,24,512]{2,1,0:T(8,128)(2,1)S(1)}, bf16[6,24,512]{2,1,0:T(8,128)(2,1)S(1)}, u32[]{:S(2)}, u32[]{:S(2)}) %collective-permute-start.7) | collective-permute-done | bytes 147488 | tf_op jit(solution)/shard_map/ppermute | solution.py:348
  55.9 0.8 %place.1 = bf16[12,24,2048]{2,1,0:T(8,128)(2,1)} custom-call(s32[1]{0:T(128)} %bitcast.2.me_ref, bf16[6,24,512]{2,1,0:T(8,128)(2,1)S(1)} %collective-permute-done.6.c1, bf16[6,24,512]{2,1,0:T(8,128)(2,1)S(1)} %collective-permute-done.7.c2, bf16[6,24,512]{2,1,0:T(8,128)(2,1)S(1)} %collective-permute-done.8.c3, ...), custom_call_target="tpu_custom_call", output_to_operand_aliasing={{}: (4, {})} | custom-call | tf_op jit(solution)/shard_map/place/pallas_call | solution.py:331
  (24 shorter events, 0.1 us)
Async XLA Ops:
  0.6 1.3 %copy-start = (bf16[24,12,2048]{2,0,1:T(8,128)(2,1)S(1)}, bf16[24,12,2048]{2,0,1:T(8,128)(2,1)}, u32[]{:S(2)}) copy-start(bf16[24,12,2048]{2,0,1:T(8,128)(2,1)} %param.7) | copy-start | bytes 3538948
  1.9 9.6 %copy-start.4 = (f32[12,1,128]{2,1,0:T(1,128)S(1)}, f32[12,1,128]{2,1,0:T(1,128)}, u32[]{:S(2)}) copy-start(f32[12,1,128]{2,1,0:T(1,128)} %param.9) | copy-start | bytes 18436
  1.9 9.6 %copy-start.5 = (f32[12,1,128]{2,1,0:T(1,128)S(1)}, f32[12,1,128]{2,1,0:T(1,128)}, u32[]{:S(2)}) copy-start(f32[12,1,128]{2,1,0:T(1,128)} %param.8) | copy-start | bytes 18436
  1.9 9.6 %copy-start.6 = (s32[12,1,2]{0,2,1:T(2,128)S(1)}, s32[12,1,2]{0,2,1:T(2,128)}, u32[]{:S(2)}) copy-start(s32[12,1,2]{0,2,1:T(2,128)} %param.11) | copy-start | bytes 292
  1.9 11.8 %copy-start.2 = (bf16[12,1,2,128,128]{4,3,2,1,0:T(8,128)(2,1)S(1)}, bf16[12,1,2,128,128]{4,3,2,1,0:T(8,128)(2,1)}, u32[]{:S(2)}) copy-start(bf16[12,1,2,128,128]{4,3,2,1,0:T(8,128)(2,1)} %param.10) | copy-start | bytes 2359300
  2.0 9.7 %collective-permute-start = (bf16[4,24,512]{2,1,0:T(8,128)(2,1)S(1)}, bf16[4,24,512]{2,1,0:T(8,128)(2,1)S(1)}, u32[]{:S(2)}, u32[]{:S(2)}) collective-permute-start(bf16[4,24,512]{2,1,0:T(8,128)(2,1)S(1)} %get-tuple-element.21), channel_id=1, source_target_pairs={{0,32},{32,64},{64,96},{96,0},{1,33},{33,65},{65,97},{97,1},{2,34}... | collective-permute-start | bytes 294920 | tf_op jit(solution)/shard_map/ppermute | solution.py:348
  3.8 9.9 %collective-permute-start.1 = (bf16[4,24,512]{2,1,0:T(8,128)(2,1)S(1)}, bf16[4,24,512]{2,1,0:T(8,128)(2,1)S(1)}, u32[]{:S(2)}, u32[]{:S(2)}) collective-permute-start(bf16[4,24,512]{2,1,0:T(8,128)(2,1)S(1)} %get-tuple-element.22), channel_id=1, source_target_pairs={{0,64},{32,96},{64,0},{96,32},{1,65},{33,97},{65,1},{97,33},{2,66}... | collective-permute-start | bytes 294920 | tf_op jit(solution)/shard_map/ppermute | solution.py:348
  6.7 7.0 %collective-permute-start.2 = (bf16[4,24,512]{2,1,0:T(8,128)(2,1)S(1)}, bf16[4,24,512]{2,1,0:T(8,128)(2,1)S(1)}, u32[]{:S(2)}, u32[]{:S(2)}) collective-permute-start(bf16[4,24,512]{2,1,0:T(8,128)(2,1)S(1)} %get-tuple-element.23), channel_id=1, source_target_pairs={{0,96},{32,0},{64,32},{96,64},{1,97},{33,1},{65,33},{97,65},{2,98}... | collective-permute-start | bytes 294920 | tf_op jit(solution)/shard_map/ppermute | solution.py:348
  9.2 0.8 %copy-start.3 = (bf16[26,24,512]{2,1,0:T(8,128)(2,1)}, bf16[26,24,512]{2,1,0:T(8,128)(2,1)S(1)}, u32[]{:S(2)}) copy-start(bf16[26,24,512]{2,1,0:T(8,128)(2,1)S(1)} %get-tuple-element.26) | copy-start | bytes 1916932
  10.0 34.3 %collective-permute-start.3 = (bf16[26,24,512]{2,1,0:T(8,128)(2,1)}, bf16[26,24,512]{2,1,0:T(8,128)(2,1)S(1)}, u32[]{:S(2)}, u32[]{:S(2)}) collective-permute-start(bf16[26,24,512]{2,1,0:T(8,128)(2,1)} %get-tuple-element.24), channel_id=1, source_target_pairs={{0,32},{32,64},{64,96},{96,0},{1,33},{33,65},{65,97},{97,1},{2,34}... | collective-permute-start | bytes 1916936 | tf_op jit(solution)/shard_map/ppermute | solution.py:348
  10.7 33.6 %collective-permute-start.4 = (bf16[26,24,512]{2,1,0:T(8,128)(2,1)}, bf16[26,24,512]{2,1,0:T(8,128)(2,1)S(1)}, u32[]{:S(2)}, u32[]{:S(2)}) collective-permute-start(bf16[26,24,512]{2,1,0:T(8,128)(2,1)} %get-tuple-element.25), channel_id=1, source_target_pairs={{0,64},{32,96},{64,0},{96,32},{1,65},{33,97},{65,1},{97,33},{2,66}... | collective-permute-start | bytes 1916936 | tf_op jit(solution)/shard_map/ppermute | solution.py:348
  11.7 32.6 %collective-permute-start.5 = (bf16[26,24,512]{2,1,0:T(8,128)(2,1)}, bf16[26,24,512]{2,1,0:T(8,128)(2,1)S(1)}, u32[]{:S(2)}, u32[]{:S(2)}) collective-permute-start(bf16[26,24,512]{2,1,0:T(8,128)(2,1)} %copy-done.3), channel_id=1, source_target_pairs={{0,96},{32,0},{64,32},{96,64},{1,97},{33,1},{65,33},{97,65},{2,98}... | collective-permute-start | bytes 1916936 | tf_op jit(solution)/shard_map/ppermute | solution.py:348
  42.8 1.6 %copy-start.1 = (bf16[24,12,2048]{2,0,1:T(8,128)(2,1)S(1)}, bf16[24,12,2048]{2,0,1:T(8,128)(2,1)}, u32[]{:S(2)}) copy-start(bf16[24,12,2048]{2,0,1:T(8,128)(2,1)} %param.7) | copy-start | bytes 3538948
  44.8 7.1 %collective-permute-start.6 = (bf16[6,24,512]{2,1,0:T(8,128)(2,1)S(1)}, bf16[6,24,512]{2,1,0:T(8,128)(2,1)S(1)}, u32[]{:S(2)}, u32[]{:S(2)}) collective-permute-start(bf16[6,24,512]{2,1,0:T(8,128)(2,1)S(1)} %get-tuple-element.27), channel_id=1, source_target_pairs={{0,32},{32,64},{64,96},{96,0},{1,33},{33,65},{65,97},{97,1},{2,34}... | collective-permute-start | bytes 442376 | tf_op jit(solution)/shard_map/ppermute | solution.py:348
  45.7 10.2 %collective-permute-start.7 = (bf16[6,24,512]{2,1,0:T(8,128)(2,1)S(1)}, bf16[6,24,512]{2,1,0:T(8,128)(2,1)S(1)}, u32[]{:S(2)}, u32[]{:S(2)}) collective-permute-start(bf16[6,24,512]{2,1,0:T(8,128)(2,1)S(1)} %get-tuple-element.28), channel_id=1, source_target_pairs={{0,64},{32,96},{64,0},{96,32},{1,65},{33,97},{65,1},{97,33},{2,66}... | collective-permute-start | bytes 442376 | tf_op jit(solution)/shard_map/ppermute | solution.py:348
  49.4 6.4 %collective-permute-start.8 = (bf16[6,24,512]{2,1,0:T(8,128)(2,1)S(1)}, bf16[6,24,512]{2,1,0:T(8,128)(2,1)S(1)}, u32[]{:S(2)}, u32[]{:S(2)}) collective-permute-start(bf16[6,24,512]{2,1,0:T(8,128)(2,1)S(1)} %get-tuple-element.29), channel_id=1, source_target_pairs={{0,96},{32,0},{64,32},{96,64},{1,97},{33,1},{65,33},{97,65},{2,98}... | collective-permute-start | bytes 442376 | tf_op jit(solution)/shard_map/ppermute | solution.py:348

commit v7 on v6

--- a/solution.py
+++ b/solution.py
@@ -20,7 +20,7 @@
 HALF = K // 2
 PLANE = 16
 COLUMN = 8
-NEAR = 6
+NEAR = 8
 COST = 40_000_000_000
 FAR = V - NEAR
 NEXT = NEAR - VOBS
@@ -179,18 +179,34 @@
     return small + jnp.dot(a_high, b_high, preferred_element_type=jnp.float32)
 
 
+def narrow(folded):
+    _, lane = indices()
+    high = folded.astype(jnp.bfloat16).astype(jnp.float32)
+    low = pltpu.roll(folded - high, 3, 1)
+    return jnp.where((lane >= K + 3) & (lane < K + 6), low, high).astype(jnp.bfloat16)
+
+
+def widen(total):
+    _, lane = indices()
+    return jnp.where((lane >= K) & (lane < K + 3), total + pltpu.roll(total, 125, 1), total)
+
+
 def spread_kernel(parts_ref, out_ref):
-    total = parts_ref[0]
+    total = parts_ref[0].astype(jnp.float32)
     for part in range(1, parts_ref.shape[0]):
-        total = total + parts_ref[part]
+        total = total + parts_ref[part].astype(jnp.float32)
+    if parts_ref.dtype == jnp.bfloat16:
+        total = widen(total)
+    if out_ref.dtype == jnp.bfloat16:
+        total = narrow(total)
     for copy in range(out_ref.shape[0]):
         out_ref[copy] = total
 
 
-def spread_sum(parts, copies):
+def spread_sum(parts, copies, dtype=jnp.float32):
     return pl.pallas_call(
         spread_kernel,
-        out_shape=jax.ShapeDtypeStruct((copies, HALF, 128), jnp.float32),
+        out_shape=jax.ShapeDtypeStruct((copies, HALF, 128), dtype),
         in_specs=[VMEM],
         out_specs=VMEM,
         compiler_params=ROOM,
@@ -353,7 +369,7 @@
 
 
 def total(folded):
-    copies = exchange(spread_sum(folded[None], PLANE), ("x", "z"))
+    copies = exchange(spread_sum(folded[None], PLANE, jnp.bfloat16), ("x", "z"))
     copies = exchange(spread_sum(copies, COLUMN), ("member", "core"))
     return spread_sum(copies, 1)[0]
 

time: 56.9 us -> 56.6 us (level)
  waiting for transfers between devices: 5.01 us -> 7.92 us
  blocking collectives: 27.5 us -> 26.4 us
  starting transfers between devices: 14 us -> 12.9 us
  local copies, waits for them, and re-layouts: 2.3 us -> 1.47 us
    ppermute x9, waiting for transfers between devices: 5.01 us -> 7.92 us  [scatter(): lax.ppermute(chunk, 'member', ring(s))]
    all_to_all x2, blocking collectives: 27.5 us -> 26.4 us  [exchange(): return lax.all_to_all(copies, axes, 0, 0, tiled=True)]
    ppermute x9, starting transfers between devices: 14 us -> 12.9 us  [scatter(): lax.ppermute(chunk, 'member', ring(s))]
    unnamed x16 -> x14, local copies, waits for them, and re-layouts: 2.22 us -> 1.38 us
where the time goes in v7:
time: 56.6 us; the launch traced here: 56.4 us
  blocking collectives  26.4 us (47%)
  starting transfers between devices  12.9 us (23%)
  waiting for transfers between devices  7.92 us (14%)
  Pallas kernels  6.89 us (12%)
  local copies, waits for them, and re-layouts  1.47 us (3%)
  between operations  0.76 us (1%)
    all_to_all x2, blocking collectives, exchange(): return lax.all_to_all(copies, axes, 0, 0, tiled=True)  26.4 us
    ppermute x9, starting transfers between devices, scatter(): lax.ppermute(chunk, 'member', ring(s))  12.9 us
    ppermute x9, waiting for transfers between devices, scatter(): lax.ppermute(chunk, 'member', ring(s))  7.92 us
    pallas_call x1, Pallas kernels, transform(): pl.pallas_call(transform_kernel, out_shape=jax.ShapeDtypeStruct((K, K), j...  1.53 us
    pallas_call x1, Pallas kernels, observe(): pl.pallas_call(observe_kernel, out_shape=jax.ShapeDtypeStruct((HALF, 128)...  1.48 us
    unnamed x14, local copies, waits for them, and re-layouts  1.38 us
    pallas_call x1, Pallas kernels, analyse_far(): pl.pallas_call(far_kernel, out_shape=[jax.ShapeDtypeStruct((V, MEMBERS, G...  1.18 us
  transfers between devices with their start and end apart: 9, of which 2 were waited for; matrix products, arithmetic and copies ran while one was open for 0% of the time, Pallas kernels for 10%

profile of v7, /device:TPU:0, one launch (start us, length us, event | category | flops | bytes accessed | tf_op | source)
XLA Modules:
  0.0 56.4 jit_solution(12746675002245984538)
XLA Ops:
  0.6 1.3 %copy-done = bf16[24,12,2048]{2,0,1:T(8,128)(2,1)S(1)} copy-done((bf16[24,12,2048]{2,0,1:T(8,128)(2,1)S(1)}, bf16[24,12,2048]{2,0,1:T(8,128)(2,1)}, u32[]{:S(2)}) %copy-start) | copy-done | bytes 1179672
  1.9 0.1 pack.1
  2.0 1.7 %collective-permute-start = (bf16[4,24,512]{2,1,0:T(8,128)(2,1)S(1)}, bf16[4,24,512]{2,1,0:T(8,128)(2,1)S(1)}, u32[]{:S(2)}, u32[]{:S(2)}) collective-permute-start(bf16[4,24,512]{2,1,0:T(8,128)(2,1)S(1)} %get-tuple-element.21), channel_id=1, source_target_pairs={{0,32},{32,64},{64,96},{96,0},{1,33},{33,65},{65,97},{97,1},{2,34}... | collective-permute-start | bytes 294920 | tf_op jit(solution)/shard_map/ppermute | solution.py:364
  3.8 2.9 %collective-permute-start.1 = (bf16[4,24,512]{2,1,0:T(8,128)(2,1)S(1)}, bf16[4,24,512]{2,1,0:T(8,128)(2,1)S(1)}, u32[]{:S(2)}, u32[]{:S(2)}) collective-permute-start(bf16[4,24,512]{2,1,0:T(8,128)(2,1)S(1)} %get-tuple-element.22), channel_id=1, source_target_pairs={{0,64},{32,96},{64,0},{96,32},{1,65},{33,97},{65,1},{97,33},{2,66}... | collective-permute-start | bytes 294920 | tf_op jit(solution)/shard_map/ppermute | solution.py:364
  6.7 1.3 %collective-permute-start.2 = (bf16[4,24,512]{2,1,0:T(8,128)(2,1)S(1)}, bf16[4,24,512]{2,1,0:T(8,128)(2,1)S(1)}, u32[]{:S(2)}, u32[]{:S(2)}) collective-permute-start(bf16[4,24,512]{2,1,0:T(8,128)(2,1)S(1)} %get-tuple-element.23), channel_id=1, source_target_pairs={{0,96},{32,0},{64,32},{96,64},{1,97},{33,1},{65,33},{97,65},{2,98}... | collective-permute-start | bytes 294920 | tf_op jit(solution)/shard_map/ppermute | solution.py:364
  8.0 1.1 %pack_bulk.1 = (bf16[20,24,512]{2,1,0:T(8,128)(2,1)}, bf16[20,24,512]{2,1,0:T(8,128)(2,1)}, bf16[20,24,512]{2,1,0:T(8,128)(2,1)S(1)}) custom-call(s32[1]{0:T(128)} %bitcast.2.me_ref, bf16[12,24,2048]{2,1,0:T(8,128)(2,1)S(1)} %bitcast.13, bf16[4,24,512]{2,1,0:T(8,128)(2,1)S(1)} %get-tuple-element.20.c0.after_ref), custom_call_target="tpu_custom_call" | custom-call | tf_op jit(solution)/shard_map/pack_bulk/pallas_call | solution.py:86
  9.1 0.7 %collective-permute-start.3 = (bf16[20,24,512]{2,1,0:T(8,128)(2,1)}, bf16[20,24,512]{2,1,0:T(8,128)(2,1)S(1)}, u32[]{:S(2)}, u32[]{:S(2)}) collective-permute-start(bf16[20,24,512]{2,1,0:T(8,128)(2,1)} %get-tuple-element.24), channel_id=1, source_target_pairs={{0,32},{32,64},{64,96},{96,0},{1,33},{33,65},{65,97},{97,1},{2,34}... | collective-permute-start | bytes 1474568 | tf_op jit(solution)/shard_map/ppermute | solution.py:364
  9.8 0.8 %collective-permute-start.4 = (bf16[20,24,512]{2,1,0:T(8,128)(2,1)}, bf16[20,24,512]{2,1,0:T(8,128)(2,1)S(1)}, u32[]{:S(2)}, u32[]{:S(2)}) collective-permute-start(bf16[20,24,512]{2,1,0:T(8,128)(2,1)} %get-tuple-element.25), channel_id=1, source_target_pairs={{0,64},{32,96},{64,0},{96,32},{1,65},{33,97},{65,1},{97,33},{2,66}... | collective-permute-start | bytes 1474568 | tf_op jit(solution)/shard_map/ppermute | solution.py:364
  10.6 0.1 copy.9
  10.8 2.0 %collective-permute-start.5 = (bf16[20,24,512]{2,1,0:T(8,128)(2,1)S(1)}, bf16[20,24,512]{2,1,0:T(8,128)(2,1)S(1)}, u32[]{:S(2)}, u32[]{:S(2)}) collective-permute-start(bf16[20,24,512]{2,1,0:T(8,128)(2,1)S(1)} %get-tuple-element.26), channel_id=1, source_target_pairs={{0,96},{32,0},{64,32},{96,64},{1,97},{33,1},{65,33},{97,65},{2,98}... | collective-permute-start | bytes 1474568 | tf_op jit(solution)/shard_map/ppermute | solution.py:364
  12.9 1.5 %observe.1 = f32[48,128]{1,0:T(8,128)S(1)} custom-call(s32[1]{0:T(128)} %bitcast.2.me_ref, s32[24]{0:T(128)S(1)} %reshape.11.slots_ref, bf16[4,24,512]{2,1,0:T(8,128)(2,1)S(1)} %get-tuple-element.20.c0.after_ref, bf16[4,24,512]{2,1,0:T(8,128)(2,1)S(1)} %collective-permute-done.c1.o1, bf16[4,24,512]{2,1,0:T(8,128)(2,1)S(1)} %collective-permute-done.1.c2.o2, ...), custom_call_target="tpu_custom_call" | custom-call | tf_op jit(solution)/shard_map/observe/pallas_call | solution.py:163
  14.4 26.6 %conditional.1 = (f32[48,128]{1,0:T(8,128)S(1)}) conditional(s32[]{:T(128)} %convert_element_type.3, f32[48,128]{1,0:T(8,128)S(1)} %observe.1, f32[48,128]{1,0:T(8,128)S(1)} %observe.1), branch_computations={%region_0.0_spmd, %region_1.0_spmd} | conditional | bytes 786440 | solution.py:387
  14.5 15.8 %all_to_all.8.parts_ref = bf16[16,48,128]{2,1,0:T(8,128)(2,1)S(1)} all-to-all(bf16[16,48,128]{2,1,0:T(8,128)(2,1)S(1)} %spread_sum.3), channel_id=1, replica_groups=mesh['member'=4,'x'=4,'z'=4,'core'=2] {'x','z'}, dimensions={0} | all-to-all | bytes 393216 | tf_op jit(solution)/shard_map/cond/branch_1_fun/all_to_all | solution.py:368
  30.2 0.1 spread_sum.4
  30.3 10.6 %all_to_all.9.parts_ref = f32[8,48,128]{2,1,0:T(8,128)S(1)} all-to-all(f32[8,48,128]{2,1,0:T(8,128)S(1)} %spread_sum.4), channel_id=1, replica_groups=mesh['member'=4,'x'=4,'z'=4,'core'=2] {'member','core'}, dimensions={0} | all-to-all | bytes 393216 | tf_op jit(solution)/shard_map/cond/branch_1_fun/all_to_all | solution.py:368
  41.0 1.5 %transform.1.w_ref = f32[96,96]{1,0:T(8,128)S(1)} custom-call(f32[48,128]{1,0:T(8,128)S(1)} %get-tuple-element.35.parts_ref), custom_call_target="tpu_custom_call" | custom-call | flops 40000000000 | tf_op jit(solution)/shard_map/transform/pallas_call | solution.py:240
  42.6 0.5 analyse_near.1
  43.1 0.6 %collective-permute-start.6 = (bf16[8,24,512]{2,1,0:T(8,128)(2,1)S(1)}, bf16[8,24,512]{2,1,0:T(8,128)(2,1)S(1)}, u32[]{:S(2)}, u32[]{:S(2)}) collective-permute-start(bf16[8,24,512]{2,1,0:T(8,128)(2,1)S(1)} %get-tuple-element.27), channel_id=1, source_target_pairs={{0,32},{32,64},{64,96},{96,0},{1,33},{33,65},{65,97},{97,1},{2,34}... | collective-permute-start | bytes 589832 | tf_op jit(solution)/shard_map/ppermute | solution.py:364
  43.7 2.1 %collective-permute-start.7 = (bf16[8,24,512]{2,1,0:T(8,128)(2,1)S(1)}, bf16[8,24,512]{2,1,0:T(8,128)(2,1)S(1)}, u32[]{:S(2)}, u32[]{:S(2)}) collective-permute-start(bf16[8,24,512]{2,1,0:T(8,128)(2,1)S(1)} %get-tuple-element.28), channel_id=1, source_target_pairs={{0,64},{32,96},{64,0},{96,32},{1,65},{33,97},{65,1},{97,33},{2,66}... | collective-permute-start | bytes 589832 | tf_op jit(solution)/shard_map/ppermute | solution.py:364
  45.7 0.7 %collective-permute-start.8 = (bf16[8,24,512]{2,1,0:T(8,128)(2,1)S(1)}, bf16[8,24,512]{2,1,0:T(8,128)(2,1)S(1)}, u32[]{:S(2)}, u32[]{:S(2)}) collective-permute-start(bf16[8,24,512]{2,1,0:T(8,128)(2,1)S(1)} %get-tuple-element.29), channel_id=1, source_target_pairs={{0,96},{32,0},{64,32},{96,64},{1,97},{33,1},{65,33},{97,65},{2,98}... | collective-permute-start | bytes 589832 | tf_op jit(solution)/shard_map/ppermute | solution.py:364
  46.4 1.2 %analyse_far.1 = (bf16[12,24,2048]{2,1,0:T(8,128)(2,1)}, f32[96,96]{1,0:T(8,128)}) custom-call(s32[1]{0:T(128)} %bitcast.2.me_ref, f32[96,96]{1,0:T(8,128)S(1)} %transform.1.w_ref, bf16[8,24,512]{2,1,0:T(8,128)(2,1)S(1)} %get-tuple-element.30.near_ref, bf16[12,24,2048]{2,1,0:T(8,128)(2,1)S(1)} %bitcast.15, ...), custom_call_target="tpu_custom_call" | custom-call | tf_op jit(solution)/shard_map/analyse_far/pallas_call | solution.py:316
  47.6 7.3 %collective-permute-done.6.c1 = bf16[8,24,512]{2,1,0:T(8,128)(2,1)S(1)} collective-permute-done((bf16[8,24,512]{2,1,0:T(8,128)(2,1)S(1)}, bf16[8,24,512]{2,1,0:T(8,128)(2,1)S(1)}, u32[]{:S(2)}, u32[]{:S(2)}) %collective-permute-start.6) | collective-permute-done | bytes 196640 | tf_op jit(solution)/shard_map/ppermute | solution.py:364
  54.9 0.6 %collective-permute-done.8.c3 = bf16[8,24,512]{2,1,0:T(8,128)(2,1)S(1)} collective-permute-done((bf16[8,24,512]{2,1,0:T(8,128)(2,1)S(1)}, bf16[8,24,512]{2,1,0:T(8,128)(2,1)S(1)}, u32[]{:S(2)}, u32[]{:S(2)}) %collective-permute-start.8) | collective-permute-done | bytes 196640 | tf_op jit(solution)/shard_map/ppermute | solution.py:364
  55.5 0.8 %place.1 = bf16[12,24,2048]{2,1,0:T(8,128)(2,1)} custom-call(s32[1]{0:T(128)} %bitcast.2.me_ref, bf16[8,24,512]{2,1,0:T(8,128)(2,1)S(1)} %collective-permute-done.6.c1, bf16[8,24,512]{2,1,0:T(8,128)(2,1)S(1)} %collective-permute-done.7.c2, bf16[8,24,512]{2,1,0:T(8,128)(2,1)S(1)} %collective-permute-done.8.c3, ...), custom_call_target="tpu_custom_call", output_to_operand_aliasing={{}: (4, {})} | custom-call | tf_op jit(solution)/shard_map/place/pallas_call | solution.py:347
  (22 shorter events, 0.2 us)
Async XLA Ops:
  0.6 1.3 %copy-start = (bf16[24,12,2048]{2,0,1:T(8,128)(2,1)S(1)}, bf16[24,12,2048]{2,0,1:T(8,128)(2,1)}, u32[]{:S(2)}) copy-start(bf16[24,12,2048]{2,0,1:T(8,128)(2,1)} %param.7) | copy-start | bytes 3538948
  1.9 8.7 %copy-start.3 = (f32[12,1,128]{2,1,0:T(1,128)S(1)}, f32[12,1,128]{2,1,0:T(1,128)}, u32[]{:S(2)}) copy-start(f32[12,1,128]{2,1,0:T(1,128)} %param.9) | copy-start | bytes 18436
  1.9 8.7 %copy-start.4 = (f32[12,1,128]{2,1,0:T(1,128)S(1)}, f32[12,1,128]{2,1,0:T(1,128)}, u32[]{:S(2)}) copy-start(f32[12,1,128]{2,1,0:T(1,128)} %param.8) | copy-start | bytes 18436
  1.9 8.7 %copy-start.5 = (s32[12,1,2]{0,2,1:T(2,128)S(1)}, s32[12,1,2]{0,2,1:T(2,128)}, u32[]{:S(2)}) copy-start(s32[12,1,2]{0,2,1:T(2,128)} %param.11) | copy-start | bytes 292
  1.9 11.0 %copy-start.2 = (bf16[12,1,2,128,128]{4,3,2,1,0:T(8,128)(2,1)S(1)}, bf16[12,1,2,128,128]{4,3,2,1,0:T(8,128)(2,1)}, u32[]{:S(2)}) copy-start(bf16[12,1,2,128,128]{4,3,2,1,0:T(8,128)(2,1)} %param.10) | copy-start | bytes 2359300
  2.0 8.8 %collective-permute-start = (bf16[4,24,512]{2,1,0:T(8,128)(2,1)S(1)}, bf16[4,24,512]{2,1,0:T(8,128)(2,1)S(1)}, u32[]{:S(2)}, u32[]{:S(2)}) collective-permute-start(bf16[4,24,512]{2,1,0:T(8,128)(2,1)S(1)} %get-tuple-element.21), channel_id=1, source_target_pairs={{0,32},{32,64},{64,96},{96,0},{1,33},{33,65},{65,97},{97,1},{2,34}... | collective-permute-start | bytes 294920 | tf_op jit(solution)/shard_map/ppermute | solution.py:364
  3.8 9.1 %collective-permute-start.1 = (bf16[4,24,512]{2,1,0:T(8,128)(2,1)S(1)}, bf16[4,24,512]{2,1,0:T(8,128)(2,1)S(1)}, u32[]{:S(2)}, u32[]{:S(2)}) collective-permute-start(bf16[4,24,512]{2,1,0:T(8,128)(2,1)S(1)} %get-tuple-element.22), channel_id=1, source_target_pairs={{0,64},{32,96},{64,0},{96,32},{1,65},{33,97},{65,1},{97,33},{2,66}... | collective-permute-start | bytes 294920 | tf_op jit(solution)/shard_map/ppermute | solution.py:364
  6.7 6.2 %collective-permute-start.2 = (bf16[4,24,512]{2,1,0:T(8,128)(2,1)S(1)}, bf16[4,24,512]{2,1,0:T(8,128)(2,1)S(1)}, u32[]{:S(2)}, u32[]{:S(2)}) collective-permute-start(bf16[4,24,512]{2,1,0:T(8,128)(2,1)S(1)} %get-tuple-element.23), channel_id=1, source_target_pairs={{0,96},{32,0},{64,32},{96,64},{1,97},{33,1},{65,33},{97,65},{2,98}... | collective-permute-start | bytes 294920 | tf_op jit(solution)/shard_map/ppermute | solution.py:364
  9.1 33.4 %collective-permute-start.3 = (bf16[20,24,512]{2,1,0:T(8,128)(2,1)}, bf16[20,24,512]{2,1,0:T(8,128)(2,1)S(1)}, u32[]{:S(2)}, u32[]{:S(2)}) collective-permute-start(bf16[20,24,512]{2,1,0:T(8,128)(2,1)} %get-tuple-element.24), channel_id=1, source_target_pairs={{0,32},{32,64},{64,96},{96,0},{1,33},{33,65},{65,97},{97,1},{2,34}... | collective-permute-start | bytes 1474568 | tf_op jit(solution)/shard_map/ppermute | solution.py:364
  9.8 32.7 %collective-permute-start.4 = (bf16[20,24,512]{2,1,0:T(8,128)(2,1)}, bf16[20,24,512]{2,1,0:T(8,128)(2,1)S(1)}, u32[]{:S(2)}, u32[]{:S(2)}) collective-permute-start(bf16[20,24,512]{2,1,0:T(8,128)(2,1)} %get-tuple-element.25), channel_id=1, source_target_pairs={{0,64},{32,96},{64,0},{96,32},{1,65},{33,97},{65,1},{97,33},{2,66}... | collective-permute-start | bytes 1474568 | tf_op jit(solution)/shard_map/ppermute | solution.py:364
  10.8 31.7 %collective-permute-start.5 = (bf16[20,24,512]{2,1,0:T(8,128)(2,1)S(1)}, bf16[20,24,512]{2,1,0:T(8,128)(2,1)S(1)}, u32[]{:S(2)}, u32[]{:S(2)}) collective-permute-start(bf16[20,24,512]{2,1,0:T(8,128)(2,1)S(1)} %get-tuple-element.26), channel_id=1, source_target_pairs={{0,96},{32,0},{64,32},{96,64},{1,97},{33,1},{65,33},{97,65},{2,98}... | collective-permute-start | bytes 1474568 | tf_op jit(solution)/shard_map/ppermute | solution.py:364
  41.0 1.6 %copy-start.1 = (bf16[24,12,2048]{2,0,1:T(8,128)(2,1)S(1)}, bf16[24,12,2048]{2,0,1:T(8,128)(2,1)}, u32[]{:S(2)}) copy-start(bf16[24,12,2048]{2,0,1:T(8,128)(2,1)} %param.7) | copy-start | bytes 3538948
  43.1 11.9 %collective-permute-start.6 = (bf16[8,24,512]{2,1,0:T(8,128)(2,1)S(1)}, bf16[8,24,512]{2,1,0:T(8,128)(2,1)S(1)}, u32[]{:S(2)}, u32[]{:S(2)}) collective-permute-start(bf16[8,24,512]{2,1,0:T(8,128)(2,1)S(1)} %get-tuple-element.27), channel_id=1, source_target_pairs={{0,32},{32,64},{64,96},{96,0},{1,33},{33,65},{65,97},{97,1},{2,34}... | collective-permute-start | bytes 589832 | tf_op jit(solution)/shard_map/ppermute | solution.py:364
  43.7 11.2 %collective-permute-start.7 = (bf16[8,24,512]{2,1,0:T(8,128)(2,1)S(1)}, bf16[8,24,512]{2,1,0:T(8,128)(2,1)S(1)}, u32[]{:S(2)}, u32[]{:S(2)}) collective-permute-start(bf16[8,24,512]{2,1,0:T(8,128)(2,1)S(1)} %get-tuple-element.28), channel_id=1, source_target_pairs={{0,64},{32,96},{64,0},{96,32},{1,65},{33,97},{65,1},{97,33},{2,66}... | collective-permute-start | bytes 589832 | tf_op jit(solution)/shard_map/ppermute | solution.py:364
  45.7 9.8 %collective-permute-start.8 = (bf16[8,24,512]{2,1,0:T(8,128)(2,1)S(1)}, bf16[8,24,512]{2,1,0:T(8,128)(2,1)S(1)}, u32[]{:S(2)}, u32[]{:S(2)}) collective-permute-start(bf16[8,24,512]{2,1,0:T(8,128)(2,1)S(1)} %get-tuple-element.29), channel_id=1, source_target_pairs={{0,96},{32,0},{64,32},{96,64},{1,97},{33,1},{65,33},{97,65},{2,98}... | collective-permute-start | bytes 589832 | tf_op jit(solution)/shard_map/ppermute | solution.py:364

commit v8 on v7

--- a/solution.py
+++ b/solution.py
@@ -20,7 +20,7 @@
 HALF = K // 2
 PLANE = 16
 COLUMN = 8
-NEAR = 8
+NEAR = 7
 COST = 40_000_000_000
 FAR = V - NEAR
 NEXT = NEAR - VOBS
@@ -144,13 +144,13 @@
     spread, scaled = [], []
     projected = jnp.zeros((K, 128), jnp.float32)
     for b in range(BLOCKS):
-        picked = [state[slots_ref[b * NNZ + j]].astype(jnp.bfloat16) for j in range(NNZ)]
+        picked = [state[slots_ref[j, b]].astype(jnp.bfloat16) for j in range(NNZ)]
         mapping = jnp.concatenate([op_ref[b, j] for j in range(NNZ)], axis=1)
         pred = dot_rows(jnp.concatenate(picked, axis=1), mapping)
         mean = jnp.sum(pred, axis=0, keepdims=True) * (1.0 / K)
         spread.append(pred - mean)
-        scaled.append(spread[-1] * (1.0 / var_ref[b : b + 1, :]))
-        projected += scaled[-1] * (y_ref[b : b + 1, :] - mean)
+        scaled.append(spread[-1] * (1.0 / var_ref[b]))
+        projected += scaled[-1] * (y_ref[b] - mean)
     high, low = split(jnp.concatenate(scaled, axis=1))
     spread_high, spread_low = split(jnp.concatenate(spread, axis=1))
     both = dot_rows(jnp.concatenate([high, low], axis=0), spread_high)
@@ -382,7 +382,7 @@
     observed = scatter(packed[1:])
     bulk = scatter(pack_bulk(me, prior, packed[0]))
     folded = observe(
-        me, slots.reshape(-1), [packed[0]] + observed, mapping[:, 0], readings[:, 0], error_spread[:, 0]
+        me, jnp.transpose(slots, (1, 2, 0))[0], [packed[0]] + observed, mapping[:, 0], readings, error_spread
     )
     folded = lax.cond(member < GROUPS, total, lambda x: x, folded)
     weights = transform(folded)

time: 56.6 us -> 56 us (0.989)
  waiting for transfers between devices: 7.92 us -> 6.75 us
  Pallas kernels: 6.89 us -> 7.72 us
    ppermute x9, waiting for transfers between devices: 7.92 us -> 6.75 us  [scatter(): lax.ppermute(chunk, 'member', ring(s))]
    pallas_call x1, Pallas kernels: 0.12 us -> 0.8 us  [pack(): pl.pallas_call(pack_kernel, out_shape=[jax.ShapeDtypeStruct((VOBS, MEMBER...]
    unnamed x14 -> x12, local copies, waits for them, and re-layouts: 1.38 us -> 1.29 us
where the time goes in v8:
time: 56 us; the launch traced here: 55.8 us
  blocking collectives  26.4 us (47%)
  starting transfers between devices  12.9 us (23%)
  Pallas kernels  7.72 us (14%)
  waiting for transfers between devices  6.75 us (12%)
  local copies, waits for them, and re-layouts  1.29 us (2%)
  between operations  0.77 us (1%)
    all_to_all x2, blocking collectives, exchange(): return lax.all_to_all(copies, axes, 0, 0, tiled=True)  26.4 us
    ppermute x9, starting transfers between devices, scatter(): lax.ppermute(chunk, 'member', ring(s))  12.9 us
    ppermute x9, waiting for transfers between devices, scatter(): lax.ppermute(chunk, 'member', ring(s))  6.75 us
    pallas_call x1, Pallas kernels, transform(): pl.pallas_call(transform_kernel, out_shape=jax.ShapeDtypeStruct((K, K), j...  1.53 us
    pallas_call x1, Pallas kernels, observe(): pl.pallas_call(observe_kernel, out_shape=jax.ShapeDtypeStruct((HALF, 128)...  1.5 us
    pallas_call x1, Pallas kernels, analyse_far(): pl.pallas_call(far_kernel, out_shape=[jax.ShapeDtypeStruct((V, MEMBERS, G...  1.31 us
    unnamed x12, local copies, waits for them, and re-layouts  1.29 us
  transfers between devices with their start and end apart: 9, of which 2 were waited for; matrix products, arithmetic and copies ran while one was open for 0% of the time, Pallas kernels for 10%

profile of v8, /device:TPU:0, one launch (start us, length us, event | category | flops | bytes accessed | tf_op | source)
XLA Modules:
  0.0 55.8 jit_solution(273661408590433049)
XLA Ops:
  0.6 1.3 %copy-done = bf16[24,12,2048]{2,0,1:T(8,128)(2,1)S(1)} copy-done((bf16[24,12,2048]{2,0,1:T(8,128)(2,1)S(1)}, bf16[24,12,2048]{2,0,1:T(8,128)(2,1)}, u32[]{:S(2)}) %copy-start) | copy-done | bytes 1179672
  1.9 0.8 %pack.1 = (bf16[4,24,512]{2,1,0:T(8,128)(2,1)S(1)}, bf16[4,24,512]{2,1,0:T(8,128)(2,1)S(1)}, bf16[4,24,512]{2,1,0:T(8,128)(2,1)}, bf16[4,24,512]{2,1,0:T(8,128)(2,1)}) custom-call(s32[1]{0:T(128)} %bitcast.2.me_ref, bf16[12,24,2048]{2,1,0:T(8,128)(2,1)S(1)} %bitcast.9), custom_call_target="tpu_custom_call" | custom-call | tf_op jit(solution)/shard_map/pack/pallas_call | solution.py:57
  2.7 1.7 %collective-permute-start = (bf16[4,24,512]{2,1,0:T(8,128)(2,1)S(1)}, bf16[4,24,512]{2,1,0:T(8,128)(2,1)S(1)}, u32[]{:S(2)}, u32[]{:S(2)}) collective-permute-start(bf16[4,24,512]{2,1,0:T(8,128)(2,1)S(1)} %get-tuple-element.21), channel_id=1, source_target_pairs={{0,32},{32,64},{64,96},{96,0},{1,33},{33,65},{65,97},{97,1},{2,34}... | collective-permute-start | bytes 294920 | tf_op jit(solution)/shard_map/ppermute | solution.py:364
  4.5 2.9 %collective-permute-start.1 = (bf16[4,24,512]{2,1,0:T(8,128)(2,1)}, bf16[4,24,512]{2,1,0:T(8,128)(2,1)S(1)}, u32[]{:S(2)}, u32[]{:S(2)}) collective-permute-start(bf16[4,24,512]{2,1,0:T(8,128)(2,1)} %get-tuple-element.22), channel_id=1, source_target_pairs={{0,64},{32,96},{64,0},{96,32},{1,65},{33,97},{65,1},{97,33},{2,66}... | collective-permute-start | bytes 294920 | tf_op jit(solution)/shard_map/ppermute | solution.py:364
  7.4 1.3 %collective-permute-start.2 = (bf16[4,24,512]{2,1,0:T(8,128)(2,1)}, bf16[4,24,512]{2,1,0:T(8,128)(2,1)S(1)}, u32[]{:S(2)}, u32[]{:S(2)}) collective-permute-start(bf16[4,24,512]{2,1,0:T(8,128)(2,1)} %get-tuple-element.23), channel_id=1, source_target_pairs={{0,96},{32,0},{64,32},{96,64},{1,97},{33,1},{65,33},{97,65},{2,98}... | collective-permute-start | bytes 294920 | tf_op jit(solution)/shard_map/ppermute | solution.py:364
  8.7 1.1 %pack_bulk.1 = (bf16[23,24,512]{2,1,0:T(8,128)(2,1)}, bf16[23,24,512]{2,1,0:T(8,128)(2,1)}, bf16[23,24,512]{2,1,0:T(8,128)(2,1)S(1)}) custom-call(s32[1]{0:T(128)} %bitcast.2.me_ref, bf16[12,24,2048]{2,1,0:T(8,128)(2,1)S(1)} %bitcast.10, bf16[4,24,512]{2,1,0:T(8,128)(2,1)S(1)} %get-tuple-element.20.c0.after_ref), custom_call_target="tpu_custom_call" | custom-call | tf_op jit(solution)/shard_map/pack_bulk/pallas_call | solution.py:86
  9.8 0.7 %collective-permute-start.3 = (bf16[23,24,512]{2,1,0:T(8,128)(2,1)}, bf16[23,24,512]{2,1,0:T(8,128)(2,1)S(1)}, u32[]{:S(2)}, u32[]{:S(2)}) collective-permute-start(bf16[23,24,512]{2,1,0:T(8,128)(2,1)} %get-tuple-element.24), channel_id=1, source_target_pairs={{0,32},{32,64},{64,96},{96,0},{1,33},{33,65},{65,97},{97,1},{2,34}... | collective-permute-start | bytes 1695752 | tf_op jit(solution)/shard_map/ppermute | solution.py:364
  10.6 0.8 %collective-permute-start.4 = (bf16[23,24,512]{2,1,0:T(8,128)(2,1)}, bf16[23,24,512]{2,1,0:T(8,128)(2,1)S(1)}, u32[]{:S(2)}, u32[]{:S(2)}) collective-permute-start(bf16[23,24,512]{2,1,0:T(8,128)(2,1)} %get-tuple-element.25), channel_id=1, source_target_pairs={{0,64},{32,96},{64,0},{96,32},{1,65},{33,97},{65,1},{97,33},{2,66}... | collective-permute-start | bytes 1695752 | tf_op jit(solution)/shard_map/ppermute | solution.py:364
  11.4 2.0 %collective-permute-start.5 = (bf16[23,24,512]{2,1,0:T(8,128)(2,1)S(1)}, bf16[23,24,512]{2,1,0:T(8,128)(2,1)S(1)}, u32[]{:S(2)}, u32[]{:S(2)}) collective-permute-start(bf16[23,24,512]{2,1,0:T(8,128)(2,1)S(1)} %get-tuple-element.26), channel_id=1, source_target_pairs={{0,96},{32,0},{64,32},{96,64},{1,97},{33,1},{65,33},{97,65},{2,98}... | collective-permute-start | bytes 1695752 | tf_op jit(solution)/shard_map/ppermute | solution.py:364
  13.4 1.5 %observe.1 = f32[48,128]{1,0:T(8,128)S(1)} custom-call(s32[1]{0:T(128)} %bitcast.2.me_ref, s32[2,12]{1,0:T(2,128)S(1)} %bitcast.14, bf16[4,24,512]{2,1,0:T(8,128)(2,1)S(1)} %get-tuple-element.20.c0.after_ref, bf16[4,24,512]{2,1,0:T(8,128)(2,1)S(1)} %collective-permute-done.c1.o1, bf16[4,24,512]{2,1,0:T(8,128)(2,1)S(1)} %collective-permute-done.1.c2.o2, ...), custom_call_target="tpu_custom_call" | custom-call | tf_op jit(solution)/shard_map/observe/pallas_call | solution.py:163
  14.9 26.6 %conditional.1 = (f32[48,128]{1,0:T(8,128)S(1)}) conditional(s32[]{:T(128)} %convert_element_type.3, f32[48,128]{1,0:T(8,128)S(1)} %observe.1, f32[48,128]{1,0:T(8,128)S(1)} %observe.1), branch_computations={%region_0.0_spmd, %region_1.0_spmd} | conditional | bytes 786440 | solution.py:387
  14.9 0.1 spread_sum.3
  15.0 15.8 %all_to_all.8.parts_ref = bf16[16,48,128]{2,1,0:T(8,128)(2,1)S(1)} all-to-all(bf16[16,48,128]{2,1,0:T(8,128)(2,1)S(1)} %spread_sum.3), channel_id=1, replica_groups=mesh['member'=4,'x'=4,'z'=4,'core'=2] {'x','z'}, dimensions={0} | all-to-all | bytes 393216 | tf_op jit(solution)/shard_map/cond/branch_1_fun/all_to_all | solution.py:368
  30.8 0.1 spread_sum.4
  30.9 10.6 %all_to_all.9.parts_ref = f32[8,48,128]{2,1,0:T(8,128)S(1)} all-to-all(f32[8,48,128]{2,1,0:T(8,128)S(1)} %spread_sum.4), channel_id=1, replica_groups=mesh['member'=4,'x'=4,'z'=4,'core'=2] {'member','core'}, dimensions={0} | all-to-all | bytes 393216 | tf_op jit(solution)/shard_map/cond/branch_1_fun/all_to_all | solution.py:368
  41.5 1.5 %transform.1.w_ref = f32[96,96]{1,0:T(8,128)S(1)} custom-call(f32[48,128]{1,0:T(8,128)S(1)} %get-tuple-element.33.parts_ref), custom_call_target="tpu_custom_call" | custom-call | flops 40000000000 | tf_op jit(solution)/shard_map/transform/pallas_call | solution.py:240
  43.1 0.5 analyse_near.1
  43.6 0.6 %collective-permute-start.6 = (bf16[7,24,512]{2,1,0:T(8,128)(2,1)S(1)}, bf16[7,24,512]{2,1,0:T(8,128)(2,1)S(1)}, u32[]{:S(2)}, u32[]{:S(2)}) collective-permute-start(bf16[7,24,512]{2,1,0:T(8,128)(2,1)S(1)} %get-tuple-element.27), channel_id=1, source_target_pairs={{0,32},{32,64},{64,96},{96,0},{1,33},{33,65},{65,97},{97,1},{2,34}... | collective-permute-start | bytes 516104 | tf_op jit(solution)/shard_map/ppermute | solution.py:364
  44.2 2.1 %collective-permute-start.7 = (bf16[7,24,512]{2,1,0:T(8,128)(2,1)S(1)}, bf16[7,24,512]{2,1,0:T(8,128)(2,1)S(1)}, u32[]{:S(2)}, u32[]{:S(2)}) collective-permute-start(bf16[7,24,512]{2,1,0:T(8,128)(2,1)S(1)} %get-tuple-element.28), channel_id=1, source_target_pairs={{0,64},{32,96},{64,0},{96,32},{1,65},{33,97},{65,1},{97,33},{2,66}... | collective-permute-start | bytes 516104 | tf_op jit(solution)/shard_map/ppermute | solution.py:364
  46.2 0.7 %collective-permute-start.8 = (bf16[7,24,512]{2,1,0:T(8,128)(2,1)S(1)}, bf16[7,24,512]{2,1,0:T(8,128)(2,1)S(1)}, u32[]{:S(2)}, u32[]{:S(2)}) collective-permute-start(bf16[7,24,512]{2,1,0:T(8,128)(2,1)S(1)} %get-tuple-element.29), channel_id=1, source_target_pairs={{0,96},{32,0},{64,32},{96,64},{1,97},{33,1},{65,33},{97,65},{2,98}... | collective-permute-start | bytes 516104 | tf_op jit(solution)/shard_map/ppermute | solution.py:364
  46.9 1.3 %analyse_far.1 = (bf16[12,24,2048]{2,1,0:T(8,128)(2,1)}, f32[96,96]{1,0:T(8,128)}) custom-call(s32[1]{0:T(128)} %bitcast.2.me_ref, f32[96,96]{1,0:T(8,128)S(1)} %transform.1.w_ref, bf16[7,24,512]{2,1,0:T(8,128)(2,1)S(1)} %get-tuple-element.30.near_ref, bf16[12,24,2048]{2,1,0:T(8,128)(2,1)S(1)} %bitcast.12, ...), custom_call_target="tpu_custom_call" | custom-call | tf_op jit(solution)/shard_map/analyse_far/pallas_call | solution.py:316
  48.3 6.1 %collective-permute-done.6.c1 = bf16[7,24,512]{2,1,0:T(8,128)(2,1)S(1)} collective-permute-done((bf16[7,24,512]{2,1,0:T(8,128)(2,1)S(1)}, bf16[7,24,512]{2,1,0:T(8,128)(2,1)S(1)}, u32[]{:S(2)}, u32[]{:S(2)}) %collective-permute-start.6) | collective-permute-done | bytes 172064 | tf_op jit(solution)/shard_map/ppermute | solution.py:364
  54.4 0.6 %collective-permute-done.8.c3 = bf16[7,24,512]{2,1,0:T(8,128)(2,1)S(1)} collective-permute-done((bf16[7,24,512]{2,1,0:T(8,128)(2,1)S(1)}, bf16[7,24,512]{2,1,0:T(8,128)(2,1)S(1)}, u32[]{:S(2)}, u32[]{:S(2)}) %collective-permute-start.8) | collective-permute-done | bytes 172064 | tf_op jit(solution)/shard_map/ppermute | solution.py:364
  55.0 0.8 %place.1 = bf16[12,24,2048]{2,1,0:T(8,128)(2,1)} custom-call(s32[1]{0:T(128)} %bitcast.2.me_ref, bf16[7,24,512]{2,1,0:T(8,128)(2,1)S(1)} %collective-permute-done.6.c1, bf16[7,24,512]{2,1,0:T(8,128)(2,1)S(1)} %collective-permute-done.7.c2, bf16[7,24,512]{2,1,0:T(8,128)(2,1)S(1)} %collective-permute-done.8.c3, ...), custom_call_target="tpu_custom_call", output_to_operand_aliasing={{}: (4, {})} | custom-call | tf_op jit(solution)/shard_map/place/pallas_call | solution.py:347
  (19 shorter events, 0.1 us)
Async XLA Ops:
  0.6 1.3 %copy-start = (bf16[24,12,2048]{2,0,1:T(8,128)(2,1)S(1)}, bf16[24,12,2048]{2,0,1:T(8,128)(2,1)}, u32[]{:S(2)}) copy-start(bf16[24,12,2048]{2,0,1:T(8,128)(2,1)} %param.7) | copy-start | bytes 3538948
  1.9 11.4 %copy-start.2 = (bf16[12,1,2,128,128]{4,3,2,1,0:T(8,128)(2,1)S(1)}, bf16[12,1,2,128,128]{4,3,2,1,0:T(8,128)(2,1)}, u32[]{:S(2)}) copy-start(bf16[12,1,2,128,128]{4,3,2,1,0:T(8,128)(2,1)} %param.10) | copy-start | bytes 2359300
  1.9 11.4 %copy-start.3 = (f32[12,1,128]{2,1,0:T(1,128)S(1)}, f32[12,1,128]{2,1,0:T(1,128)}, u32[]{:S(2)}) copy-start(f32[12,1,128]{2,1,0:T(1,128)} %y_ref.1) | copy-start | bytes 18436
  1.9 11.5 %copy-start.4 = (f32[12,1,128]{2,1,0:T(1,128)S(1)}, f32[12,1,128]{2,1,0:T(1,128)}, u32[]{:S(2)}) copy-start(f32[12,1,128]{2,1,0:T(1,128)} %var_ref.1) | copy-start | bytes 18436
  1.9 11.5 %copy-start.5 = (s32[12,1,2]{0,2,1:T(2,128)S(1)}, s32[12,1,2]{0,2,1:T(2,128)}, u32[]{:S(2)}) copy-start(s32[12,1,2]{0,2,1:T(2,128)} %param.11) | copy-start | bytes 292
  2.7 8.6 %collective-permute-start = (bf16[4,24,512]{2,1,0:T(8,128)(2,1)S(1)}, bf16[4,24,512]{2,1,0:T(8,128)(2,1)S(1)}, u32[]{:S(2)}, u32[]{:S(2)}) collective-permute-start(bf16[4,24,512]{2,1,0:T(8,128)(2,1)S(1)} %get-tuple-element.21), channel_id=1, source_target_pairs={{0,32},{32,64},{64,96},{96,0},{1,33},{33,65},{65,97},{97,1},{2,34}... | collective-permute-start | bytes 294920 | tf_op jit(solution)/shard_map/ppermute | solution.py:364
  4.5 8.9 %collective-permute-start.1 = (bf16[4,24,512]{2,1,0:T(8,128)(2,1)}, bf16[4,24,512]{2,1,0:T(8,128)(2,1)S(1)}, u32[]{:S(2)}, u32[]{:S(2)}) collective-permute-start(bf16[4,24,512]{2,1,0:T(8,128)(2,1)} %get-tuple-element.22), channel_id=1, source_target_pairs={{0,64},{32,96},{64,0},{96,32},{1,65},{33,97},{65,1},{97,33},{2,66}... | collective-permute-start | bytes 294920 | tf_op jit(solution)/shard_map/ppermute | solution.py:364
  7.4 6.0 %collective-permute-start.2 = (bf16[4,24,512]{2,1,0:T(8,128)(2,1)}, bf16[4,24,512]{2,1,0:T(8,128)(2,1)S(1)}, u32[]{:S(2)}, u32[]{:S(2)}) collective-permute-start(bf16[4,24,512]{2,1,0:T(8,128)(2,1)} %get-tuple-element.23), channel_id=1, source_target_pairs={{0,96},{32,0},{64,32},{96,64},{1,97},{33,1},{65,33},{97,65},{2,98}... | collective-permute-start | bytes 294920 | tf_op jit(solution)/shard_map/ppermute | solution.py:364
  9.8 33.2 %collective-permute-start.3 = (bf16[23,24,512]{2,1,0:T(8,128)(2,1)}, bf16[23,24,512]{2,1,0:T(8,128)(2,1)S(1)}, u32[]{:S(2)}, u32[]{:S(2)}) collective-permute-start(bf16[23,24,512]{2,1,0:T(8,128)(2,1)} %get-tuple-element.24), channel_id=1, source_target_pairs={{0,32},{32,64},{64,96},{96,0},{1,33},{33,65},{65,97},{97,1},{2,34}... | collective-permute-start | bytes 1695752 | tf_op jit(solution)/shard_map/ppermute | solution.py:364
  10.6 32.5 %collective-permute-start.4 = (bf16[23,24,512]{2,1,0:T(8,128)(2,1)}, bf16[23,24,512]{2,1,0:T(8,128)(2,1)S(1)}, u32[]{:S(2)}, u32[]{:S(2)}) collective-permute-start(bf16[23,24,512]{2,1,0:T(8,128)(2,1)} %get-tuple-element.25), channel_id=1, source_target_pairs={{0,64},{32,96},{64,0},{96,32},{1,65},{33,97},{65,1},{97,33},{2,66}... | collective-permute-start | bytes 1695752 | tf_op jit(solution)/shard_map/ppermute | solution.py:364
  11.4 31.7 %collective-permute-start.5 = (bf16[23,24,512]{2,1,0:T(8,128)(2,1)S(1)}, bf16[23,24,512]{2,1,0:T(8,128)(2,1)S(1)}, u32[]{:S(2)}, u32[]{:S(2)}) collective-permute-start(bf16[23,24,512]{2,1,0:T(8,128)(2,1)S(1)} %get-tuple-element.26), channel_id=1, source_target_pairs={{0,96},{32,0},{64,32},{96,64},{1,97},{33,1},{65,33},{97,65},{2,98}... | collective-permute-start | bytes 1695752 | tf_op jit(solution)/shard_map/ppermute | solution.py:364
  41.5 1.6 %copy-start.1 = (bf16[24,12,2048]{2,0,1:T(8,128)(2,1)S(1)}, bf16[24,12,2048]{2,0,1:T(8,128)(2,1)}, u32[]{:S(2)}) copy-start(bf16[24,12,2048]{2,0,1:T(8,128)(2,1)} %param.7) | copy-start | bytes 3538948
  43.6 10.8 %collective-permute-start.6 = (bf16[7,24,512]{2,1,0:T(8,128)(2,1)S(1)}, bf16[7,24,512]{2,1,0:T(8,128)(2,1)S(1)}, u32[]{:S(2)}, u32[]{:S(2)}) collective-permute-start(bf16[7,24,512]{2,1,0:T(8,128)(2,1)S(1)} %get-tuple-element.27), channel_id=1, source_target_pairs={{0,32},{32,64},{64,96},{96,0},{1,33},{33,65},{65,97},{97,1},{2,34}... | collective-permute-start | bytes 516104 | tf_op jit(solution)/shard_map/ppermute | solution.py:364
  44.2 10.2 %collective-permute-start.7 = (bf16[7,24,512]{2,1,0:T(8,128)(2,1)S(1)}, bf16[7,24,512]{2,1,0:T(8,128)(2,1)S(1)}, u32[]{:S(2)}, u32[]{:S(2)}) collective-permute-start(bf16[7,24,512]{2,1,0:T(8,128)(2,1)S(1)} %get-tuple-element.28), channel_id=1, source_target_pairs={{0,64},{32,96},{64,0},{96,32},{1,65},{33,97},{65,1},{97,33},{2,66}... | collective-permute-start | bytes 516104 | tf_op jit(solution)/shard_map/ppermute | solution.py:364
  46.2 8.7 %collective-permute-start.8 = (bf16[7,24,512]{2,1,0:T(8,128)(2,1)S(1)}, bf16[7,24,512]{2,1,0:T(8,128)(2,1)S(1)}, u32[]{:S(2)}, u32[]{:S(2)}) collective-permute-start(bf16[7,24,512]{2,1,0:T(8,128)(2,1)S(1)} %get-tuple-element.29), channel_id=1, source_target_pairs={{0,96},{32,0},{64,32},{96,64},{1,97},{33,1},{65,33},{97,65},{2,98}... | collective-permute-start | bytes 516104 | tf_op jit(solution)/shard_map/ppermute | solution.py:364

commit v9 on v8

--- a/solution.py
+++ b/solution.py
@@ -376,7 +376,8 @@
 
 def body(prior, readings, error_spread, mapping, slots):
     member = lax.axis_index("member").astype(jnp.int32)
-    me = member.reshape(1)
+    always = member < GROUPS
+    me = (member + 1 - always.astype(jnp.int32)).reshape(1)
     prior = jnp.transpose(prior, (1, 0, 2))
     packed = pack(me, prior)
     observed = scatter(packed[1:])
@@ -384,7 +385,7 @@
     folded = observe(
         me, jnp.transpose(slots, (1, 2, 0))[0], [packed[0]] + observed, mapping[:, 0], readings, error_spread
     )
-    folded = lax.cond(member < GROUPS, total, lambda x: x, folded)
+    folded = lax.cond(always, total, lambda x: x, folded)
     weights = transform(folded)
     near = analyse_near(me, weights, prior, observed, bulk)
     arrived = scatter(near[1:])

time: 56 us -> 55.2 us (0.986)
  Pallas kernels: 7.72 us -> 6.86 us
    pallas_call x1, Pallas kernels: 0.8 us -> 0.12 us  [pack(): pl.pallas_call(pack_kernel, out_shape=[jax.ShapeDtypeStruct((VOBS, MEMBER...]
where the time goes in v9:
time: 55.2 us; the launch traced here: 54.9 us
  blocking collectives  26.4 us (48%)
  starting transfers between devices  12.9 us (23%)
  Pallas kernels  6.86 us (12%)
  waiting for transfers between devices  6.73 us (12%)
  local copies, waits for them, and re-layouts  1.29 us (2%)
  between operations  0.77 us (1%)
    all_to_all x2, blocking collectives, exchange(): return lax.all_to_all(copies, axes, 0, 0, tiled=True)  26.4 us
    ppermute x9, starting transfers between devices, scatter(): lax.ppermute(chunk, 'member', ring(s))  12.9 us
    ppermute x9, waiting for transfers between devices, scatter(): lax.ppermute(chunk, 'member', ring(s))  6.73 us
    pallas_call x1, Pallas kernels, transform(): pl.pallas_call(transform_kernel, out_shape=jax.ShapeDtypeStruct((K, K), j...  1.53 us
    pallas_call x1, Pallas kernels, observe(): pl.pallas_call(observe_kernel, out_shape=jax.ShapeDtypeStruct((HALF, 128)...  1.5 us
    pallas_call x1, Pallas kernels, analyse_far(): pl.pallas_call(far_kernel, out_shape=[jax.ShapeDtypeStruct((V, MEMBERS, G...  1.3 us
    unnamed x12, local copies, waits for them, and re-layouts  1.29 us
  transfers between devices with their start and end apart: 9, of which 2 were waited for; matrix products, arithmetic and copies ran while one was open for 0% of the time, Pallas kernels for 10%

profile of v9, /device:TPU:0, one launch (start us, length us, event | category | flops | bytes accessed | tf_op | source)
XLA Modules:
  0.0 54.9 jit_solution(5363237611655957488)
XLA Ops:
  0.6 1.3 %copy-done = bf16[24,12,2048]{2,0,1:T(8,128)(2,1)S(1)} copy-done((bf16[24,12,2048]{2,0,1:T(8,128)(2,1)S(1)}, bf16[24,12,2048]{2,0,1:T(8,128)(2,1)}, u32[]{:S(2)}) %copy-start) | copy-done | bytes 1179672
  1.9 0.1 pack.1
  2.0 1.7 %collective-permute-start = (bf16[4,24,512]{2,1,0:T(8,128)(2,1)S(1)}, bf16[4,24,512]{2,1,0:T(8,128)(2,1)S(1)}, u32[]{:S(2)}, u32[]{:S(2)}) collective-permute-start(bf16[4,24,512]{2,1,0:T(8,128)(2,1)S(1)} %get-tuple-element.21), channel_id=1, source_target_pairs={{0,32},{32,64},{64,96},{96,0},{1,33},{33,65},{65,97},{97,1},{2,34}... | collective-permute-start | bytes 294920 | tf_op jit(solution)/shard_map/ppermute | solution.py:364
  3.8 2.9 %collective-permute-start.1 = (bf16[4,24,512]{2,1,0:T(8,128)(2,1)S(1)}, bf16[4,24,512]{2,1,0:T(8,128)(2,1)S(1)}, u32[]{:S(2)}, u32[]{:S(2)}) collective-permute-start(bf16[4,24,512]{2,1,0:T(8,128)(2,1)S(1)} %get-tuple-element.22), channel_id=1, source_target_pairs={{0,64},{32,96},{64,0},{96,32},{1,65},{33,97},{65,1},{97,33},{2,66}... | collective-permute-start | bytes 294920 | tf_op jit(solution)/shard_map/ppermute | solution.py:364
  6.7 1.3 %collective-permute-start.2 = (bf16[4,24,512]{2,1,0:T(8,128)(2,1)S(1)}, bf16[4,24,512]{2,1,0:T(8,128)(2,1)S(1)}, u32[]{:S(2)}, u32[]{:S(2)}) collective-permute-start(bf16[4,24,512]{2,1,0:T(8,128)(2,1)S(1)} %get-tuple-element.23), channel_id=1, source_target_pairs={{0,96},{32,0},{64,32},{96,64},{1,97},{33,1},{65,33},{97,65},{2,98}... | collective-permute-start | bytes 294920 | tf_op jit(solution)/shard_map/ppermute | solution.py:364
  8.0 0.9 %pack_bulk.1 = (bf16[23,24,512]{2,1,0:T(8,128)(2,1)}, bf16[23,24,512]{2,1,0:T(8,128)(2,1)S(1)}, bf16[23,24,512]{2,1,0:T(8,128)(2,1)S(1)}) custom-call(s32[1]{0:T(128)} %bitcast.2.me_ref, bf16[12,24,2048]{2,1,0:T(8,128)(2,1)S(1)} %bitcast.10, bf16[4,24,512]{2,1,0:T(8,128)(2,1)S(1)} %get-tuple-element.20.c0.after_ref), custom_call_target="tpu_custom_call" | custom-call | tf_op jit(solution)/shard_map/pack_bulk/pallas_call | solution.py:86
  9.0 0.7 %collective-permute-start.3 = (bf16[23,24,512]{2,1,0:T(8,128)(2,1)}, bf16[23,24,512]{2,1,0:T(8,128)(2,1)S(1)}, u32[]{:S(2)}, u32[]{:S(2)}) collective-permute-start(bf16[23,24,512]{2,1,0:T(8,128)(2,1)} %get-tuple-element.24), channel_id=1, source_target_pairs={{0,32},{32,64},{64,96},{96,0},{1,33},{33,65},{65,97},{97,1},{2,34}... | collective-permute-start | bytes 1695752 | tf_op jit(solution)/shard_map/ppermute | solution.py:364
  9.7 0.8 %collective-permute-start.4 = (bf16[23,24,512]{2,1,0:T(8,128)(2,1)S(1)}, bf16[23,24,512]{2,1,0:T(8,128)(2,1)S(1)}, u32[]{:S(2)}, u32[]{:S(2)}) collective-permute-start(bf16[23,24,512]{2,1,0:T(8,128)(2,1)S(1)} %get-tuple-element.25), channel_id=1, source_target_pairs={{0,64},{32,96},{64,0},{96,32},{1,65},{33,97},{65,1},{97,33},{2,66}... | collective-permute-start | bytes 1695752 | tf_op jit(solution)/shard_map/ppermute | solution.py:364
  10.5 2.0 %collective-permute-start.5 = (bf16[23,24,512]{2,1,0:T(8,128)(2,1)S(1)}, bf16[23,24,512]{2,1,0:T(8,128)(2,1)S(1)}, u32[]{:S(2)}, u32[]{:S(2)}) collective-permute-start(bf16[23,24,512]{2,1,0:T(8,128)(2,1)S(1)} %get-tuple-element.26), channel_id=1, source_target_pairs={{0,96},{32,0},{64,32},{96,64},{1,97},{33,1},{65,33},{97,65},{2,98}... | collective-permute-start | bytes 1695752 | tf_op jit(solution)/shard_map/ppermute | solution.py:364
  12.5 1.5 %observe.1 = f32[48,128]{1,0:T(8,128)S(1)} custom-call(s32[1]{0:T(128)} %bitcast.2.me_ref, s32[2,12]{1,0:T(2,128)S(1)} %bitcast.14, bf16[4,24,512]{2,1,0:T(8,128)(2,1)S(1)} %get-tuple-element.20.c0.after_ref, bf16[4,24,512]{2,1,0:T(8,128)(2,1)S(1)} %collective-permute-done.c1.o1, bf16[4,24,512]{2,1,0:T(8,128)(2,1)S(1)} %collective-permute-done.1.c2.o2, ...), custom_call_target="tpu_custom_call" | custom-call | tf_op jit(solution)/shard_map/observe/pallas_call | solution.py:163
  14.0 26.6 %conditional.1 = (f32[48,128]{1,0:T(8,128)S(1)}) conditional(s32[]{:T(128)} %convert_element_type.4, f32[48,128]{1,0:T(8,128)S(1)} %observe.1, f32[48,128]{1,0:T(8,128)S(1)} %observe.1), branch_computations={%region_0.0_spmd, %region_1.0_spmd} | conditional | bytes 786440 | solution.py:388
  14.0 0.1 spread_sum.3
  14.1 15.8 %all_to_all.8.parts_ref = bf16[16,48,128]{2,1,0:T(8,128)(2,1)S(1)} all-to-all(bf16[16,48,128]{2,1,0:T(8,128)(2,1)S(1)} %spread_sum.3), channel_id=1, replica_groups=mesh['member'=4,'x'=4,'z'=4,'core'=2] {'x','z'}, dimensions={0} | all-to-all | bytes 393216 | tf_op jit(solution)/shard_map/cond/branch_1_fun/all_to_all | solution.py:368
  29.9 0.1 spread_sum.4
  30.0 10.6 %all_to_all.9.parts_ref = f32[8,48,128]{2,1,0:T(8,128)S(1)} all-to-all(f32[8,48,128]{2,1,0:T(8,128)S(1)} %spread_sum.4), channel_id=1, replica_groups=mesh['member'=4,'x'=4,'z'=4,'core'=2] {'member','core'}, dimensions={0} | all-to-all | bytes 393216 | tf_op jit(solution)/shard_map/cond/branch_1_fun/all_to_all | solution.py:368
  40.7 1.5 %transform.1.w_ref = f32[96,96]{1,0:T(8,128)S(1)} custom-call(f32[48,128]{1,0:T(8,128)S(1)} %get-tuple-element.33.parts_ref), custom_call_target="tpu_custom_call" | custom-call | flops 40000000000 | tf_op jit(solution)/shard_map/transform/pallas_call | solution.py:240
  42.2 0.5 analyse_near.1
  42.7 0.6 %collective-permute-start.6 = (bf16[7,24,512]{2,1,0:T(8,128)(2,1)S(1)}, bf16[7,24,512]{2,1,0:T(8,128)(2,1)S(1)}, u32[]{:S(2)}, u32[]{:S(2)}) collective-permute-start(bf16[7,24,512]{2,1,0:T(8,128)(2,1)S(1)} %get-tuple-element.27), channel_id=1, source_target_pairs={{0,32},{32,64},{64,96},{96,0},{1,33},{33,65},{65,97},{97,1},{2,34}... | collective-permute-start | bytes 516104 | tf_op jit(solution)/shard_map/ppermute | solution.py:364
  43.3 2.1 %collective-permute-start.7 = (bf16[7,24,512]{2,1,0:T(8,128)(2,1)S(1)}, bf16[7,24,512]{2,1,0:T(8,128)(2,1)S(1)}, u32[]{:S(2)}, u32[]{:S(2)}) collective-permute-start(bf16[7,24,512]{2,1,0:T(8,128)(2,1)S(1)} %get-tuple-element.28), channel_id=1, source_target_pairs={{0,64},{32,96},{64,0},{96,32},{1,65},{33,97},{65,1},{97,33},{2,66}... | collective-permute-start | bytes 516104 | tf_op jit(solution)/shard_map/ppermute | solution.py:364
  45.4 0.7 %collective-permute-start.8 = (bf16[7,24,512]{2,1,0:T(8,128)(2,1)S(1)}, bf16[7,24,512]{2,1,0:T(8,128)(2,1)S(1)}, u32[]{:S(2)}, u32[]{:S(2)}) collective-permute-start(bf16[7,24,512]{2,1,0:T(8,128)(2,1)S(1)} %get-tuple-element.29), channel_id=1, source_target_pairs={{0,96},{32,0},{64,32},{96,64},{1,97},{33,1},{65,33},{97,65},{2,98}... | collective-permute-start | bytes 516104 | tf_op jit(solution)/shard_map/ppermute | solution.py:364
  46.1 1.3 %analyse_far.1 = (bf16[12,24,2048]{2,1,0:T(8,128)(2,1)}, f32[96,96]{1,0:T(8,128)}) custom-call(s32[1]{0:T(128)} %bitcast.2.me_ref, f32[96,96]{1,0:T(8,128)S(1)} %transform.1.w_ref, bf16[7,24,512]{2,1,0:T(8,128)(2,1)S(1)} %get-tuple-element.30.near_ref, bf16[12,24,2048]{2,1,0:T(8,128)(2,1)S(1)} %bitcast.12, ...), custom_call_target="tpu_custom_call" | custom-call | tf_op jit(solution)/shard_map/analyse_far/pallas_call | solution.py:316
  47.4 6.1 %collective-permute-done.6.c1 = bf16[7,24,512]{2,1,0:T(8,128)(2,1)S(1)} collective-permute-done((bf16[7,24,512]{2,1,0:T(8,128)(2,1)S(1)}, bf16[7,24,512]{2,1,0:T(8,128)(2,1)S(1)}, u32[]{:S(2)}, u32[]{:S(2)}) %collective-permute-start.6) | collective-permute-done | bytes 172064 | tf_op jit(solution)/shard_map/ppermute | solution.py:364
  53.5 0.6 %collective-permute-done.8.c3 = bf16[7,24,512]{2,1,0:T(8,128)(2,1)S(1)} collective-permute-done((bf16[7,24,512]{2,1,0:T(8,128)(2,1)S(1)}, bf16[7,24,512]{2,1,0:T(8,128)(2,1)S(1)}, u32[]{:S(2)}, u32[]{:S(2)}) %collective-permute-start.8) | collective-permute-done | bytes 172064 | tf_op jit(solution)/shard_map/ppermute | solution.py:364
  54.1 0.8 %place.1 = bf16[12,24,2048]{2,1,0:T(8,128)(2,1)} custom-call(s32[1]{0:T(128)} %bitcast.2.me_ref, bf16[7,24,512]{2,1,0:T(8,128)(2,1)S(1)} %collective-permute-done.6.c1, bf16[7,24,512]{2,1,0:T(8,128)(2,1)S(1)} %collective-permute-done.7.c2, bf16[7,24,512]{2,1,0:T(8,128)(2,1)S(1)} %collective-permute-done.8.c3, ...), custom_call_target="tpu_custom_call", output_to_operand_aliasing={{}: (4, {})} | custom-call | tf_op jit(solution)/shard_map/place/pallas_call | solution.py:347
  (19 shorter events, 0.1 us)
Async XLA Ops:
  0.6 1.3 %copy-start = (bf16[24,12,2048]{2,0,1:T(8,128)(2,1)S(1)}, bf16[24,12,2048]{2,0,1:T(8,128)(2,1)}, u32[]{:S(2)}) copy-start(bf16[24,12,2048]{2,0,1:T(8,128)(2,1)} %param.7) | copy-start | bytes 3538948
  1.9 10.6 %copy-start.2 = (bf16[12,1,2,128,128]{4,3,2,1,0:T(8,128)(2,1)S(1)}, bf16[12,1,2,128,128]{4,3,2,1,0:T(8,128)(2,1)}, u32[]{:S(2)}) copy-start(bf16[12,1,2,128,128]{4,3,2,1,0:T(8,128)(2,1)} %param.10) | copy-start | bytes 2359300
  1.9 10.6 %copy-start.3 = (f32[12,1,128]{2,1,0:T(1,128)S(1)}, f32[12,1,128]{2,1,0:T(1,128)}, u32[]{:S(2)}) copy-start(f32[12,1,128]{2,1,0:T(1,128)} %y_ref.1) | copy-start | bytes 18436
  1.9 10.6 %copy-start.4 = (f32[12,1,128]{2,1,0:T(1,128)S(1)}, f32[12,1,128]{2,1,0:T(1,128)}, u32[]{:S(2)}) copy-start(f32[12,1,128]{2,1,0:T(1,128)} %var_ref.1) | copy-start | bytes 18436
  1.9 10.6 %copy-start.5 = (s32[12,1,2]{0,2,1:T(2,128)S(1)}, s32[12,1,2]{0,2,1:T(2,128)}, u32[]{:S(2)}) copy-start(s32[12,1,2]{0,2,1:T(2,128)} %param.11) | copy-start | bytes 292
  2.0 8.5 %collective-permute-start = (bf16[4,24,512]{2,1,0:T(8,128)(2,1)S(1)}, bf16[4,24,512]{2,1,0:T(8,128)(2,1)S(1)}, u32[]{:S(2)}, u32[]{:S(2)}) collective-permute-start(bf16[4,24,512]{2,1,0:T(8,128)(2,1)S(1)} %get-tuple-element.21), channel_id=1, source_target_pairs={{0,32},{32,64},{64,96},{96,0},{1,33},{33,65},{65,97},{97,1},{2,34}... | collective-permute-start | bytes 294920 | tf_op jit(solution)/shard_map/ppermute | solution.py:364
  3.8 8.7 %collective-permute-start.1 = (bf16[4,24,512]{2,1,0:T(8,128)(2,1)S(1)}, bf16[4,24,512]{2,1,0:T(8,128)(2,1)S(1)}, u32[]{:S(2)}, u32[]{:S(2)}) collective-permute-start(bf16[4,24,512]{2,1,0:T(8,128)(2,1)S(1)} %get-tuple-element.22), channel_id=1, source_target_pairs={{0,64},{32,96},{64,0},{96,32},{1,65},{33,97},{65,1},{97,33},{2,66}... | collective-permute-start | bytes 294920 | tf_op jit(solution)/shard_map/ppermute | solution.py:364
  6.7 5.8 %collective-permute-start.2 = (bf16[4,24,512]{2,1,0:T(8,128)(2,1)S(1)}, bf16[4,24,512]{2,1,0:T(8,128)(2,1)S(1)}, u32[]{:S(2)}, u32[]{:S(2)}) collective-permute-start(bf16[4,24,512]{2,1,0:T(8,128)(2,1)S(1)} %get-tuple-element.23), channel_id=1, source_target_pairs={{0,96},{32,0},{64,32},{96,64},{1,97},{33,1},{65,33},{97,65},{2,98}... | collective-permute-start | bytes 294920 | tf_op jit(solution)/shard_map/ppermute | solution.py:364
  9.0 33.2 %collective-permute-start.3 = (bf16[23,24,512]{2,1,0:T(8,128)(2,1)}, bf16[23,24,512]{2,1,0:T(8,128)(2,1)S(1)}, u32[]{:S(2)}, u32[]{:S(2)}) collective-permute-start(bf16[23,24,512]{2,1,0:T(8,128)(2,1)} %get-tuple-element.24), channel_id=1, source_target_pairs={{0,32},{32,64},{64,96},{96,0},{1,33},{33,65},{65,97},{97,1},{2,34}... | collective-permute-start | bytes 1695752 | tf_op jit(solution)/shard_map/ppermute | solution.py:364
  9.7 32.5 %collective-permute-start.4 = (bf16[23,24,512]{2,1,0:T(8,128)(2,1)S(1)}, bf16[23,24,512]{2,1,0:T(8,128)(2,1)S(1)}, u32[]{:S(2)}, u32[]{:S(2)}) collective-permute-start(bf16[23,24,512]{2,1,0:T(8,128)(2,1)S(1)} %get-tuple-element.25), channel_id=1, source_target_pairs={{0,64},{32,96},{64,0},{96,32},{1,65},{33,97},{65,1},{97,33},{2,66}... | collective-permute-start | bytes 1695752 | tf_op jit(solution)/shard_map/ppermute | solution.py:364
  10.5 31.7 %collective-permute-start.5 = (bf16[23,24,512]{2,1,0:T(8,128)(2,1)S(1)}, bf16[23,24,512]{2,1,0:T(8,128)(2,1)S(1)}, u32[]{:S(2)}, u32[]{:S(2)}) collective-permute-start(bf16[23,24,512]{2,1,0:T(8,128)(2,1)S(1)} %get-tuple-element.26), channel_id=1, source_target_pairs={{0,96},{32,0},{64,32},{96,64},{1,97},{33,1},{65,33},{97,65},{2,98}... | collective-permute-start | bytes 1695752 | tf_op jit(solution)/shard_map/ppermute | solution.py:364
  40.7 1.6 %copy-start.1 = (bf16[24,12,2048]{2,0,1:T(8,128)(2,1)S(1)}, bf16[24,12,2048]{2,0,1:T(8,128)(2,1)}, u32[]{:S(2)}) copy-start(bf16[24,12,2048]{2,0,1:T(8,128)(2,1)} %param.7) | copy-start | bytes 3538948
  42.7 10.8 %collective-permute-start.6 = (bf16[7,24,512]{2,1,0:T(8,128)(2,1)S(1)}, bf16[7,24,512]{2,1,0:T(8,128)(2,1)S(1)}, u32[]{:S(2)}, u32[]{:S(2)}) collective-permute-start(bf16[7,24,512]{2,1,0:T(8,128)(2,1)S(1)} %get-tuple-element.27), channel_id=1, source_target_pairs={{0,32},{32,64},{64,96},{96,0},{1,33},{33,65},{65,97},{97,1},{2,34}... | collective-permute-start | bytes 516104 | tf_op jit(solution)/shard_map/ppermute | solution.py:364
  43.3 10.2 %collective-permute-start.7 = (bf16[7,24,512]{2,1,0:T(8,128)(2,1)S(1)}, bf16[7,24,512]{2,1,0:T(8,128)(2,1)S(1)}, u32[]{:S(2)}, u32[]{:S(2)}) collective-permute-start(bf16[7,24,512]{2,1,0:T(8,128)(2,1)S(1)} %get-tuple-element.28), channel_id=1, source_target_pairs={{0,64},{32,96},{64,0},{96,32},{1,65},{33,97},{65,1},{97,33},{2,66}... | collective-permute-start | bytes 516104 | tf_op jit(solution)/shard_map/ppermute | solution.py:364
  45.4 8.7 %collective-permute-start.8 = (bf16[7,24,512]{2,1,0:T(8,128)(2,1)S(1)}, bf16[7,24,512]{2,1,0:T(8,128)(2,1)S(1)}, u32[]{:S(2)}, u32[]{:S(2)}) collective-permute-start(bf16[7,24,512]{2,1,0:T(8,128)(2,1)S(1)} %get-tuple-element.29), channel_id=1, source_target_pairs={{0,96},{32,0},{64,32},{96,64},{1,97},{33,1},{65,33},{97,65},{2,98}... | collective-permute-start | bytes 516104 | tf_op jit(solution)/shard_map/ppermute | solution.py:364

commit v10 on v9

--- a/solution.py
+++ b/solution.py
@@ -180,15 +180,19 @@
 
 
 def narrow(folded):
-    _, lane = indices()
+    row, lane = indices()
     high = folded.astype(jnp.bfloat16).astype(jnp.float32)
-    low = pltpu.roll(folded - high, 3, 1)
-    return jnp.where((lane >= K + 3) & (lane < K + 6), low, high).astype(jnp.bfloat16)
+    rest = folded - high
+    low = pltpu.roll(rest, 3, 1)
+    diagonal = jnp.sum(jnp.where(lane == row, rest, 0.0), axis=1, keepdims=True)
+    out = jnp.where((lane >= K + 3) & (lane < K + 6), low, high)
+    return jnp.where(lane == K + 6, diagonal, out).astype(jnp.bfloat16)
 
 
 def widen(total):
-    _, lane = indices()
-    return jnp.where((lane >= K) & (lane < K + 3), total + pltpu.roll(total, 125, 1), total)
+    row, lane = indices()
+    out = jnp.where((lane >= K) & (lane < K + 3), total + pltpu.roll(total, 125, 1), total)
+    return jnp.where(lane == row, out + total[:, K + 6 : K + 7], out)
 
 
 def spread_kernel(parts_ref, out_ref):
@@ -370,7 +374,7 @@
 
 def total(folded):
     copies = exchange(spread_sum(folded[None], PLANE, jnp.bfloat16), ("x", "z"))
-    copies = exchange(spread_sum(copies, COLUMN), ("member", "core"))
+    copies = exchange(spread_sum(copies, COLUMN, jnp.bfloat16), ("member", "core"))
     return spread_sum(copies, 1)[0]
 
 

time: 55.2 us -> 54.4 us (0.986)
  blocking collectives: 26.4 us -> 25.3 us
    all_to_all x2, blocking collectives: 26.4 us -> 25.3 us  [exchange(): return lax.all_to_all(copies, axes, 0, 0, tiled=True)]
where the time goes in v10:
time: 54.4 us; the launch traced here: 54.2 us
  blocking collectives  25.3 us (47%)
  starting transfers between devices  13.1 us (24%)
  Pallas kernels  7.05 us (13%)
  waiting for transfers between devices  6.65 us (12%)
  local copies, waits for them, and re-layouts  1.29 us (2%)
  between operations  0.77 us (1%)
    all_to_all x2, blocking collectives, exchange(): return lax.all_to_all(copies, axes, 0, 0, tiled=True)  25.3 us
    ppermute x9, starting transfers between devices, scatter(): lax.ppermute(chunk, 'member', ring(s))  13.1 us
    ppermute x9, waiting for transfers between devices, scatter(): lax.ppermute(chunk, 'member', ring(s))  6.65 us
    pallas_call x1, Pallas kernels, transform(): pl.pallas_call(transform_kernel, out_shape=jax.ShapeDtypeStruct((K, K), j...  1.53 us
    pallas_call x1, Pallas kernels, observe(): pl.pallas_call(observe_kernel, out_shape=jax.ShapeDtypeStruct((HALF, 128)...  1.5 us
    pallas_call x1, Pallas kernels, analyse_far(): pl.pallas_call(far_kernel, out_shape=[jax.ShapeDtypeStruct((V, MEMBERS, G...  1.31 us
    unnamed x12, local copies, waits for them, and re-layouts  1.29 us
  transfers between devices with their start and end apart: 9, of which 2 were waited for; matrix products, arithmetic and copies ran while one was open for 0% of the time, Pallas kernels for 10%

profile of v10, /device:TPU:0, one launch (start us, length us, event | category | flops | bytes accessed | tf_op | source)
XLA Modules:
  0.0 54.2 jit_solution(4951005741847823768)
XLA Ops:
  0.6 1.3 %copy-done = bf16[24,12,2048]{2,0,1:T(8,128)(2,1)S(1)} copy-done((bf16[24,12,2048]{2,0,1:T(8,128)(2,1)S(1)}, bf16[24,12,2048]{2,0,1:T(8,128)(2,1)}, u32[]{:S(2)}) %copy-start) | copy-done | bytes 1179672
  1.9 0.1 pack.1
  2.0 1.7 %collective-permute-start = (bf16[4,24,512]{2,1,0:T(8,128)(2,1)S(1)}, bf16[4,24,512]{2,1,0:T(8,128)(2,1)S(1)}, u32[]{:S(2)}, u32[]{:S(2)}) collective-permute-start(bf16[4,24,512]{2,1,0:T(8,128)(2,1)S(1)} %get-tuple-element.21), channel_id=1, source_target_pairs={{0,32},{32,64},{64,96},{96,0},{1,33},{33,65},{65,97},{97,1},{2,34}... | collective-permute-start | bytes 294920 | tf_op jit(solution)/shard_map/ppermute | solution.py:368
  3.8 2.9 %collective-permute-start.1 = (bf16[4,24,512]{2,1,0:T(8,128)(2,1)S(1)}, bf16[4,24,512]{2,1,0:T(8,128)(2,1)S(1)}, u32[]{:S(2)}, u32[]{:S(2)}) collective-permute-start(bf16[4,24,512]{2,1,0:T(8,128)(2,1)S(1)} %get-tuple-element.22), channel_id=1, source_target_pairs={{0,64},{32,96},{64,0},{96,32},{1,65},{33,97},{65,1},{97,33},{2,66}... | collective-permute-start | bytes 294920 | tf_op jit(solution)/shard_map/ppermute | solution.py:368
  6.7 1.3 %collective-permute-start.2 = (bf16[4,24,512]{2,1,0:T(8,128)(2,1)S(1)}, bf16[4,24,512]{2,1,0:T(8,128)(2,1)S(1)}, u32[]{:S(2)}, u32[]{:S(2)}) collective-permute-start(bf16[4,24,512]{2,1,0:T(8,128)(2,1)S(1)} %get-tuple-element.23), channel_id=1, source_target_pairs={{0,96},{32,0},{64,32},{96,64},{1,97},{33,1},{65,33},{97,65},{2,98}... | collective-permute-start | bytes 294920 | tf_op jit(solution)/shard_map/ppermute | solution.py:368
  8.0 0.9 %pack_bulk.1 = (bf16[23,24,512]{2,1,0:T(8,128)(2,1)}, bf16[23,24,512]{2,1,0:T(8,128)(2,1)S(1)}, bf16[23,24,512]{2,1,0:T(8,128)(2,1)S(1)}) custom-call(s32[1]{0:T(128)} %bitcast.2.me_ref, bf16[12,24,2048]{2,1,0:T(8,128)(2,1)S(1)} %bitcast.10, bf16[4,24,512]{2,1,0:T(8,128)(2,1)S(1)} %get-tuple-element.20.c0.after_ref), custom_call_target="tpu_custom_call" | custom-call | tf_op jit(solution)/shard_map/pack_bulk/pallas_call | solution.py:86
  9.0 0.7 %collective-permute-start.3 = (bf16[23,24,512]{2,1,0:T(8,128)(2,1)}, bf16[23,24,512]{2,1,0:T(8,128)(2,1)S(1)}, u32[]{:S(2)}, u32[]{:S(2)}) collective-permute-start(bf16[23,24,512]{2,1,0:T(8,128)(2,1)} %get-tuple-element.24), channel_id=1, source_target_pairs={{0,32},{32,64},{64,96},{96,0},{1,33},{33,65},{65,97},{97,1},{2,34}... | collective-permute-start | bytes 1695752 | tf_op jit(solution)/shard_map/ppermute | solution.py:368
  9.7 0.8 %collective-permute-start.4 = (bf16[23,24,512]{2,1,0:T(8,128)(2,1)S(1)}, bf16[23,24,512]{2,1,0:T(8,128)(2,1)S(1)}, u32[]{:S(2)}, u32[]{:S(2)}) collective-permute-start(bf16[23,24,512]{2,1,0:T(8,128)(2,1)S(1)} %get-tuple-element.25), channel_id=1, source_target_pairs={{0,64},{32,96},{64,0},{96,32},{1,65},{33,97},{65,1},{97,33},{2,66}... | collective-permute-start | bytes 1695752 | tf_op jit(solution)/shard_map/ppermute | solution.py:368
  10.5 2.0 %collective-permute-start.5 = (bf16[23,24,512]{2,1,0:T(8,128)(2,1)S(1)}, bf16[23,24,512]{2,1,0:T(8,128)(2,1)S(1)}, u32[]{:S(2)}, u32[]{:S(2)}) collective-permute-start(bf16[23,24,512]{2,1,0:T(8,128)(2,1)S(1)} %get-tuple-element.26), channel_id=1, source_target_pairs={{0,96},{32,0},{64,32},{96,64},{1,97},{33,1},{65,33},{97,65},{2,98}... | collective-permute-start | bytes 1695752 | tf_op jit(solution)/shard_map/ppermute | solution.py:368
  12.5 1.5 %observe.1 = f32[48,128]{1,0:T(8,128)S(1)} custom-call(s32[1]{0:T(128)} %bitcast.2.me_ref, s32[2,12]{1,0:T(2,128)S(1)} %bitcast.14, bf16[4,24,512]{2,1,0:T(8,128)(2,1)S(1)} %get-tuple-element.20.c0.after_ref, bf16[4,24,512]{2,1,0:T(8,128)(2,1)S(1)} %collective-permute-done.c1.o1, bf16[4,24,512]{2,1,0:T(8,128)(2,1)S(1)} %collective-permute-done.1.c2.o2, ...), custom_call_target="tpu_custom_call" | custom-call | tf_op jit(solution)/shard_map/observe/pallas_call | solution.py:163
  14.0 25.8 %conditional.1 = (f32[48,128]{1,0:T(8,128)S(1)}) conditional(s32[]{:T(128)} %convert_element_type.4, f32[48,128]{1,0:T(8,128)S(1)} %observe.1, f32[48,128]{1,0:T(8,128)S(1)} %observe.1), branch_computations={%region_0.0_spmd, %region_1.0_spmd} | conditional | bytes 589832 | solution.py:392
  14.1 0.1 spread_sum.3
  14.2 15.8 %all_to_all.8.parts_ref = bf16[16,48,128]{2,1,0:T(8,128)(2,1)S(1)} all-to-all(bf16[16,48,128]{2,1,0:T(8,128)(2,1)S(1)} %spread_sum.3), channel_id=1, replica_groups=mesh['member'=4,'x'=4,'z'=4,'core'=2] {'x','z'}, dimensions={0} | all-to-all | bytes 393216 | tf_op jit(solution)/shard_map/cond/branch_1_fun/all_to_all | solution.py:372
  29.9 0.2 spread_sum.4
  30.1 9.6 %all_to_all.9.parts_ref = bf16[8,48,128]{2,1,0:T(8,128)(2,1)S(1)} all-to-all(bf16[8,48,128]{2,1,0:T(8,128)(2,1)S(1)} %spread_sum.4), channel_id=1, replica_groups=mesh['member'=4,'x'=4,'z'=4,'core'=2] {'member','core'}, dimensions={0} | all-to-all | bytes 196608 | tf_op jit(solution)/shard_map/cond/branch_1_fun/all_to_all | solution.py:372
  39.8 1.5 %transform.1.w_ref = f32[96,96]{1,0:T(8,128)S(1)} custom-call(f32[48,128]{1,0:T(8,128)S(1)} %get-tuple-element.33.parts_ref), custom_call_target="tpu_custom_call" | custom-call | flops 40000000000 | tf_op jit(solution)/shard_map/transform/pallas_call | solution.py:244
  41.4 0.5 analyse_near.1
  41.9 0.6 %collective-permute-start.6 = (bf16[7,24,512]{2,1,0:T(8,128)(2,1)S(1)}, bf16[7,24,512]{2,1,0:T(8,128)(2,1)S(1)}, u32[]{:S(2)}, u32[]{:S(2)}) collective-permute-start(bf16[7,24,512]{2,1,0:T(8,128)(2,1)S(1)} %get-tuple-element.27), channel_id=1, source_target_pairs={{0,32},{32,64},{64,96},{96,0},{1,33},{33,65},{65,97},{97,1},{2,34}... | collective-permute-start | bytes 516104 | tf_op jit(solution)/shard_map/ppermute | solution.py:368
  42.5 2.0 %collective-permute-start.7 = (bf16[7,24,512]{2,1,0:T(8,128)(2,1)S(1)}, bf16[7,24,512]{2,1,0:T(8,128)(2,1)S(1)}, u32[]{:S(2)}, u32[]{:S(2)}) collective-permute-start(bf16[7,24,512]{2,1,0:T(8,128)(2,1)S(1)} %get-tuple-element.28), channel_id=1, source_target_pairs={{0,64},{32,96},{64,0},{96,32},{1,65},{33,97},{65,1},{97,33},{2,66}... | collective-permute-start | bytes 516104 | tf_op jit(solution)/shard_map/ppermute | solution.py:368
  44.5 0.9 %collective-permute-start.8 = (bf16[7,24,512]{2,1,0:T(8,128)(2,1)S(1)}, bf16[7,24,512]{2,1,0:T(8,128)(2,1)S(1)}, u32[]{:S(2)}, u32[]{:S(2)}) collective-permute-start(bf16[7,24,512]{2,1,0:T(8,128)(2,1)S(1)} %get-tuple-element.29), channel_id=1, source_target_pairs={{0,96},{32,0},{64,32},{96,64},{1,97},{33,1},{65,33},{97,65},{2,98}... | collective-permute-start | bytes 516104 | tf_op jit(solution)/shard_map/ppermute | solution.py:368
  45.5 1.3 %analyse_far.1 = (bf16[12,24,2048]{2,1,0:T(8,128)(2,1)}, f32[96,96]{1,0:T(8,128)}) custom-call(s32[1]{0:T(128)} %bitcast.2.me_ref, f32[96,96]{1,0:T(8,128)S(1)} %transform.1.w_ref, bf16[7,24,512]{2,1,0:T(8,128)(2,1)S(1)} %get-tuple-element.30.near_ref, bf16[12,24,2048]{2,1,0:T(8,128)(2,1)S(1)} %bitcast.12, ...), custom_call_target="tpu_custom_call" | custom-call | tf_op jit(solution)/shard_map/analyse_far/pallas_call | solution.py:320
  46.8 6.0 %collective-permute-done.6.c1 = bf16[7,24,512]{2,1,0:T(8,128)(2,1)S(1)} collective-permute-done((bf16[7,24,512]{2,1,0:T(8,128)(2,1)S(1)}, bf16[7,24,512]{2,1,0:T(8,128)(2,1)S(1)}, u32[]{:S(2)}, u32[]{:S(2)}) %collective-permute-start.6) | collective-permute-done | bytes 172064 | tf_op jit(solution)/shard_map/ppermute | solution.py:368
  52.8 0.6 %collective-permute-done.8.c3 = bf16[7,24,512]{2,1,0:T(8,128)(2,1)S(1)} collective-permute-done((bf16[7,24,512]{2,1,0:T(8,128)(2,1)S(1)}, bf16[7,24,512]{2,1,0:T(8,128)(2,1)S(1)}, u32[]{:S(2)}, u32[]{:S(2)}) %collective-permute-start.8) | collective-permute-done | bytes 172064 | tf_op jit(solution)/shard_map/ppermute | solution.py:368
  53.4 0.8 %place.1 = bf16[12,24,2048]{2,1,0:T(8,128)(2,1)} custom-call(s32[1]{0:T(128)} %bitcast.2.me_ref, bf16[7,24,512]{2,1,0:T(8,128)(2,1)S(1)} %collective-permute-done.6.c1, bf16[7,24,512]{2,1,0:T(8,128)(2,1)S(1)} %collective-permute-done.7.c2, bf16[7,24,512]{2,1,0:T(8,128)(2,1)S(1)} %collective-permute-done.8.c3, ...), custom_call_target="tpu_custom_call", output_to_operand_aliasing={{}: (4, {})} | custom-call | tf_op jit(solution)/shard_map/place/pallas_call | solution.py:351
  (19 shorter events, 0.1 us)
Async XLA Ops:
  0.6 1.3 %copy-start = (bf16[24,12,2048]{2,0,1:T(8,128)(2,1)S(1)}, bf16[24,12,2048]{2,0,1:T(8,128)(2,1)}, u32[]{:S(2)}) copy-start(bf16[24,12,2048]{2,0,1:T(8,128)(2,1)} %param.7) | copy-start | bytes 3538948
  1.9 10.6 %copy-start.2 = (bf16[12,1,2,128,128]{4,3,2,1,0:T(8,128)(2,1)S(1)}, bf16[12,1,2,128,128]{4,3,2,1,0:T(8,128)(2,1)}, u32[]{:S(2)}) copy-start(bf16[12,1,2,128,128]{4,3,2,1,0:T(8,128)(2,1)} %param.10) | copy-start | bytes 2359300
  1.9 10.6 %copy-start.3 = (f32[12,1,128]{2,1,0:T(1,128)S(1)}, f32[12,1,128]{2,1,0:T(1,128)}, u32[]{:S(2)}) copy-start(f32[12,1,128]{2,1,0:T(1,128)} %y_ref.1) | copy-start | bytes 18436
  1.9 10.6 %copy-start.4 = (f32[12,1,128]{2,1,0:T(1,128)S(1)}, f32[12,1,128]{2,1,0:T(1,128)}, u32[]{:S(2)}) copy-start(f32[12,1,128]{2,1,0:T(1,128)} %var_ref.1) | copy-start | bytes 18436
  1.9 10.6 %copy-start.5 = (s32[12,1,2]{0,2,1:T(2,128)S(1)}, s32[12,1,2]{0,2,1:T(2,128)}, u32[]{:S(2)}) copy-start(s32[12,1,2]{0,2,1:T(2,128)} %param.11) | copy-start | bytes 292
  2.0 8.5 %collective-permute-start = (bf16[4,24,512]{2,1,0:T(8,128)(2,1)S(1)}, bf16[4,24,512]{2,1,0:T(8,128)(2,1)S(1)}, u32[]{:S(2)}, u32[]{:S(2)}) collective-permute-start(bf16[4,24,512]{2,1,0:T(8,128)(2,1)S(1)} %get-tuple-element.21), channel_id=1, source_target_pairs={{0,32},{32,64},{64,96},{96,0},{1,33},{33,65},{65,97},{97,1},{2,34}... | collective-permute-start | bytes 294920 | tf_op jit(solution)/shard_map/ppermute | solution.py:368
  3.8 8.7 %collective-permute-start.1 = (bf16[4,24,512]{2,1,0:T(8,128)(2,1)S(1)}, bf16[4,24,512]{2,1,0:T(8,128)(2,1)S(1)}, u32[]{:S(2)}, u32[]{:S(2)}) collective-permute-start(bf16[4,24,512]{2,1,0:T(8,128)(2,1)S(1)} %get-tuple-element.22), channel_id=1, source_target_pairs={{0,64},{32,96},{64,0},{96,32},{1,65},{33,97},{65,1},{97,33},{2,66}... | collective-permute-start | bytes 294920 | tf_op jit(solution)/shard_map/ppermute | solution.py:368
  6.7 5.8 %collective-permute-start.2 = (bf16[4,24,512]{2,1,0:T(8,128)(2,1)S(1)}, bf16[4,24,512]{2,1,0:T(8,128)(2,1)S(1)}, u32[]{:S(2)}, u32[]{:S(2)}) collective-permute-start(bf16[4,24,512]{2,1,0:T(8,128)(2,1)S(1)} %get-tuple-element.23), channel_id=1, source_target_pairs={{0,96},{32,0},{64,32},{96,64},{1,97},{33,1},{65,33},{97,65},{2,98}... | collective-permute-start | bytes 294920 | tf_op jit(solution)/shard_map/ppermute | solution.py:368
  9.0 32.4 %collective-permute-start.3 = (bf16[23,24,512]{2,1,0:T(8,128)(2,1)}, bf16[23,24,512]{2,1,0:T(8,128)(2,1)S(1)}, u32[]{:S(2)}, u32[]{:S(2)}) collective-permute-start(bf16[23,24,512]{2,1,0:T(8,128)(2,1)} %get-tuple-element.24), channel_id=1, source_target_pairs={{0,32},{32,64},{64,96},{96,0},{1,33},{33,65},{65,97},{97,1},{2,34}... | collective-permute-start | bytes 1695752 | tf_op jit(solution)/shard_map/ppermute | solution.py:368
  9.7 31.6 %collective-permute-start.4 = (bf16[23,24,512]{2,1,0:T(8,128)(2,1)S(1)}, bf16[23,24,512]{2,1,0:T(8,128)(2,1)S(1)}, u32[]{:S(2)}, u32[]{:S(2)}) collective-permute-start(bf16[23,24,512]{2,1,0:T(8,128)(2,1)S(1)} %get-tuple-element.25), channel_id=1, source_target_pairs={{0,64},{32,96},{64,0},{96,32},{1,65},{33,97},{65,1},{97,33},{2,66}... | collective-permute-start | bytes 1695752 | tf_op jit(solution)/shard_map/ppermute | solution.py:368
  10.5 30.9 %collective-permute-start.5 = (bf16[23,24,512]{2,1,0:T(8,128)(2,1)S(1)}, bf16[23,24,512]{2,1,0:T(8,128)(2,1)S(1)}, u32[]{:S(2)}, u32[]{:S(2)}) collective-permute-start(bf16[23,24,512]{2,1,0:T(8,128)(2,1)S(1)} %get-tuple-element.26), channel_id=1, source_target_pairs={{0,96},{32,0},{64,32},{96,64},{1,97},{33,1},{65,33},{97,65},{2,98}... | collective-permute-start | bytes 1695752 | tf_op jit(solution)/shard_map/ppermute | solution.py:368
  39.8 1.6 %copy-start.1 = (bf16[24,12,2048]{2,0,1:T(8,128)(2,1)S(1)}, bf16[24,12,2048]{2,0,1:T(8,128)(2,1)}, u32[]{:S(2)}) copy-start(bf16[24,12,2048]{2,0,1:T(8,128)(2,1)} %param.7) | copy-start | bytes 3538948
  41.9 10.9 %collective-permute-start.6 = (bf16[7,24,512]{2,1,0:T(8,128)(2,1)S(1)}, bf16[7,24,512]{2,1,0:T(8,128)(2,1)S(1)}, u32[]{:S(2)}, u32[]{:S(2)}) collective-permute-start(bf16[7,24,512]{2,1,0:T(8,128)(2,1)S(1)} %get-tuple-element.27), channel_id=1, source_target_pairs={{0,32},{32,64},{64,96},{96,0},{1,33},{33,65},{65,97},{97,1},{2,34}... | collective-permute-start | bytes 516104 | tf_op jit(solution)/shard_map/ppermute | solution.py:368
  42.5 10.3 %collective-permute-start.7 = (bf16[7,24,512]{2,1,0:T(8,128)(2,1)S(1)}, bf16[7,24,512]{2,1,0:T(8,128)(2,1)S(1)}, u32[]{:S(2)}, u32[]{:S(2)}) collective-permute-start(bf16[7,24,512]{2,1,0:T(8,128)(2,1)S(1)} %get-tuple-element.28), channel_id=1, source_target_pairs={{0,64},{32,96},{64,0},{96,32},{1,65},{33,97},{65,1},{97,33},{2,66}... | collective-permute-start | bytes 516104 | tf_op jit(solution)/shard_map/ppermute | solution.py:368
  44.5 8.9 %collective-permute-start.8 = (bf16[7,24,512]{2,1,0:T(8,128)(2,1)S(1)}, bf16[7,24,512]{2,1,0:T(8,128)(2,1)S(1)}, u32[]{:S(2)}, u32[]{:S(2)}) collective-permute-start(bf16[7,24,512]{2,1,0:T(8,128)(2,1)S(1)} %get-tuple-element.29), channel_id=1, source_target_pairs={{0,96},{32,0},{64,32},{96,64},{1,97},{33,1},{65,33},{97,65},{2,98}... | collective-permute-start | bytes 516104 | tf_op jit(solution)/shard_map/ppermute | solution.py:368

commit v11 on v10

--- a/solution.py
+++ b/solution.py
@@ -156,13 +156,15 @@
     both = dot_rows(jnp.concatenate([high, low], axis=0), spread_high)
     gram = both[:K] + both[K:] + dot_rows(high, spread_low)
     projected = jnp.sum(projected, axis=1, keepdims=True)
-    out_ref[...] = fold(jnp.concatenate([gram, projected, jnp.zeros((K, 127 - K), jnp.float32)], axis=1))
+    folded = narrow(fold(jnp.concatenate([gram, projected, jnp.zeros((K, 127 - K), jnp.float32)], axis=1)))
+    for copy in range(PLANE):
+        out_ref[copy] = folded
 
 
 def observe(me, slots, chunks, op, values, variances):
     return pl.pallas_call(
         observe_kernel,
-        out_shape=jax.ShapeDtypeStruct((HALF, 128), jnp.float32),
+        out_shape=jax.ShapeDtypeStruct((PLANE, HALF, 128), jnp.bfloat16),
         in_specs=[SMEM, SMEM] + [VMEM] * 7,
         out_specs=VMEM,
         scratch_shapes=[pltpu.VMEM((VOBS * TILE // 128, K, 128), jnp.float32)],
@@ -195,12 +197,15 @@
     return jnp.where(lane == row, out + total[:, K + 6 : K + 7], out)
 
 
-def spread_kernel(parts_ref, out_ref):
+def sum_parts(parts_ref):
     total = parts_ref[0].astype(jnp.float32)
     for part in range(1, parts_ref.shape[0]):
         total = total + parts_ref[part].astype(jnp.float32)
-    if parts_ref.dtype == jnp.bfloat16:
-        total = widen(total)
+    return widen(total) if parts_ref.dtype == jnp.bfloat16 else total
+
+
+def spread_kernel(parts_ref, out_ref):
+    total = sum_parts(parts_ref)
     if out_ref.dtype == jnp.bfloat16:
         total = narrow(total)
     for copy in range(out_ref.shape[0]):
@@ -219,7 +224,7 @@
 
 
 def transform_kernel(parts_ref, weights_ref):
-    folded = parts_ref[...]
+    folded = sum_parts(parts_ref)
     gram, projected = unfold(folded)
     row = lax.broadcasted_iota(jnp.int32, (K, K), 0)
     col = lax.broadcasted_iota(jnp.int32, (K, K), 1)
@@ -372,10 +377,10 @@
     return lax.all_to_all(copies, axes, 0, 0, tiled=True)
 
 
-def total(folded):
-    copies = exchange(spread_sum(folded[None], PLANE, jnp.bfloat16), ("x", "z"))
+def total(copies):
+    copies = exchange(copies, ("x", "z"))
     copies = exchange(spread_sum(copies, COLUMN, jnp.bfloat16), ("member", "core"))
-    return spread_sum(copies, 1)[0]
+    return copies
 
 
 def body(prior, readings, error_spread, mapping, slots):
@@ -389,7 +394,9 @@
     folded = observe(
         me, jnp.transpose(slots, (1, 2, 0))[0], [packed[0]] + observed, mapping[:, 0], readings, error_spread
     )
-    folded = lax.cond(always, total, lambda x: x, folded)
+    folded = lax.cond(
+        always, total, lambda x: jnp.zeros((COLUMN, HALF, 128), jnp.bfloat16), folded
+    )
     weights = transform(folded)
     near = analyse_near(me, weights, prior, observed, bulk)
     arrived = scatter(near[1:])

time: 54.4 us -> 54.4 us (level)
  no operation moved by 1% of the time
where the time goes in v11:
time: 54.4 us; the launch traced here: 54.2 us
  blocking collectives  25.3 us (47%)
  starting transfers between devices  13.1 us (24%)
  Pallas kernels  7.05 us (13%)
  waiting for transfers between devices  6.66 us (12%)
  local copies, waits for them, and re-layouts  1.28 us (2%)
  between operations  0.75 us (1%)
    all_to_all x2, blocking collectives, exchange(): return lax.all_to_all(copies, axes, 0, 0, tiled=True)  25.3 us
    ppermute x9, starting transfers between devices, scatter(): lax.ppermute(chunk, 'member', ring(s))  13.1 us
    ppermute x9, waiting for transfers between devices, scatter(): lax.ppermute(chunk, 'member', ring(s))  6.66 us
    pallas_call x1, Pallas kernels, observe(): pl.pallas_call(observe_kernel, out_shape=jax.ShapeDtypeStruct((PLANE, HAL...  1.61 us
    pallas_call x1, Pallas kernels, transform(): pl.pallas_call(transform_kernel, out_shape=jax.ShapeDtypeStruct((K, K), j...  1.61 us
    pallas_call x1, Pallas kernels, analyse_far(): pl.pallas_call(far_kernel, out_shape=[jax.ShapeDtypeStruct((V, MEMBERS, G...  1.31 us
    unnamed x12, local copies, waits for them, and re-layouts  1.28 us
  transfers between devices with their start and end apart: 9, of which 2 were waited for; matrix products, arithmetic and copies ran while one was open for 0% of the time, Pallas kernels for 10%

profile of v11, /device:TPU:0, one launch (start us, length us, event | category | flops | bytes accessed | tf_op | source)
XLA Modules:
  0.0 54.2 jit_solution(17399354231492300564)
XLA Ops:
  0.6 0.0 copy-start
  0.6 1.3 %copy-done = bf16[24,12,2048]{2,0,1:T(8,128)(2,1)S(1)} copy-done((bf16[24,12,2048]{2,0,1:T(8,128)(2,1)S(1)}, bf16[24,12,2048]{2,0,1:T(8,128)(2,1)}, u32[]{:S(2)}) %copy-start) | copy-done | bytes 1179672
  1.9 0.1 pack.1
  2.0 1.7 %collective-permute-start = (bf16[4,24,512]{2,1,0:T(8,128)(2,1)S(1)}, bf16[4,24,512]{2,1,0:T(8,128)(2,1)S(1)}, u32[]{:S(2)}, u32[]{:S(2)}) collective-permute-start(bf16[4,24,512]{2,1,0:T(8,128)(2,1)S(1)} %get-tuple-element.20), channel_id=1, source_target_pairs={{0,32},{32,64},{64,96},{96,0},{1,33},{33,65},{65,97},{97,1},{2,34}... | collective-permute-start | bytes 294920 | tf_op jit(solution)/shard_map/ppermute | solution.py:373
  3.8 2.9 %collective-permute-start.1 = (bf16[4,24,512]{2,1,0:T(8,128)(2,1)S(1)}, bf16[4,24,512]{2,1,0:T(8,128)(2,1)S(1)}, u32[]{:S(2)}, u32[]{:S(2)}) collective-permute-start(bf16[4,24,512]{2,1,0:T(8,128)(2,1)S(1)} %get-tuple-element.21), channel_id=1, source_target_pairs={{0,64},{32,96},{64,0},{96,32},{1,65},{33,97},{65,1},{97,33},{2,66}... | collective-permute-start | bytes 294920 | tf_op jit(solution)/shard_map/ppermute | solution.py:373
  6.7 1.3 %collective-permute-start.2 = (bf16[4,24,512]{2,1,0:T(8,128)(2,1)S(1)}, bf16[4,24,512]{2,1,0:T(8,128)(2,1)S(1)}, u32[]{:S(2)}, u32[]{:S(2)}) collective-permute-start(bf16[4,24,512]{2,1,0:T(8,128)(2,1)S(1)} %get-tuple-element.22), channel_id=1, source_target_pairs={{0,96},{32,0},{64,32},{96,64},{1,97},{33,1},{65,33},{97,65},{2,98}... | collective-permute-start | bytes 294920 | tf_op jit(solution)/shard_map/ppermute | solution.py:373
  8.0 0.9 %pack_bulk.1 = (bf16[23,24,512]{2,1,0:T(8,128)(2,1)}, bf16[23,24,512]{2,1,0:T(8,128)(2,1)S(1)}, bf16[23,24,512]{2,1,0:T(8,128)(2,1)S(1)}) custom-call(s32[1]{0:T(128)} %bitcast.me_ref, bf16[12,24,2048]{2,1,0:T(8,128)(2,1)S(1)} %bitcast.8, bf16[4,24,512]{2,1,0:T(8,128)(2,1)S(1)} %get-tuple-element.19.c0.after_ref), custom_call_target="tpu_custom_call" | custom-call | tf_op jit(solution)/shard_map/pack_bulk/pallas_call | solution.py:86
  9.0 0.7 %collective-permute-start.3 = (bf16[23,24,512]{2,1,0:T(8,128)(2,1)}, bf16[23,24,512]{2,1,0:T(8,128)(2,1)S(1)}, u32[]{:S(2)}, u32[]{:S(2)}) collective-permute-start(bf16[23,24,512]{2,1,0:T(8,128)(2,1)} %get-tuple-element.23), channel_id=1, source_target_pairs={{0,32},{32,64},{64,96},{96,0},{1,33},{33,65},{65,97},{97,1},{2,34}... | collective-permute-start | bytes 1695752 | tf_op jit(solution)/shard_map/ppermute | solution.py:373
  9.7 0.8 %collective-permute-start.4 = (bf16[23,24,512]{2,1,0:T(8,128)(2,1)S(1)}, bf16[23,24,512]{2,1,0:T(8,128)(2,1)S(1)}, u32[]{:S(2)}, u32[]{:S(2)}) collective-permute-start(bf16[23,24,512]{2,1,0:T(8,128)(2,1)S(1)} %get-tuple-element.24), channel_id=1, source_target_pairs={{0,64},{32,96},{64,0},{96,32},{1,65},{33,97},{65,1},{97,33},{2,66}... | collective-permute-start | bytes 1695752 | tf_op jit(solution)/shard_map/ppermute | solution.py:373
  10.5 2.0 %collective-permute-start.5 = (bf16[23,24,512]{2,1,0:T(8,128)(2,1)S(1)}, bf16[23,24,512]{2,1,0:T(8,128)(2,1)S(1)}, u32[]{:S(2)}, u32[]{:S(2)}) collective-permute-start(bf16[23,24,512]{2,1,0:T(8,128)(2,1)S(1)} %get-tuple-element.25), channel_id=1, source_target_pairs={{0,96},{32,0},{64,32},{96,64},{1,97},{33,1},{65,33},{97,65},{2,98}... | collective-permute-start | bytes 1695752 | tf_op jit(solution)/shard_map/ppermute | solution.py:373
  12.5 1.6 %observe.1 = bf16[16,48,128]{2,1,0:T(8,128)(2,1)S(1)} custom-call(s32[1]{0:T(128)} %bitcast.me_ref, s32[2,12]{1,0:T(2,128)S(1)} %bitcast.12, bf16[4,24,512]{2,1,0:T(8,128)(2,1)S(1)} %get-tuple-element.19.c0.after_ref, bf16[4,24,512]{2,1,0:T(8,128)(2,1)S(1)} %collective-permute-done.c1.o1, bf16[4,24,512]{2,1,0:T(8,128)(2,1)S(1)} %collective-permute-done.1.c2.o2, ...), custom_call_target="tpu_custom_call" | custom-call | tf_op jit(solution)/shard_map/observe/pallas_call | solution.py:165
  14.1 25.6 %conditional.1 = (bf16[8,48,128]{2,1,0:T(8,128)(2,1)S(1)}) conditional(s32[]{:T(128)} %convert_element_type.4, () %tuple.14, bf16[16,48,128]{2,1,0:T(8,128)(2,1)S(1)} %observe.1), branch_computations={%region_0.0_spmd, %region_1.0_spmd} | conditional | bytes 589832 | solution.py:397
  14.1 15.8 %all_to_all.8.parts_ref = bf16[16,48,128]{2,1,0:T(8,128)(2,1)S(1)} all-to-all(bf16[16,48,128]{2,1,0:T(8,128)(2,1)S(1)} %param.1), channel_id=1, replica_groups=mesh['member'=4,'x'=4,'z'=4,'core'=2] {'x','z'}, dimensions={0} | all-to-all | bytes 393216 | tf_op jit(solution)/shard_map/cond/branch_1_fun/all_to_all | solution.py:377
  29.9 0.2 spread_sum.1
  30.1 9.6 %all_to_all.9 = bf16[8,48,128]{2,1,0:T(8,128)(2,1)S(1)} all-to-all(bf16[8,48,128]{2,1,0:T(8,128)(2,1)S(1)} %spread_sum.1), channel_id=1, replica_groups=mesh['member'=4,'x'=4,'z'=4,'core'=2] {'member','core'}, dimensions={0} | all-to-all | bytes 196608 | tf_op jit(solution)/shard_map/cond/branch_1_fun/all_to_all | solution.py:377
  39.7 1.6 %transform.1.w_ref = f32[96,96]{1,0:T(8,128)S(1)} custom-call(bf16[8,48,128]{2,1,0:T(8,128)(2,1)S(1)} %get-tuple-element.32.parts_ref), custom_call_target="tpu_custom_call" | custom-call | flops 40000000000 | tf_op jit(solution)/shard_map/transform/pallas_call | solution.py:249
  41.4 0.5 analyse_near.1
  41.8 0.6 %collective-permute-start.6 = (bf16[7,24,512]{2,1,0:T(8,128)(2,1)S(1)}, bf16[7,24,512]{2,1,0:T(8,128)(2,1)S(1)}, u32[]{:S(2)}, u32[]{:S(2)}) collective-permute-start(bf16[7,24,512]{2,1,0:T(8,128)(2,1)S(1)} %get-tuple-element.26), channel_id=1, source_target_pairs={{0,32},{32,64},{64,96},{96,0},{1,33},{33,65},{65,97},{97,1},{2,34}... | collective-permute-start | bytes 516104 | tf_op jit(solution)/shard_map/ppermute | solution.py:373
  42.5 2.1 %collective-permute-start.7 = (bf16[7,24,512]{2,1,0:T(8,128)(2,1)S(1)}, bf16[7,24,512]{2,1,0:T(8,128)(2,1)S(1)}, u32[]{:S(2)}, u32[]{:S(2)}) collective-permute-start(bf16[7,24,512]{2,1,0:T(8,128)(2,1)S(1)} %get-tuple-element.27), channel_id=1, source_target_pairs={{0,64},{32,96},{64,0},{96,32},{1,65},{33,97},{65,1},{97,33},{2,66}... | collective-permute-start | bytes 516104 | tf_op jit(solution)/shard_map/ppermute | solution.py:373
  44.5 0.9 %collective-permute-start.8 = (bf16[7,24,512]{2,1,0:T(8,128)(2,1)S(1)}, bf16[7,24,512]{2,1,0:T(8,128)(2,1)S(1)}, u32[]{:S(2)}, u32[]{:S(2)}) collective-permute-start(bf16[7,24,512]{2,1,0:T(8,128)(2,1)S(1)} %get-tuple-element.28), channel_id=1, source_target_pairs={{0,96},{32,0},{64,32},{96,64},{1,97},{33,1},{65,33},{97,65},{2,98}... | collective-permute-start | bytes 516104 | tf_op jit(solution)/shard_map/ppermute | solution.py:373
  45.4 1.3 %analyse_far.1 = (bf16[12,24,2048]{2,1,0:T(8,128)(2,1)}, f32[96,96]{1,0:T(8,128)}) custom-call(s32[1]{0:T(128)} %bitcast.me_ref, f32[96,96]{1,0:T(8,128)S(1)} %transform.1.w_ref, bf16[7,24,512]{2,1,0:T(8,128)(2,1)S(1)} %get-tuple-element.29.near_ref, bf16[12,24,2048]{2,1,0:T(8,128)(2,1)S(1)} %bitcast.10, bf16[23,24,512]{2,1,0:T(8,128)(2,1)S(1)} %collective-permute-done.3.b1, ...), custom_call_target="tpu_custom_call" | custom-call | tf_op jit(solution)/shard_map/analyse_far/pallas_call | solution.py:325
  46.8 6.0 %collective-permute-done.6.c1 = bf16[7,24,512]{2,1,0:T(8,128)(2,1)S(1)} collective-permute-done((bf16[7,24,512]{2,1,0:T(8,128)(2,1)S(1)}, bf16[7,24,512]{2,1,0:T(8,128)(2,1)S(1)}, u32[]{:S(2)}, u32[]{:S(2)}) %collective-permute-start.6) | collective-permute-done | bytes 172064 | tf_op jit(solution)/shard_map/ppermute | solution.py:373
  52.8 0.6 %collective-permute-done.8.c3 = bf16[7,24,512]{2,1,0:T(8,128)(2,1)S(1)} collective-permute-done((bf16[7,24,512]{2,1,0:T(8,128)(2,1)S(1)}, bf16[7,24,512]{2,1,0:T(8,128)(2,1)S(1)}, u32[]{:S(2)}, u32[]{:S(2)}) %collective-permute-start.8) | collective-permute-done | bytes 172064 | tf_op jit(solution)/shard_map/ppermute | solution.py:373
  53.4 0.8 %place.1 = bf16[12,24,2048]{2,1,0:T(8,128)(2,1)} custom-call(s32[1]{0:T(128)} %bitcast.me_ref, bf16[7,24,512]{2,1,0:T(8,128)(2,1)S(1)} %collective-permute-done.6.c1, bf16[7,24,512]{2,1,0:T(8,128)(2,1)S(1)} %collective-permute-done.7.c2, bf16[7,24,512]{2,1,0:T(8,128)(2,1)S(1)} %collective-permute-done.8.c3, ...), custom_call_target="tpu_custom_call", output_to_operand_aliasing={{}: (4, {})} | custom-call | tf_op jit(solution)/shard_map/place/pallas_call | solution.py:356
  (17 shorter events, 0.0 us)
Async XLA Ops:
  0.6 1.3 %copy-start = (bf16[24,12,2048]{2,0,1:T(8,128)(2,1)S(1)}, bf16[24,12,2048]{2,0,1:T(8,128)(2,1)}, u32[]{:S(2)}) copy-start(bf16[24,12,2048]{2,0,1:T(8,128)(2,1)} %param.7) | copy-start | bytes 3538948
  1.9 10.6 %copy-start.2 = (bf16[12,1,2,128,128]{4,3,2,1,0:T(8,128)(2,1)S(1)}, bf16[12,1,2,128,128]{4,3,2,1,0:T(8,128)(2,1)}, u32[]{:S(2)}) copy-start(bf16[12,1,2,128,128]{4,3,2,1,0:T(8,128)(2,1)} %param.10) | copy-start | bytes 2359300
  1.9 10.6 %copy-start.3 = (f32[12,1,128]{2,1,0:T(1,128)S(1)}, f32[12,1,128]{2,1,0:T(1,128)}, u32[]{:S(2)}) copy-start(f32[12,1,128]{2,1,0:T(1,128)} %y_ref.1) | copy-start | bytes 18436
  1.9 10.6 %copy-start.4 = (f32[12,1,128]{2,1,0:T(1,128)S(1)}, f32[12,1,128]{2,1,0:T(1,128)}, u32[]{:S(2)}) copy-start(f32[12,1,128]{2,1,0:T(1,128)} %var_ref.1) | copy-start | bytes 18436
  1.9 10.6 %copy-start.5 = (s32[12,1,2]{0,2,1:T(2,128)S(1)}, s32[12,1,2]{0,2,1:T(2,128)}, u32[]{:S(2)}) copy-start(s32[12,1,2]{0,2,1:T(2,128)} %param.11) | copy-start | bytes 292
  2.0 8.5 %collective-permute-start = (bf16[4,24,512]{2,1,0:T(8,128)(2,1)S(1)}, bf16[4,24,512]{2,1,0:T(8,128)(2,1)S(1)}, u32[]{:S(2)}, u32[]{:S(2)}) collective-permute-start(bf16[4,24,512]{2,1,0:T(8,128)(2,1)S(1)} %get-tuple-element.20), channel_id=1, source_target_pairs={{0,32},{32,64},{64,96},{96,0},{1,33},{33,65},{65,97},{97,1},{2,34}... | collective-permute-start | bytes 294920 | tf_op jit(solution)/shard_map/ppermute | solution.py:373
  3.8 8.7 %collective-permute-start.1 = (bf16[4,24,512]{2,1,0:T(8,128)(2,1)S(1)}, bf16[4,24,512]{2,1,0:T(8,128)(2,1)S(1)}, u32[]{:S(2)}, u32[]{:S(2)}) collective-permute-start(bf16[4,24,512]{2,1,0:T(8,128)(2,1)S(1)} %get-tuple-element.21), channel_id=1, source_target_pairs={{0,64},{32,96},{64,0},{96,32},{1,65},{33,97},{65,1},{97,33},{2,66}... | collective-permute-start | bytes 294920 | tf_op jit(solution)/shard_map/ppermute | solution.py:373
  6.7 5.8 %collective-permute-start.2 = (bf16[4,24,512]{2,1,0:T(8,128)(2,1)S(1)}, bf16[4,24,512]{2,1,0:T(8,128)(2,1)S(1)}, u32[]{:S(2)}, u32[]{:S(2)}) collective-permute-start(bf16[4,24,512]{2,1,0:T(8,128)(2,1)S(1)} %get-tuple-element.22), channel_id=1, source_target_pairs={{0,96},{32,0},{64,32},{96,64},{1,97},{33,1},{65,33},{97,65},{2,98}... | collective-permute-start | bytes 294920 | tf_op jit(solution)/shard_map/ppermute | solution.py:373
  9.0 32.3 %collective-permute-start.3 = (bf16[23,24,512]{2,1,0:T(8,128)(2,1)}, bf16[23,24,512]{2,1,0:T(8,128)(2,1)S(1)}, u32[]{:S(2)}, u32[]{:S(2)}) collective-permute-start(bf16[23,24,512]{2,1,0:T(8,128)(2,1)} %get-tuple-element.23), channel_id=1, source_target_pairs={{0,32},{32,64},{64,96},{96,0},{1,33},{33,65},{65,97},{97,1},{2,34}... | collective-permute-start | bytes 1695752 | tf_op jit(solution)/shard_map/ppermute | solution.py:373
  9.7 31.6 %collective-permute-start.4 = (bf16[23,24,512]{2,1,0:T(8,128)(2,1)S(1)}, bf16[23,24,512]{2,1,0:T(8,128)(2,1)S(1)}, u32[]{:S(2)}, u32[]{:S(2)}) collective-permute-start(bf16[23,24,512]{2,1,0:T(8,128)(2,1)S(1)} %get-tuple-element.24), channel_id=1, source_target_pairs={{0,64},{32,96},{64,0},{96,32},{1,65},{33,97},{65,1},{97,33},{2,66}... | collective-permute-start | bytes 1695752 | tf_op jit(solution)/shard_map/ppermute | solution.py:373
  10.5 30.8 %collective-permute-start.5 = (bf16[23,24,512]{2,1,0:T(8,128)(2,1)S(1)}, bf16[23,24,512]{2,1,0:T(8,128)(2,1)S(1)}, u32[]{:S(2)}, u32[]{:S(2)}) collective-permute-start(bf16[23,24,512]{2,1,0:T(8,128)(2,1)S(1)} %get-tuple-element.25), channel_id=1, source_target_pairs={{0,96},{32,0},{64,32},{96,64},{1,97},{33,1},{65,33},{97,65},{2,98}... | collective-permute-start | bytes 1695752 | tf_op jit(solution)/shard_map/ppermute | solution.py:373
  39.7 1.6 %copy-start.1 = (bf16[24,12,2048]{2,0,1:T(8,128)(2,1)S(1)}, bf16[24,12,2048]{2,0,1:T(8,128)(2,1)}, u32[]{:S(2)}) copy-start(bf16[24,12,2048]{2,0,1:T(8,128)(2,1)} %param.7) | copy-start | bytes 3538948
  41.8 10.9 %collective-permute-start.6 = (bf16[7,24,512]{2,1,0:T(8,128)(2,1)S(1)}, bf16[7,24,512]{2,1,0:T(8,128)(2,1)S(1)}, u32[]{:S(2)}, u32[]{:S(2)}) collective-permute-start(bf16[7,24,512]{2,1,0:T(8,128)(2,1)S(1)} %get-tuple-element.26), channel_id=1, source_target_pairs={{0,32},{32,64},{64,96},{96,0},{1,33},{33,65},{65,97},{97,1},{2,34}... | collective-permute-start | bytes 516104 | tf_op jit(solution)/shard_map/ppermute | solution.py:373
  42.5 10.3 %collective-permute-start.7 = (bf16[7,24,512]{2,1,0:T(8,128)(2,1)S(1)}, bf16[7,24,512]{2,1,0:T(8,128)(2,1)S(1)}, u32[]{:S(2)}, u32[]{:S(2)}) collective-permute-start(bf16[7,24,512]{2,1,0:T(8,128)(2,1)S(1)} %get-tuple-element.27), channel_id=1, source_target_pairs={{0,64},{32,96},{64,0},{96,32},{1,65},{33,97},{65,1},{97,33},{2,66}... | collective-permute-start | bytes 516104 | tf_op jit(solution)/shard_map/ppermute | solution.py:373
  44.5 8.9 %collective-permute-start.8 = (bf16[7,24,512]{2,1,0:T(8,128)(2,1)S(1)}, bf16[7,24,512]{2,1,0:T(8,128)(2,1)S(1)}, u32[]{:S(2)}, u32[]{:S(2)}) collective-permute-start(bf16[7,24,512]{2,1,0:T(8,128)(2,1)S(1)} %get-tuple-element.28), channel_id=1, source_target_pairs={{0,96},{32,0},{64,32},{96,64},{1,97},{33,1},{65,33},{97,65},{2,98}... | collective-permute-start | bytes 516104 | tf_op jit(solution)/shard_map/ppermute | solution.py:373

commit v12 on v11

--- a/solution.py
+++ b/solution.py
@@ -156,15 +156,13 @@
     both = dot_rows(jnp.concatenate([high, low], axis=0), spread_high)
     gram = both[:K] + both[K:] + dot_rows(high, spread_low)
     projected = jnp.sum(projected, axis=1, keepdims=True)
-    folded = narrow(fold(jnp.concatenate([gram, projected, jnp.zeros((K, 127 - K), jnp.float32)], axis=1)))
-    for copy in range(PLANE):
-        out_ref[copy] = folded
+    out_ref[...] = fold(jnp.concatenate([gram, projected, jnp.zeros((K, 127 - K), jnp.float32)], axis=1))
 
 
 def observe(me, slots, chunks, op, values, variances):
     return pl.pallas_call(
         observe_kernel,
-        out_shape=jax.ShapeDtypeStruct((PLANE, HALF, 128), jnp.bfloat16),
+        out_shape=jax.ShapeDtypeStruct((HALF, 128), jnp.float32),
         in_specs=[SMEM, SMEM] + [VMEM] * 7,
         out_specs=VMEM,
         scratch_shapes=[pltpu.VMEM((VOBS * TILE // 128, K, 128), jnp.float32)],
@@ -377,8 +375,8 @@
     return lax.all_to_all(copies, axes, 0, 0, tiled=True)
 
 
-def total(copies):
-    copies = exchange(copies, ("x", "z"))
+def total(folded):
+    copies = exchange(spread_sum(folded[None], PLANE, jnp.bfloat16), ("x", "z"))
     copies = exchange(spread_sum(copies, COLUMN, jnp.bfloat16), ("member", "core"))
     return copies
 

time: 54.4 us -> 54.4 us (level)
  no operation moved by 1% of the time
where the time goes in v12:
time: 54.4 us; the launch traced here: 54.2 us
  blocking collectives  25.4 us (47%)
  starting transfers between devices  13.1 us (24%)
  Pallas kernels  7.04 us (13%)
  waiting for transfers between devices  6.66 us (12%)
  local copies, waits for them, and re-layouts  1.28 us (2%)
  between operations  0.76 us (1%)
    all_to_all x2, blocking collectives, exchange(): return lax.all_to_all(copies, axes, 0, 0, tiled=True)  25.4 us
    ppermute x9, starting transfers between devices, scatter(): lax.ppermute(chunk, 'member', ring(s))  13.1 us
    ppermute x9, waiting for transfers between devices, scatter(): lax.ppermute(chunk, 'member', ring(s))  6.66 us
    pallas_call x1, Pallas kernels, transform(): pl.pallas_call(transform_kernel, out_shape=jax.ShapeDtypeStruct((K, K), j...  1.61 us
    pallas_call x1, Pallas kernels, observe(): pl.pallas_call(observe_kernel, out_shape=jax.ShapeDtypeStruct((HALF, 128)...  1.5 us
    pallas_call x1, Pallas kernels, analyse_far(): pl.pallas_call(far_kernel, out_shape=[jax.ShapeDtypeStruct((V, MEMBERS, G...  1.31 us
    unnamed x12, local copies, waits for them, and re-layouts  1.28 us
  transfers between devices with their start and end apart: 9, of which 2 were waited for; matrix products, arithmetic and copies ran while one was open for 0% of the time, Pallas kernels for 10%

profile of v12, /device:TPU:0, one launch (start us, length us, event | category | flops | bytes accessed | tf_op | source)
XLA Modules:
  0.0 54.2 jit_solution(12236566972319375369)
XLA Ops:
  0.6 1.3 %copy-done = bf16[24,12,2048]{2,0,1:T(8,128)(2,1)S(1)} copy-done((bf16[24,12,2048]{2,0,1:T(8,128)(2,1)S(1)}, bf16[24,12,2048]{2,0,1:T(8,128)(2,1)}, u32[]{:S(2)}) %copy-start) | copy-done | bytes 1179672
  1.9 0.1 pack.1
  2.0 1.7 %collective-permute-start = (bf16[4,24,512]{2,1,0:T(8,128)(2,1)S(1)}, bf16[4,24,512]{2,1,0:T(8,128)(2,1)S(1)}, u32[]{:S(2)}, u32[]{:S(2)}) collective-permute-start(bf16[4,24,512]{2,1,0:T(8,128)(2,1)S(1)} %get-tuple-element.20), channel_id=1, source_target_pairs={{0,32},{32,64},{64,96},{96,0},{1,33},{33,65},{65,97},{97,1},{2,34}... | collective-permute-start | bytes 294920 | tf_op jit(solution)/shard_map/ppermute | solution.py:371
  3.8 2.9 %collective-permute-start.1 = (bf16[4,24,512]{2,1,0:T(8,128)(2,1)S(1)}, bf16[4,24,512]{2,1,0:T(8,128)(2,1)S(1)}, u32[]{:S(2)}, u32[]{:S(2)}) collective-permute-start(bf16[4,24,512]{2,1,0:T(8,128)(2,1)S(1)} %get-tuple-element.21), channel_id=1, source_target_pairs={{0,64},{32,96},{64,0},{96,32},{1,65},{33,97},{65,1},{97,33},{2,66}... | collective-permute-start | bytes 294920 | tf_op jit(solution)/shard_map/ppermute | solution.py:371
  6.7 1.3 %collective-permute-start.2 = (bf16[4,24,512]{2,1,0:T(8,128)(2,1)S(1)}, bf16[4,24,512]{2,1,0:T(8,128)(2,1)S(1)}, u32[]{:S(2)}, u32[]{:S(2)}) collective-permute-start(bf16[4,24,512]{2,1,0:T(8,128)(2,1)S(1)} %get-tuple-element.22), channel_id=1, source_target_pairs={{0,96},{32,0},{64,32},{96,64},{1,97},{33,1},{65,33},{97,65},{2,98}... | collective-permute-start | bytes 294920 | tf_op jit(solution)/shard_map/ppermute | solution.py:371
  8.0 0.9 %pack_bulk.1 = (bf16[23,24,512]{2,1,0:T(8,128)(2,1)}, bf16[23,24,512]{2,1,0:T(8,128)(2,1)S(1)}, bf16[23,24,512]{2,1,0:T(8,128)(2,1)S(1)}) custom-call(s32[1]{0:T(128)} %bitcast.1.me_ref, bf16[12,24,2048]{2,1,0:T(8,128)(2,1)S(1)} %bitcast.9, bf16[4,24,512]{2,1,0:T(8,128)(2,1)S(1)} %get-tuple-element.19.c0.after_ref), custom_call_target="tpu_custom_call" | custom-call | tf_op jit(solution)/shard_map/pack_bulk/pallas_call | solution.py:86
  9.0 0.7 %collective-permute-start.3 = (bf16[23,24,512]{2,1,0:T(8,128)(2,1)}, bf16[23,24,512]{2,1,0:T(8,128)(2,1)S(1)}, u32[]{:S(2)}, u32[]{:S(2)}) collective-permute-start(bf16[23,24,512]{2,1,0:T(8,128)(2,1)} %get-tuple-element.23), channel_id=1, source_target_pairs={{0,32},{32,64},{64,96},{96,0},{1,33},{33,65},{65,97},{97,1},{2,34}... | collective-permute-start | bytes 1695752 | tf_op jit(solution)/shard_map/ppermute | solution.py:371
  9.7 0.8 %collective-permute-start.4 = (bf16[23,24,512]{2,1,0:T(8,128)(2,1)S(1)}, bf16[23,24,512]{2,1,0:T(8,128)(2,1)S(1)}, u32[]{:S(2)}, u32[]{:S(2)}) collective-permute-start(bf16[23,24,512]{2,1,0:T(8,128)(2,1)S(1)} %get-tuple-element.24), channel_id=1, source_target_pairs={{0,64},{32,96},{64,0},{96,32},{1,65},{33,97},{65,1},{97,33},{2,66}... | collective-permute-start | bytes 1695752 | tf_op jit(solution)/shard_map/ppermute | solution.py:371
  10.5 2.0 %collective-permute-start.5 = (bf16[23,24,512]{2,1,0:T(8,128)(2,1)S(1)}, bf16[23,24,512]{2,1,0:T(8,128)(2,1)S(1)}, u32[]{:S(2)}, u32[]{:S(2)}) collective-permute-start(bf16[23,24,512]{2,1,0:T(8,128)(2,1)S(1)} %get-tuple-element.25), channel_id=1, source_target_pairs={{0,96},{32,0},{64,32},{96,64},{1,97},{33,1},{65,33},{97,65},{2,98}... | collective-permute-start | bytes 1695752 | tf_op jit(solution)/shard_map/ppermute | solution.py:371
  12.5 1.5 %observe.1 = f32[48,128]{1,0:T(8,128)S(1)} custom-call(s32[1]{0:T(128)} %bitcast.1.me_ref, s32[2,12]{1,0:T(2,128)S(1)} %bitcast.13, bf16[4,24,512]{2,1,0:T(8,128)(2,1)S(1)} %get-tuple-element.19.c0.after_ref, bf16[4,24,512]{2,1,0:T(8,128)(2,1)S(1)} %collective-permute-done.c1.o1, bf16[4,24,512]{2,1,0:T(8,128)(2,1)S(1)} %collective-permute-done.1.c2.o2, ...), custom_call_target="tpu_custom_call" | custom-call | tf_op jit(solution)/shard_map/observe/pallas_call | solution.py:163
  14.0 25.7 %conditional.1 = (bf16[8,48,128]{2,1,0:T(8,128)(2,1)S(1)}) conditional(s32[]{:T(128)} %convert_element_type.4, () %tuple.14, f32[48,128]{1,0:T(8,128)S(1)} %observe.1), branch_computations={%region_0.0_spmd, %region_1.0_spmd} | conditional | bytes 589832 | solution.py:395
  14.0 0.1 spread_sum.2
  14.2 15.8 %all_to_all.8.parts_ref = bf16[16,48,128]{2,1,0:T(8,128)(2,1)S(1)} all-to-all(bf16[16,48,128]{2,1,0:T(8,128)(2,1)S(1)} %spread_sum.2), channel_id=1, replica_groups=mesh['member'=4,'x'=4,'z'=4,'core'=2] {'x','z'}, dimensions={0} | all-to-all | bytes 393216 | tf_op jit(solution)/shard_map/cond/branch_1_fun/all_to_all | solution.py:375
  29.9 0.2 spread_sum.3
  30.1 9.6 %all_to_all.9 = bf16[8,48,128]{2,1,0:T(8,128)(2,1)S(1)} all-to-all(bf16[8,48,128]{2,1,0:T(8,128)(2,1)S(1)} %spread_sum.3), channel_id=1, replica_groups=mesh['member'=4,'x'=4,'z'=4,'core'=2] {'member','core'}, dimensions={0} | all-to-all | bytes 196608 | tf_op jit(solution)/shard_map/cond/branch_1_fun/all_to_all | solution.py:375
  39.7 1.6 %transform.1.w_ref = f32[96,96]{1,0:T(8,128)S(1)} custom-call(bf16[8,48,128]{2,1,0:T(8,128)(2,1)S(1)} %get-tuple-element.32.parts_ref), custom_call_target="tpu_custom_call" | custom-call | flops 40000000000 | tf_op jit(solution)/shard_map/transform/pallas_call | solution.py:247
  41.4 0.5 analyse_near.1
  41.8 0.6 %collective-permute-start.6 = (bf16[7,24,512]{2,1,0:T(8,128)(2,1)S(1)}, bf16[7,24,512]{2,1,0:T(8,128)(2,1)S(1)}, u32[]{:S(2)}, u32[]{:S(2)}) collective-permute-start(bf16[7,24,512]{2,1,0:T(8,128)(2,1)S(1)} %get-tuple-element.26), channel_id=1, source_target_pairs={{0,32},{32,64},{64,96},{96,0},{1,33},{33,65},{65,97},{97,1},{2,34}... | collective-permute-start | bytes 516104 | tf_op jit(solution)/shard_map/ppermute | solution.py:371
  42.5 2.1 %collective-permute-start.7 = (bf16[7,24,512]{2,1,0:T(8,128)(2,1)S(1)}, bf16[7,24,512]{2,1,0:T(8,128)(2,1)S(1)}, u32[]{:S(2)}, u32[]{:S(2)}) collective-permute-start(bf16[7,24,512]{2,1,0:T(8,128)(2,1)S(1)} %get-tuple-element.27), channel_id=1, source_target_pairs={{0,64},{32,96},{64,0},{96,32},{1,65},{33,97},{65,1},{97,33},{2,66}... | collective-permute-start | bytes 516104 | tf_op jit(solution)/shard_map/ppermute | solution.py:371
  44.5 0.9 %collective-permute-start.8 = (bf16[7,24,512]{2,1,0:T(8,128)(2,1)S(1)}, bf16[7,24,512]{2,1,0:T(8,128)(2,1)S(1)}, u32[]{:S(2)}, u32[]{:S(2)}) collective-permute-start(bf16[7,24,512]{2,1,0:T(8,128)(2,1)S(1)} %get-tuple-element.28), channel_id=1, source_target_pairs={{0,96},{32,0},{64,32},{96,64},{1,97},{33,1},{65,33},{97,65},{2,98}... | collective-permute-start | bytes 516104 | tf_op jit(solution)/shard_map/ppermute | solution.py:371
  45.4 1.3 %analyse_far.1 = (bf16[12,24,2048]{2,1,0:T(8,128)(2,1)}, f32[96,96]{1,0:T(8,128)}) custom-call(s32[1]{0:T(128)} %bitcast.1.me_ref, f32[96,96]{1,0:T(8,128)S(1)} %transform.1.w_ref, bf16[7,24,512]{2,1,0:T(8,128)(2,1)S(1)} %get-tuple-element.29.near_ref, bf16[12,24,2048]{2,1,0:T(8,128)(2,1)S(1)} %bitcast.11, ...), custom_call_target="tpu_custom_call" | custom-call | tf_op jit(solution)/shard_map/analyse_far/pallas_call | solution.py:323
  46.8 6.0 %collective-permute-done.6.c1 = bf16[7,24,512]{2,1,0:T(8,128)(2,1)S(1)} collective-permute-done((bf16[7,24,512]{2,1,0:T(8,128)(2,1)S(1)}, bf16[7,24,512]{2,1,0:T(8,128)(2,1)S(1)}, u32[]{:S(2)}, u32[]{:S(2)}) %collective-permute-start.6) | collective-permute-done | bytes 172064 | tf_op jit(solution)/shard_map/ppermute | solution.py:371
  52.8 0.6 %collective-permute-done.8.c3 = bf16[7,24,512]{2,1,0:T(8,128)(2,1)S(1)} collective-permute-done((bf16[7,24,512]{2,1,0:T(8,128)(2,1)S(1)}, bf16[7,24,512]{2,1,0:T(8,128)(2,1)S(1)}, u32[]{:S(2)}, u32[]{:S(2)}) %collective-permute-start.8) | collective-permute-done | bytes 172064 | tf_op jit(solution)/shard_map/ppermute | solution.py:371
  53.4 0.8 %place.1 = bf16[12,24,2048]{2,1,0:T(8,128)(2,1)} custom-call(s32[1]{0:T(128)} %bitcast.1.me_ref, bf16[7,24,512]{2,1,0:T(8,128)(2,1)S(1)} %collective-permute-done.6.c1, bf16[7,24,512]{2,1,0:T(8,128)(2,1)S(1)} %collective-permute-done.7.c2, bf16[7,24,512]{2,1,0:T(8,128)(2,1)S(1)} %collective-permute-done.8.c3, ...), custom_call_target="tpu_custom_call", output_to_operand_aliasing={{}: (4, {})} | custom-call | tf_op jit(solution)/shard_map/place/pallas_call | solution.py:354
  (18 shorter events, 0.0 us)
Async XLA Ops:
  0.6 1.3 %copy-start = (bf16[24,12,2048]{2,0,1:T(8,128)(2,1)S(1)}, bf16[24,12,2048]{2,0,1:T(8,128)(2,1)}, u32[]{:S(2)}) copy-start(bf16[24,12,2048]{2,0,1:T(8,128)(2,1)} %param.7) | copy-start | bytes 3538948
  1.9 10.6 %copy-start.2 = (bf16[12,1,2,128,128]{4,3,2,1,0:T(8,128)(2,1)S(1)}, bf16[12,1,2,128,128]{4,3,2,1,0:T(8,128)(2,1)}, u32[]{:S(2)}) copy-start(bf16[12,1,2,128,128]{4,3,2,1,0:T(8,128)(2,1)} %param.10) | copy-start | bytes 2359300
  1.9 10.6 %copy-start.3 = (f32[12,1,128]{2,1,0:T(1,128)S(1)}, f32[12,1,128]{2,1,0:T(1,128)}, u32[]{:S(2)}) copy-start(f32[12,1,128]{2,1,0:T(1,128)} %y_ref.1) | copy-start | bytes 18436
  1.9 10.6 %copy-start.4 = (f32[12,1,128]{2,1,0:T(1,128)S(1)}, f32[12,1,128]{2,1,0:T(1,128)}, u32[]{:S(2)}) copy-start(f32[12,1,128]{2,1,0:T(1,128)} %var_ref.1) | copy-start | bytes 18436
  1.9 10.6 %copy-start.5 = (s32[12,1,2]{0,2,1:T(2,128)S(1)}, s32[12,1,2]{0,2,1:T(2,128)}, u32[]{:S(2)}) copy-start(s32[12,1,2]{0,2,1:T(2,128)} %param.11) | copy-start | bytes 292
  2.0 8.5 %collective-permute-start = (bf16[4,24,512]{2,1,0:T(8,128)(2,1)S(1)}, bf16[4,24,512]{2,1,0:T(8,128)(2,1)S(1)}, u32[]{:S(2)}, u32[]{:S(2)}) collective-permute-start(bf16[4,24,512]{2,1,0:T(8,128)(2,1)S(1)} %get-tuple-element.20), channel_id=1, source_target_pairs={{0,32},{32,64},{64,96},{96,0},{1,33},{33,65},{65,97},{97,1},{2,34}... | collective-permute-start | bytes 294920 | tf_op jit(solution)/shard_map/ppermute | solution.py:371
  3.8 8.7 %collective-permute-start.1 = (bf16[4,24,512]{2,1,0:T(8,128)(2,1)S(1)}, bf16[4,24,512]{2,1,0:T(8,128)(2,1)S(1)}, u32[]{:S(2)}, u32[]{:S(2)}) collective-permute-start(bf16[4,24,512]{2,1,0:T(8,128)(2,1)S(1)} %get-tuple-element.21), channel_id=1, source_target_pairs={{0,64},{32,96},{64,0},{96,32},{1,65},{33,97},{65,1},{97,33},{2,66}... | collective-permute-start | bytes 294920 | tf_op jit(solution)/shard_map/ppermute | solution.py:371
  6.7 5.8 %collective-permute-start.2 = (bf16[4,24,512]{2,1,0:T(8,128)(2,1)S(1)}, bf16[4,24,512]{2,1,0:T(8,128)(2,1)S(1)}, u32[]{:S(2)}, u32[]{:S(2)}) collective-permute-start(bf16[4,24,512]{2,1,0:T(8,128)(2,1)S(1)} %get-tuple-element.22), channel_id=1, source_target_pairs={{0,96},{32,0},{64,32},{96,64},{1,97},{33,1},{65,33},{97,65},{2,98}... | collective-permute-start | bytes 294920 | tf_op jit(solution)/shard_map/ppermute | solution.py:371
  9.0 32.4 %collective-permute-start.3 = (bf16[23,24,512]{2,1,0:T(8,128)(2,1)}, bf16[23,24,512]{2,1,0:T(8,128)(2,1)S(1)}, u32[]{:S(2)}, u32[]{:S(2)}) collective-permute-start(bf16[23,24,512]{2,1,0:T(8,128)(2,1)} %get-tuple-element.23), channel_id=1, source_target_pairs={{0,32},{32,64},{64,96},{96,0},{1,33},{33,65},{65,97},{97,1},{2,34}... | collective-permute-start | bytes 1695752 | tf_op jit(solution)/shard_map/ppermute | solution.py:371
  9.7 31.6 %collective-permute-start.4 = (bf16[23,24,512]{2,1,0:T(8,128)(2,1)S(1)}, bf16[23,24,512]{2,1,0:T(8,128)(2,1)S(1)}, u32[]{:S(2)}, u32[]{:S(2)}) collective-permute-start(bf16[23,24,512]{2,1,0:T(8,128)(2,1)S(1)} %get-tuple-element.24), channel_id=1, source_target_pairs={{0,64},{32,96},{64,0},{96,32},{1,65},{33,97},{65,1},{97,33},{2,66}... | collective-permute-start | bytes 1695752 | tf_op jit(solution)/shard_map/ppermute | solution.py:371
  10.5 30.8 %collective-permute-start.5 = (bf16[23,24,512]{2,1,0:T(8,128)(2,1)S(1)}, bf16[23,24,512]{2,1,0:T(8,128)(2,1)S(1)}, u32[]{:S(2)}, u32[]{:S(2)}) collective-permute-start(bf16[23,24,512]{2,1,0:T(8,128)(2,1)S(1)} %get-tuple-element.25), channel_id=1, source_target_pairs={{0,96},{32,0},{64,32},{96,64},{1,97},{33,1},{65,33},{97,65},{2,98}... | collective-permute-start | bytes 1695752 | tf_op jit(solution)/shard_map/ppermute | solution.py:371
  39.7 1.6 %copy-start.1 = (bf16[24,12,2048]{2,0,1:T(8,128)(2,1)S(1)}, bf16[24,12,2048]{2,0,1:T(8,128)(2,1)}, u32[]{:S(2)}) copy-start(bf16[24,12,2048]{2,0,1:T(8,128)(2,1)} %param.7) | copy-start | bytes 3538948
  41.8 10.9 %collective-permute-start.6 = (bf16[7,24,512]{2,1,0:T(8,128)(2,1)S(1)}, bf16[7,24,512]{2,1,0:T(8,128)(2,1)S(1)}, u32[]{:S(2)}, u32[]{:S(2)}) collective-permute-start(bf16[7,24,512]{2,1,0:T(8,128)(2,1)S(1)} %get-tuple-element.26), channel_id=1, source_target_pairs={{0,32},{32,64},{64,96},{96,0},{1,33},{33,65},{65,97},{97,1},{2,34}... | collective-permute-start | bytes 516104 | tf_op jit(solution)/shard_map/ppermute | solution.py:371
  42.5 10.3 %collective-permute-start.7 = (bf16[7,24,512]{2,1,0:T(8,128)(2,1)S(1)}, bf16[7,24,512]{2,1,0:T(8,128)(2,1)S(1)}, u32[]{:S(2)}, u32[]{:S(2)}) collective-permute-start(bf16[7,24,512]{2,1,0:T(8,128)(2,1)S(1)} %get-tuple-element.27), channel_id=1, source_target_pairs={{0,64},{32,96},{64,0},{96,32},{1,65},{33,97},{65,1},{97,33},{2,66}... | collective-permute-start | bytes 516104 | tf_op jit(solution)/shard_map/ppermute | solution.py:371
  44.5 8.9 %collective-permute-start.8 = (bf16[7,24,512]{2,1,0:T(8,128)(2,1)S(1)}, bf16[7,24,512]{2,1,0:T(8,128)(2,1)S(1)}, u32[]{:S(2)}, u32[]{:S(2)}) collective-permute-start(bf16[7,24,512]{2,1,0:T(8,128)(2,1)S(1)} %get-tuple-element.28), channel_id=1, source_target_pairs={{0,96},{32,0},{64,32},{96,64},{1,97},{33,1},{65,33},{97,65},{2,98}... | collective-permute-start | bytes 516104 | tf_op jit(solution)/shard_map/ppermute | solution.py:371
